TPU v7x, 32 devices: a whole 2x2x4 slice. The times are simulated.
32 devices in a mesh: fsdp: 16 (over z, x, core), rep: 2 (over y).
Axes of the slice: x: 2, y: 2, z: 4, core: 2. Of those that a mesh axis runs over, the one named last changes fastest.
Arguments:
- tokens: bfloat16 [8192, 1024], P(('fsdp', 'rep')), may hold values from -6 to 6
- counts: int32 [32], P(('fsdp', 'rep')), may hold values from 128 to 256, as said below
- segments: int32 [8192], P(('fsdp', 'rep')), may hold values from 0 to 8191, as said below
- norm1_gain: bfloat16 [1024], P(('fsdp', 'rep')), may hold values from 0.25 to 1.75
- in_weight: bfloat16 [1024, 3072], P(('fsdp', 'rep')), may hold values from -0.1875 to 0.1875
- conv_kernel: bfloat16 [3, 1024], P(None, ('fsdp', 'rep')), may hold values from -3 to 3
- out_weight: bfloat16 [1024, 1024], P(('fsdp', 'rep')), may hold values from -0.1875 to 0.1875
- norm2_gain: bfloat16 [1024], P(('fsdp', 'rep')), may hold values from 0.25 to 1.75
- gate_weight: bfloat16 [1024, 4608], P(('fsdp', 'rep')), may hold values from -0.1875 to 0.1875
- up_weight: bfloat16 [1024, 4608], P(('fsdp', 'rep')), may hold values from -0.1875 to 0.1875
- down_weight: bfloat16 [4608, 1024], P(('fsdp', 'rep')), may hold values from -0.125 to 0.125
- cotangent: bfloat16 [8192, 1024], P(('fsdp', 'rep')), may hold values from -6 to 6
Outputs:
- mixed: bfloat16 [8192, 1024], P(('fsdp', 'rep'))
- token_grad: float32 [8192, 1024], P(('fsdp', 'rep'))
- norm1_gain_grad: float32 [1024], P(('fsdp', 'rep'))
- in_weight_grad: float32 [1024, 3072], P(('fsdp', 'rep'))
- conv_kernel_grad: float32 [3, 1024], P(None, ('fsdp', 'rep'))
- out_weight_grad: float32 [1024, 1024], P(('fsdp', 'rep'))
- norm2_gain_grad: float32 [1024], P(('fsdp', 'rep'))
- gate_weight_grad: float32 [1024, 4608], P(('fsdp', 'rep'))
- up_weight_grad: float32 [1024, 4608], P(('fsdp', 'rep'))
- down_weight_grad: float32 [4608, 1024], P(('fsdp', 'rep'))
Inputs may be any that keep to these rules, and one draw needn't show every extreme that they name: counts[d] is the number of live slots at the front of device block d of 256 rows; some device has all 256 live. `segments`: a sequence's id is the index of its first token slot; ids never fall, and a sequence lies within one aligned block of 256 rows.
All inputs are finite; a program needn't handle non-finite values.
Results may differ from a plain program's by a relative error of at most 0.0097.
Values may be sent and summed in bfloat16 or wider, within the bound.
No kernel may reach another device: no remote copies, remote signals or barrier semaphores. Data moves between devices by JAX's collectives and lax.ppermute only.
A program may use at most 256 MiB of HBM per device.

v0:
```python
import jax
import jax.numpy as jnp
from jax import lax
from jax.sharding import PartitionSpec as P

EPS = 1e-05


def contract_rows(left, right):
    return lax.dot_general(
        left, right, (((0,), (0,)), ((), ())), preferred_element_type=jnp.float32
    )


def contract_cols(left, right):
    return lax.dot_general(
        left, right, (((1,), (1,)), ((), ())), preferred_element_type=jnp.float32
    )


def shifted(values, steps):
    return jnp.concatenate(
        [jnp.zeros((steps, values.shape[1]), values.dtype), values[:-steps]], axis=0
    )


def lifted(values, steps):
    return jnp.concatenate(
        [values[steps:], jnp.zeros((steps, values.shape[1]), values.dtype)], axis=0
    )


def norm_back(grad_norm, source, scale, gain):
    weighted = grad_norm * gain
    gain_grad = jnp.sum(grad_norm * source * scale, axis=0)
    source_grad = scale * weighted - source * scale**3 * jnp.mean(
        weighted * source, axis=1, keepdims=True
    )
    return (source_grad, gain_grad)


def local(
    tokens,
    counts,
    segments,
    norm1_gain,
    in_weight,
    conv_kernel,
    out_weight,
    norm2_gain,
    gate_weight,
    up_weight,
    down_weight,
    cotangent,
):
    width = tokens.shape[1]
    slots = tokens.shape[0]
    hidden_units = gate_weight.shape[1]
    gain_one, in_full, kernel_full, out_full = (
        lax.all_gather(norm1_gain, ("fsdp", "rep"), axis=0, tiled=True),
        lax.all_gather(in_weight, ("fsdp", "rep"), axis=0, tiled=True),
        lax.all_gather(conv_kernel, ("fsdp", "rep"), axis=1, tiled=True),
        lax.all_gather(out_weight, ("fsdp", "rep"), axis=0, tiled=True),
    )
    source = tokens.astype(jnp.float32)
    scale_one = lax.rsqrt(jnp.mean(source * source, axis=1, keepdims=True) + EPS)
    gain_first = gain_one.astype(jnp.float32)
    normed_one = (source * scale_one * gain_first).astype(jnp.bfloat16)
    projected = jnp.dot(normed_one, in_full, preferred_element_type=jnp.float32)
    first = projected[:, :width]
    second = projected[:, width : 2 * width]
    stream = projected[:, 2 * width :]
    product = first * stream
    same_one = jnp.concatenate(
        [jnp.zeros((1,), jnp.float32), (segments[1:] == segments[:-1]).astype(jnp.float32)]
    )[:, None]
    same_two = jnp.concatenate(
        [jnp.zeros((2,), jnp.float32), (segments[2:] == segments[:-2]).astype(jnp.float32)]
    )[:, None]
    kernel_vals = kernel_full.astype(jnp.float32)
    back_one = shifted(product, 1) * same_one
    back_two = shifted(product, 2) * same_two
    convolved = kernel_vals[0] * product + kernel_vals[1] * back_one + kernel_vals[2] * back_two
    mixer = (second * convolved).astype(jnp.bfloat16)
    hidden = source + jnp.dot(mixer, out_full, preferred_element_type=jnp.float32)
    gain_two, gate_full, up_full, down_full = (
        lax.all_gather(norm2_gain, ("fsdp", "rep"), axis=0, tiled=True),
        lax.all_gather(gate_weight, ("fsdp", "rep"), axis=0, tiled=True),
        lax.all_gather(up_weight, ("fsdp", "rep"), axis=0, tiled=True),
        lax.all_gather(down_weight, ("fsdp", "rep"), axis=0, tiled=True),
    )
    scale_two = lax.rsqrt(jnp.mean(hidden * hidden, axis=1, keepdims=True) + EPS)
    gain_second = gain_two.astype(jnp.float32)
    normed_two = (hidden * scale_two * gain_second).astype(jnp.bfloat16)
    gate = jnp.dot(normed_two, gate_full, preferred_element_type=jnp.float32)
    upper = jnp.dot(normed_two, up_full, preferred_element_type=jnp.float32)
    sigma = jax.nn.sigmoid(gate)
    swish = gate * sigma
    act = (swish * upper).astype(jnp.bfloat16)
    ffn = jnp.dot(act, down_full, preferred_element_type=jnp.float32)
    live = (jnp.arange(slots) < counts[0]).astype(jnp.float32)[:, None]
    mixed = (live * (hidden + ffn)).astype(jnp.bfloat16)
    gain_two, gate_full, up_full, down_full = (
        lax.all_gather(norm2_gain, ("fsdp", "rep"), axis=0, tiled=True),
        lax.all_gather(gate_weight, ("fsdp", "rep"), axis=0, tiled=True),
        lax.all_gather(up_weight, ("fsdp", "rep"), axis=0, tiled=True),
        lax.all_gather(down_weight, ("fsdp", "rep"), axis=0, tiled=True),
    )
    gain_second = gain_two.astype(jnp.float32)
    dout = cotangent.astype(jnp.float32) * live
    dffn = dout.astype(jnp.bfloat16)
    down_shard = lax.psum_scatter(
        contract_rows(act, dffn), ("fsdp", "rep"), scatter_dimension=0, tiled=True
    )
    dact = contract_cols(dffn, down_full)
    dgate = (dact * upper * sigma * (1.0 + gate * (1.0 - sigma))).astype(jnp.bfloat16)
    dupper = (dact * swish).astype(jnp.bfloat16)
    dnormed_two = contract_cols(dgate, gate_full) + contract_cols(dupper, up_full)
    hidden_part, gain_two_grad = norm_back(dnormed_two, hidden, scale_two, gain_second)
    dhidden = dout + hidden_part
    gain_one, in_full, kernel_full, out_full = (
        lax.all_gather(norm1_gain, ("fsdp", "rep"), axis=0, tiled=True),
        lax.all_gather(in_weight, ("fsdp", "rep"), axis=0, tiled=True),
        lax.all_gather(conv_kernel, ("fsdp", "rep"), axis=1, tiled=True),
        lax.all_gather(out_weight, ("fsdp", "rep"), axis=0, tiled=True),
    )
    gain_first = gain_one.astype(jnp.float32)
    kernel_vals = kernel_full.astype(jnp.float32)
    dbranch = dhidden.astype(jnp.bfloat16)
    dmixer = contract_cols(dbranch, out_full)
    dsecond = dmixer * convolved
    dconv = dmixer * second
    kernel_grad = jnp.stack(
        [
            jnp.sum(dconv * product, axis=0),
            jnp.sum(dconv * back_one, axis=0),
            jnp.sum(dconv * back_two, axis=0),
        ],
        axis=0,
    )
    dproduct = (
        kernel_vals[0] * dconv
        + kernel_vals[1] * lifted(dconv * same_one, 1)
        + kernel_vals[2] * lifted(dconv * same_two, 2)
    )
    dprojected = jnp.concatenate([dproduct * stream, dsecond, dproduct * first], axis=1).astype(
        jnp.bfloat16
    )
    dnormed_one = contract_cols(dprojected, in_full)
    source_part, gain_one_grad = norm_back(dnormed_one, source, scale_one, gain_first)
    token_grad = dhidden + source_part
    every_rows = lax.psum_scatter(
        jnp.concatenate(
            [
                contract_rows(normed_one, dprojected),
                contract_rows(mixer, dbranch),
                contract_rows(normed_two, dgate),
                contract_rows(normed_two, dupper),
            ],
            axis=1,
        ),
        ("fsdp", "rep"),
        scatter_dimension=0,
        tiled=True,
    )
    gain_one_shard, kernel_shard, gain_two_shard = (
        lax.psum_scatter(gain_one_grad, ("fsdp", "rep"), scatter_dimension=0, tiled=True),
        lax.psum_scatter(kernel_grad, ("fsdp", "rep"), scatter_dimension=1, tiled=True),
        lax.psum_scatter(gain_two_grad, ("fsdp", "rep"), scatter_dimension=0, tiled=True),
    )
    in_shard = every_rows[:, : 3 * width]
    out_shard = every_rows[:, 3 * width : 4 * width]
    gate_shard = every_rows[:, 4 * width : 4 * width + hidden_units]
    up_shard = every_rows[:, 4 * width + hidden_units :]
    return (
        mixed,
        token_grad,
        gain_one_shard,
        in_shard,
        kernel_shard,
        out_shard,
        gain_two_shard,
        gate_shard,
        up_shard,
        down_shard,
    )


def solution(mesh):
    in_specs = (
        P(("fsdp", "rep"), None),
        P(("fsdp", "rep")),
        P(("fsdp", "rep")),
        P(("fsdp", "rep")),
        P(("fsdp", "rep"), None),
        P(None, ("fsdp", "rep")),
        P(("fsdp", "rep"), None),
        P(("fsdp", "rep")),
        P(("fsdp", "rep"), None),
        P(("fsdp", "rep"), None),
        P(("fsdp", "rep"), None),
        P(("fsdp", "rep"), None),
    )
    out_specs = (
        P(("fsdp", "rep"), None),
        P(("fsdp", "rep"), None),
        P(("fsdp", "rep")),
        P(("fsdp", "rep"), None),
        P(None, ("fsdp", "rep")),
        P(("fsdp", "rep"), None),
        P(("fsdp", "rep")),
        P(("fsdp", "rep"), None),
        P(("fsdp", "rep"), None),
        P(("fsdp", "rep"), None),
    )
    return jax.shard_map(local, mesh=mesh, in_specs=in_specs, out_specs=out_specs, check_vma=False)
```

profile of v0, /device:TPU:0, one launch (start us, length us, event | category | flops | bytes accessed | tf_op | source)
XLA Modules:
  0.0 1935.0 jit_solution(17348102764284692327)
XLA Ops:
  14.8 42.4 %all-reduce.10 = (bf16[1024]{0:T(1024)(128)(2,1)S(1)}, bf16[1024]{0:T(1024)(128)(2,1)S(1)}) all-reduce(bf16[1024]{0:T(1024)(128)(2,1)S(1)} %dynamic-update-slice, bf16[1024]{0:T(1024)(128)(2,1)S(1)} %dynamic-update-slice.1), channel_id=1, replica_groups=mesh['fsdp'=16,'rep'=2] {'fsdp','rep'}, use_global_device_ids=true, to_apply=%add.5 | all-reduce | flops 2048 | bytes 8192
  57.3 66.2 %all-gather = bf16[32,32,3]{1,2,0:T(4,128)(2,1)S(1)} all-gather(bf16[1,32,3]{1,2,0:T(4,128)(2,1)} %bitcast.60), channel_id=1, replica_groups=mesh['fsdp'=16,'rep'=2] {'fsdp','rep'}, dimensions={0}, use_global_device_ids=true | all-gather | bytes 6336 | tf_op jit(solution)/shard_map/all_gather | solution.py:62
  124.9 5.1 fusion.24
  131.6 1.5 multiply_convert_fusion.7
  133.2 8.4 all-gather.9.cloned.1.call-done
  141.6 2.4 multiply_reduce_fusion.5
  144.2 81.3 %all-gather.13.cloned.1.call-done = bf16[1024,4608]{1,0:T(8,128)(2,1)} async-done(((bf16[32,4608]{1,0:T(8,128)(2,1)}), bf16[1024,4608]{1,0:T(8,128)(2,1)}) %all-gather.13.cloned.1.call-update) | async-done | bytes 9437200 | tf_op jit(solution)/shard_map/all_gather | solution.py:89
  225.5 7.9 fusion.31
  233.4 75.5 %all-gather.11.cloned.1.call-done = bf16[1024,4608]{1,0:T(8,128)(2,1)} async-done(((bf16[32,4608]{1,0:T(8,128)(2,1)}), bf16[1024,4608]{1,0:T(8,128)(2,1)}) %all-gather.11.cloned.1.call-update) | async-done | bytes 9437200 | tf_op jit(solution)/shard_map/all_gather | solution.py:88
  308.9 8.0 fusion.30
  316.8 75.5 %all-gather.15.cloned.1.call-done = bf16[4608,1024]{1,0:T(8,128)(2,1)} async-done(((bf16[144,1024]{1,0:T(8,128)(2,1)}), bf16[4608,1024]{1,0:T(8,128)(2,1)}) %all-gather.15.cloned.1.call-update) | async-done | bytes 9437200 | tf_op jit(solution)/shard_map/all_gather | solution.py:90
  392.3 10.3 multiply_convert_fusion
  402.7 10.4 fusion.34
  413.1 8.9 fusion.33
  422.0 5.4 fusion.32
  427.4 4.8 multiply_reduce_fusion
  432.7 2.7 fusion.15
  435.4 3.5 multiply_reduce_fusion.3
  444.4 6.4 fusion.13
  450.8 35.6 %pad_maximum_fusion = f32[1024,13312]{1,0:T(8,128)} fusion(f32[1024,4608]{1,0:T(8,128)} %fusion.34, f32[1024,4608]{1,0:T(8,128)} %fusion.33, f32[1024,1024]{1,0:T(8,128)} %fusion.15, f32[1024,3072]{1,0:T(8,128)} %fusion.13), kind=kLoop, calls=%fused_computation | loop fusion | flops 40894464 | bytes 109051904 | tf_op jit(solution)/shard_map/concatenate | solution.py:153
  486.5 1.6 copy-done.14
  488.2 7.9 fusion.19
  497.3 6.2 fusion.11
  503.5 40.1 %all-reduce.9 = (f32[1024]{0:T(1024)S(1)}, f32[1024]{0:T(1024)S(1)}) all-reduce(f32[1024]{0:T(1024)S(1)} %get-tuple-element.12, f32[1024]{0:T(1024)S(1)} %get-tuple-element.10), channel_id=2, replica_groups=mesh['fsdp'=16,'rep'=2] {'fsdp','rep'}, use_global_device_ids=true, to_apply=%region_5.0.clone | all-reduce | flops 2048 | bytes 16384
  544.8 2.5 fusion.8
  547.3 7.8 fusion.2
  555.1 17.3 reduce-scatter.10.cloned.1.call-done
  573.8 1138.7 %reduce-scatter.6.cloned.1.call-done = f32[32,13312]{1,0:T(8,128)} async-done(((f32[1024,13312]{1,0:T(8,128)}), f32[32,13312]{1,0:T(8,128)}) %reduce-scatter.6.cloned.1.call-update) | async-done | bytes 1703952 | tf_op jit(solution)/shard_map/reduce_scatter | solution.py:152
  1712.5 1.6 slice.88
  1714.0 1.8 slice.87
  1715.8 2.3 fusion.28
  1718.1 210.0 %reduce-scatter.8.cloned.1.call-done = f32[144,1024]{1,0:T(8,128)} async-done(((f32[4608,1024]{1,0:T(8,128)}), f32[144,1024]{1,0:T(8,128)}) %reduce-scatter.8.cloned.1.call-update) | async-done | bytes 589840 | tf_op jit(solution)/shard_map/reduce_scatter | solution.py:112
  (104 shorter events, 19.7 us)
Async XLA Ops:
  7.2 117.7 %all-gather.7.cloned.1.call-start = ((), (), s32[]{:S(2)}) async-start(), calls=%async_computation.3 | async-start | bytes 6488064 | tf_op jit(solution)/shard_map/all_gather | solution.py:61
  7.9 133.7 %all-gather.9.cloned.1.call-start = ((), (), s32[]{:S(2)}) async-start(), calls=%async_computation.4 | async-start | bytes 2162688 | tf_op jit(solution)/shard_map/all_gather | solution.py:63
  8.7 216.8 %all-gather.13.cloned.1.call-start = ((), (), s32[]{:S(2)}) async-start(), calls=%async_computation.6 | async-start | bytes 9732096 | tf_op jit(solution)/shard_map/all_gather | solution.py:89
  9.4 299.5 %all-gather.11.cloned.1.call-start = ((), (), s32[]{:S(2)}) async-start(), calls=%async_computation.5 | async-start | bytes 9732096 | tf_op jit(solution)/shard_map/all_gather | solution.py:88
  10.0 382.3 %all-gather.15.cloned.1.call-start = ((), (), s32[]{:S(2)}) async-start(), calls=%async_computation.7 | async-start | bytes 9732096 | tf_op jit(solution)/shard_map/all_gather | solution.py:90
  10.6 561.9 %reduce-scatter.10.cloned.1.call-start = ((), (), s32[]{:S(2)}) async-start(), calls=%async_computation.10 | async-start | bytes 540672
  130.0 1.6 copy-start
  130.0 11.6 copy-start.7
  144.0 288.2 %copy-start.5 = (f32[256,1024]{1,0:T(8,128)}, f32[256,1024]{1,0:T(8,128)S(1)}, u32[]{:S(2)}) copy-start(f32[256,1024]{1,0:T(8,128)S(1)} %get-tuple-element.40) | copy-start | bytes 3145732
  402.6 10.4 copy-start.12
  402.6 10.4 copy-start.13
  402.6 19.4 %slice-start.3 = ((s8[9437184]{0:T(1024)(128)(4,1)}), s8[4194304]{0:T(1024)(128)(4,1)S(1)}, s32[]{:S(2)}) async-start(s8[9437184]{0:T(1024)(128)(4,1)} %bitcast.46), calls=%async_computation.14 | async-start | bytes 8388608
  402.7 19.3 slice-start.4
  413.1 8.9 slice-start.5
  413.1 14.3 slice-start
  413.1 14.3 slice-start.1
  422.0 5.4 slice-start.2
  427.4 4.8 copy-start.15
  432.3 3.1 copy-start.10
  432.3 3.1 copy-start.11
  432.7 6.3 copy-start.2
  438.9 3.9 copy-start.1
  440.0 1272.5 %reduce-scatter.6.cloned.1.call-start = ((), (), s32[]{:S(2)}) async-start(), calls=%async_computation.8 | async-start | bytes 56229888 | tf_op jit(solution)/shard_map/reduce_scatter | solution.py:152
  440.0 2.9 copy-start.4
  442.9 1.5 copy-start.8
  442.9 1.5 copy-start.17
  486.4 1.7 copy-start.14
  486.4 1.7 copy-start.16
  486.5 1441.7 %reduce-scatter.8.cloned.1.call-start = ((), (), s32[]{:S(2)}) async-start(), calls=%async_computation.9 | async-start | bytes 19464192 | tf_op jit(solution)/shard_map/reduce_scatter | solution.py:112
  496.1 1.2 copy-start.18
  497.3 47.4 %copy-start.3 = (f32[256,1024]{1,0:T(8,128)S(1)}, f32[256,1024]{1,0:T(8,128)}, u32[]{:S(2)}) copy-start(f32[256,1024]{1,0:T(8,128)} %copy-done.2) | copy-start | bytes 3145732
  497.3 49.9 %copy-start.6 = (f32[256,1024]{1,0:T(8,128)S(1)}, f32[256,1024]{1,0:T(8,128)}, u32[]{:S(2)}) copy-start(f32[256,1024]{1,0:T(8,128)} %copy-done.5) | copy-start | bytes 3145732
  (3 other events, 2.6 us)
Sparse Core Ops, SparseCore 0:
  10.9 72.5 all-gather.6
  86.6 54.9 all-gather.8
  144.5 80.8 all-gather.12
  228.2 80.6 all-gather.10
  311.7 80.6 all-gather.14
  440.1 132.3 reduce-scatter.9
  574.8 1137.5 reduce-scatter.5
  1720.6 207.5 reduce-scatter.7
where the time goes:
time: 1940 us
  waiting for transfers between devices  1610 us (83%)
  blocking collectives  149 us (8%)
  matrix products  97.8 us (5%)
  other arithmetic  46.8 us (2%)
    reduce_scatter x1, waiting for transfers between devices, local(): lax.psum_scatter(jnp.concatenate([contract_rows(normed_one, dprojected),...  1140 us
    reduce_scatter x1, waiting for transfers between devices, local(): lax.psum_scatter(contract_rows(act, dffn), ('fsdp', 'rep'), scatter_dimen...  210 us
    unnamed x2, blocking collectives  82.5 us
    all_gather x1, waiting for transfers between devices, local(): lax.all_gather(up_weight, ('fsdp', 'rep'), axis=0, tiled=True)  81.3 us
    all_gather x1, waiting for transfers between devices, local(): lax.all_gather(gate_weight, ('fsdp', 'rep'), axis=0, tiled=True)  75.5 us
    all_gather x1, waiting for transfers between devices, local(): lax.all_gather(down_weight, ('fsdp', 'rep'), axis=0, tiled=True)  75.5 us
    all_gather x1, blocking collectives, local(): lax.all_gather(conv_kernel, ('fsdp', 'rep'), axis=1, tiled=True)  66.2 us
  transfers between devices with their start and end apart: 8, of which 7 were waited for; matrix products, arithmetic and copies ran while one was open for 6% of the time, Pallas kernels for 0%

commit v1 on v0

v1 whole, which is shorter than its diff:
```python
import jax
import jax.numpy as jnp
from jax import lax
from jax.sharding import Mesh, PartitionSpec as P

EPS = 1e-05
BF = jnp.bfloat16
F32 = jnp.float32

PLANE = ("b", "y")
COLUMN = ("t", "c")
LANES = 256


def rows_by_rows(left, right):
    return lax.dot_general(left, right, (((0,), (0,)), ((), ())), preferred_element_type=F32)


def cols_by_cols(left, right):
    return lax.dot_general(left, right, (((1,), (1,)), ((), ())), preferred_element_type=F32)


def to_peer(values, k):
    return lax.ppermute(values, PLANE, [(i, i ^ k) for i in range(4)])


def plane_gather(values):
    return [values] + [to_peer(values, k) for k in (1, 2, 3)]


def plane_sum(blocks):
    sent = [blocks[k].astype(BF) for k in (1, 2, 3)]
    total = blocks[0].astype(F32)
    for k in (1, 2, 3):
        total = total + to_peer(sent[k - 1], k).astype(F32)
    return total


def pick(blocks, i):
    return lax.dynamic_index_in_dim(blocks, i, 0, keepdims=False)


def plane_swap(blocks, member):
    got = [pick(blocks, member)] + [to_peer(pick(blocks, member ^ k), k) for k in (1, 2, 3)]
    got = jnp.stack(got)
    return jnp.stack([pick(got, member ^ j) for j in range(4)])


def norm_back(grad_norm, source, scale, gain):
    weighted = grad_norm * gain
    gain_grad = jnp.sum(grad_norm * source * scale, axis=0)
    source_grad = scale * weighted - source * scale**3 * jnp.mean(
        weighted * source, axis=1, keepdims=True
    )
    return (source_grad, gain_grad)


def shifted(values, steps):
    return jnp.pad(values, ((0, 0), (steps, 0), (0, 0)))[:, :-steps]


def lifted(values, steps):
    return jnp.pad(values, ((0, 0), (0, steps), (0, 0)))[:, steps:]


def make_local(t):
    nb = 2 * t

    def local(
        tokens,
        counts,
        segments,
        norm1_gain,
        in_weight,
        conv_kernel,
        out_weight,
        norm2_gain,
        gate_weight,
        up_weight,
        down_weight,
        cotangent,
    ):
        slots, width = tokens.shape
        r = in_weight.shape[0]
        ch = out_weight.shape[0]
        h = down_weight.shape[0]
        share = nb * ch
        taps = conv_kernel.shape[0]
        slabs = width // LANES
        member = 2 * lax.axis_index("b") + lax.axis_index("y")

        same_one = jnp.concatenate([jnp.zeros((1,), BF), (segments[1:] == segments[:-1]).astype(BF)])
        same_two = jnp.concatenate([jnp.zeros((2,), BF), (segments[2:] == segments[:-2]).astype(BF)])
        flags = jnp.concatenate([same_one, same_two])
        flags = jnp.pad(flags, (0, 16 * width - 2 * slots)).reshape(16, width)
        live = (jnp.arange(slots) < counts[0]).astype(F32)[:, None]
        dout = cotangent.astype(F32) * live
        dffn_own = dout.astype(BF)

        in_blocks = in_weight.reshape(r, 3, t, 2, 2, 2, ch).transpose(3, 5, 1, 0, 2, 4, 6)
        in_blocks = in_blocks.reshape(4, 3 * r, share)
        extra = jnp.concatenate([norm1_gain, norm2_gain, conv_kernel.reshape(-1)])
        extra = jnp.pad(extra, (0, 16 * share - extra.shape[0])).reshape(1, 16, share)
        conv_blocks = jnp.concatenate([in_blocks, jnp.broadcast_to(extra, (4, 16, share))], axis=1)
        conv_mine = plane_swap(conv_blocks, member)
        out_slabs = out_weight.reshape(ch, slabs, LANES).transpose(1, 0, 2).reshape(slabs * ch, LANES)
        conv_all = lax.all_gather(
            jnp.concatenate([conv_mine.reshape(4 * (3 * r + 16), share), out_slabs]), COLUMN
        )
        gathered = plane_gather(jnp.concatenate([tokens, flags]))
        source = jnp.stack([g[:slots] for g in gathered]).reshape(4 * slots, width).astype(F32)
        marks = jnp.stack([g[slots:].reshape(-1)[: 2 * slots] for g in gathered]).astype(F32)
        same_one = marks[:, :slots, None]
        same_two = marks[:, slots:, None]
        source, same_one, same_two = lax.optimization_barrier((source, same_one, same_two))

        def ff_blocks(w):
            return w.reshape(r, t, 2, 2, 2, h).transpose(2, 4, 0, 1, 3, 5).reshape(4, r, nb * h)

        pair = jnp.concatenate([ff_blocks(gate_weight), ff_blocks(up_weight)], axis=2)
        pair_mine = plane_swap(pair, member).reshape(4 * r, 2 * nb * h)
        pair_all = lax.all_gather(pair_mine, COLUMN)
        pair_full = pair_all.reshape(t, 2, 2, 2 * r, 2 * nb * h).transpose(0, 2, 1, 3, 4)
        pair_full = lax.optimization_barrier(pair_full.reshape(width, 2 * nb * h))
        down_full = lax.all_gather(down_weight, COLUMN, axis=0, tiled=True)
        dffn = jnp.concatenate(plane_gather(dffn_own))

        split = 4 * (3 * r + 16)
        head = conv_all[:, :split].reshape(t, 2, 2, 2, 3 * r + 16, share)
        in_full = head[:, :, :, :, : 3 * r].reshape(t, 2, 2, 2, 3, r, share)
        in_full = lax.optimization_barrier(
            in_full.transpose(0, 2, 1, 3, 5, 4, 6).reshape(width, 3 * share)
        )
        rest = head[:, :, :, :, 3 * r :].reshape(nb, 4, 16 * share)
        gains = rest[:, :, : 2 * r].reshape(t, 2, 2, 2, 2, r).transpose(4, 0, 2, 1, 3, 5)
        gains = gains.reshape(2, width).astype(F32)
        gains = lax.optimization_barrier(gains)
        gain_first, gain_second = gains[0], gains[1]
        kernel_vals = pick(rest.transpose(1, 0, 2), member)[:, 2 * r : 2 * r + taps * ch]
        kernel_vals = kernel_vals.reshape(nb, taps, ch).transpose(1, 0, 2).reshape(taps, share).astype(F32)
        out_full = conv_all[:, split:].reshape(nb, slabs, ch, LANES).transpose(0, 2, 1, 3)
        out_full, kernel_vals = lax.optimization_barrier((out_full.reshape(share, width), kernel_vals))

        scale_one = lax.rsqrt(jnp.mean(source * source, axis=1, keepdims=True) + EPS)
        normed_one = (source * scale_one * gain_first).astype(BF)
        projected = jnp.dot(normed_one, in_full, preferred_element_type=F32)
        projected = projected.reshape(4, slots, 3 * share)
        first = projected[:, :, :share]
        second = projected[:, :, share : 2 * share]
        stream = projected[:, :, 2 * share :]
        product = first * stream
        back_one = shifted(product, 1) * same_one
        back_two = shifted(product, 2) * same_two
        convolved = kernel_vals[0] * product + kernel_vals[1] * back_one + kernel_vals[2] * back_two
        mixer = (second * convolved).astype(BF).reshape(4 * slots, share)
        branch = jnp.dot(mixer, out_full, preferred_element_type=F32).reshape(4, slots, width)
        own = tokens.astype(F32)
        hidden = own + plane_sum(branch)

        scale_two = lax.rsqrt(jnp.mean(hidden * hidden, axis=1, keepdims=True) + EPS)
        normed_two_own = (hidden * scale_two * gain_second).astype(BF)
        normed_two = jnp.concatenate(plane_gather(normed_two_own))
        both = jnp.dot(normed_two, pair_full, preferred_element_type=F32)
        gate = both[:, : nb * h]
        upper = both[:, nb * h :]
        sigma = jax.nn.sigmoid(gate)
        swish = gate * sigma
        act = (swish * upper).astype(BF)
        dact = cols_by_cols(dffn, down_full)
        dgate = (dact * upper * sigma * (1.0 + gate * (1.0 - sigma))).astype(BF)
        dupper = (dact * swish).astype(BF)
        dboth = jnp.concatenate([dgate, dupper], axis=1)
        dnormed_two = plane_sum(cols_by_cols(dboth, pair_full).reshape(4, slots, width))
        down_grad = rows_by_rows(act, dffn).astype(BF)
        down_shard = lax.psum_scatter(down_grad, COLUMN, scatter_dimension=0, tiled=True).astype(F32)
        pair_grad = lax.optimization_barrier(rows_by_rows(normed_two, dboth).astype(BF))
        pair_grad = pair_grad.reshape(t, 2, 2, 2 * r, 2 * nb * h).transpose(0, 2, 1, 3, 4)
        pair_grad = lax.psum_scatter(pair_grad.reshape(nb, 4 * r, 2 * nb * h), COLUMN, scatter_dimension=0)
        ffn = plane_sum(jnp.dot(act, down_full, preferred_element_type=F32).reshape(4, slots, width))
        mixed = (live * (hidden + ffn)).astype(BF)
        hidden_part, gain_two_grad = norm_back(dnormed_two, hidden, scale_two, gain_second)
        dhidden = dout + hidden_part

        dbranch = jnp.concatenate(plane_gather(dhidden.astype(BF)))
        dmixer = cols_by_cols(dbranch, out_full).reshape(4, slots, share)
        dsecond = dmixer * convolved
        dconv = dmixer * second
        kernel_grad = jnp.stack(
            [
                jnp.sum(dconv * product, axis=(0, 1)),
                jnp.sum(dconv * back_one, axis=(0, 1)),
                jnp.sum(dconv * back_two, axis=(0, 1)),
            ]
        )
        dproduct = (
            kernel_vals[0] * dconv
            + kernel_vals[1] * lifted(dconv * same_one, 1)
            + kernel_vals[2] * lifted(dconv * same_two, 2)
        )
        dprojected = jnp.concatenate([dproduct * stream, dsecond, dproduct * first], axis=2)
        dprojected = dprojected.astype(BF).reshape(4 * slots, 3 * share)
        dnormed_part = cols_by_cols(dprojected, in_full)
        gain_one_grad = jnp.sum(dnormed_part * source * scale_one, axis=0)
        dnormed_one = plane_sum(dnormed_part.reshape(4, slots, width))
        own_scale = scale_one[:slots]
        weighted = dnormed_one * gain_first
        token_grad = (
            dhidden
            + own_scale * weighted
            - own * own_scale**3 * jnp.mean(weighted * own, axis=1, keepdims=True)
        )

        kernel_grad, gain_one_grad, gain_two_grad = lax.optimization_barrier(
            (kernel_grad, gain_one_grad, gain_two_grad)
        )
        in_grad = lax.optimization_barrier(rows_by_rows(normed_one, dprojected).astype(BF))
        in_grad = in_grad.reshape(t, 2, 2, 2, r, 3, share).transpose(0, 2, 1, 3, 5, 4, 6)
        in_grad = in_grad.reshape(nb, 4, 3 * r, share)
        gain_grads = jnp.stack([gain_one_grad, gain_two_grad]).astype(BF)
        gain_grads = gain_grads.reshape(2, t, 2, 2, 2, r).transpose(1, 3, 2, 4, 0, 5).reshape(nb, 4, 2 * r)
        gain_grads = jnp.pad(gain_grads, ((0, 0), (0, 0), (0, 16 * share - 2 * r)))
        in_grad = jnp.concatenate([in_grad, lax.optimization_barrier(gain_grads.reshape(nb, 4, 16, share))], axis=2)
        out_grad = lax.optimization_barrier(rows_by_rows(mixer, dbranch).astype(BF))
        out_grad = out_grad.reshape(nb, ch, slabs, LANES).transpose(0, 2, 1, 3).reshape(nb, slabs * ch, LANES)
        kernel_grad = kernel_grad.astype(BF).reshape(taps, nb, ch).transpose(1, 0, 2).reshape(nb, taps * ch)
        kernel_grad = jnp.pad(kernel_grad, ((0, 0), (0, 16 * share - taps * ch))).reshape(nb, 16, share)
        in_grad, out_grad, kernel_grad = lax.optimization_barrier(
            (in_grad.reshape(nb, split, share), out_grad, kernel_grad)
        )
        conv_grad = lax.optimization_barrier(jnp.concatenate([in_grad, out_grad, kernel_grad], axis=1))
        conv_grad = lax.psum_scatter(conv_grad, COLUMN, scatter_dimension=0)
        out_shard = conv_grad[split : split + slabs * ch].reshape(slabs, ch, LANES).transpose(1, 0, 2)
        out_shard = out_shard.reshape(ch, width).astype(F32)
        kernel_shard = conv_grad[split + slabs * ch :].reshape(-1)[: taps * ch].reshape(taps, ch).astype(F32)
        swapped = plane_swap(conv_grad[:split].reshape(4, 3 * r + 16, share), member)
        gain_shards = swapped[:, 3 * r :].reshape(4, 16 * share)[:, : 2 * r].astype(F32).sum(axis=0)
        in_shard = swapped[:, : 3 * r].reshape(2, 2, 3, r, t, 2, ch).transpose(3, 2, 4, 0, 5, 1, 6)
        in_shard = in_shard.reshape(r, 3 * width).astype(F32)
        pair_shard = plane_swap(pair_grad.reshape(4, r, 2 * nb * h), member)
        pair_shard = pair_shard.reshape(2, 2, r, 2, t, 2, h).transpose(3, 2, 4, 0, 5, 1, 6)
        pair_shard = pair_shard.reshape(2, r, 4 * nb * h).astype(F32)
        return (
            mixed,
            token_grad,
            gain_shards[:r],
            in_shard,
            kernel_shard,
            out_shard,
            gain_shards[r:],
            pair_shard[0],
            pair_shard[1],
            down_shard,
        )

    return local


def solution(mesh):
    t = mesh.shape["fsdp"] // 4
    grid = Mesh(mesh.devices.reshape(t, 2, 2, mesh.shape["rep"]), ("t", "b", "c", "y"))
    every = ("t", "b", "c", "y")
    in_specs = (
        P(every, None),
        P(every),
        P(every),
        P(every),
        P(every, None),
        P(None, every),
        P(every, None),
        P(every),
        P(every, None),
        P(every, None),
        P(every, None),
        P(every, None),
    )
    out_specs = (
        P(every, None),
        P(every, None),
        P(every),
        P(every, None),
        P(None, every),
        P(every, None),
        P(every),
        P(every, None),
        P(every, None),
        P(every, None),
    )
    return jax.shard_map(
        make_local(t), mesh=grid, in_specs=in_specs, out_specs=out_specs, check_vma=False
    )
```

time: 1940 us -> 382 us (0.20)
  waiting for transfers between devices: 1610 us -> 173 us
  blocking collectives: 149 us -> 0 us
  starting transfers between devices: 0.31 us -> 45.7 us
  local copies, waits for them, and re-layouts: 16.3 us -> 56.1 us
  matrix products: 97.8 us -> 59.5 us
  other arithmetic: 46.8 us -> 26.1 us
    reduce_scatter x2 -> x3, waiting for transfers between devices: 1350 us -> 43.7 us  [the longest x1 41.9 us: local(): lax.psum_scatter(pair_grad.reshape(nb, 4 * r, 2 * nb * h), COLUMN, scatte...]
    all_gather x5 -> x3, waiting for transfers between devices: 241 us -> 0.04 us  [the longest x1 0.02 us: local(): lax.all_gather(jnp.concatenate([conv_mine.reshape(4 * (3 * r + 16), share...]
    ppermute x0 -> x36, waiting for transfers between devices: none -> 129 us  [to_peer(): return lax.ppermute(values, PLANE, [(i, i ^ k) for i in range(4)])]
    unnamed x2 -> x0, blocking collectives: 82.5 us -> none
    all_gather x1 -> x0, blocking collectives: 66.2 us -> none  [local(): lax.all_gather(conv_kernel, ('fsdp', 'rep'), axis=1, tiled=True)]
    ppermute x0 -> x36, starting transfers between devices: none -> 44.8 us  [to_peer(): return lax.ppermute(values, PLANE, [(i, i ^ k) for i in range(4)])]
    dot_general x15 -> x12, matrix products: 97.8 us -> 59.5 us  [the longest x4 23 us: cols_by_cols(): lax.dot_general(left, right, (((1,), (1,)), ((), ())), preferred_element_...]
    concatenate x2 -> x6, other arithmetic: 35.7 us -> 4.01 us  [the longest x1 1.56 us: local(): jnp.concatenate([in_grad, out_grad, kernel_grad], axis=1)]
  transfers between devices with their start and end apart: 8 -> 42, of which waited for: 7 -> 31; matrix products, arithmetic and copies ran while one was open for 6% -> 27% of each run, Pallas kernels for 0% -> 0%
where the time goes in v1:
time: 382 us; the launch traced here: 376 us
  waiting for transfers between devices  173 us (45%)
  matrix products  59.5 us (16%)
  local copies, waits for them, and re-layouts  56.1 us (15%)
  starting transfers between devices  45.7 us (12%)
  other arithmetic  26.1 us (7%)
  between operations  16.1 us (4%)
    ppermute x36, waiting for transfers between devices, to_peer(): return lax.ppermute(values, PLANE, [(i, i ^ k) for i in range(4)])  129 us
    ppermute x36, starting transfers between devices, to_peer(): return lax.ppermute(values, PLANE, [(i, i ^ k) for i in range(4)])  44.8 us
    reduce_scatter x1, waiting for transfers between devices, local(): lax.psum_scatter(pair_grad.reshape(nb, 4 * r, 2 * nb * h), COLUMN, scatte...  41.9 us
    dot_general x4, matrix products, cols_by_cols(): lax.dot_general(left, right, (((1,), (1,)), ((), ())), preferred_element_...  23 us
    dot_general x4, matrix products, rows_by_rows(): lax.dot_general(left, right, (((0,), (0,)), ((), ())), preferred_element_...  17.7 us
    dot_general x1, matrix products, local(): both = jnp.dot(normed_two, pair_full, preferred_element_type=F32)  9.26 us
    unnamed x81, local copies, waits for them, and re-layouts  8.16 us
  transfers between devices with their start and end apart: 42, of which 31 were waited for; matrix products, arithmetic and copies ran while one was open for 27% of the time, Pallas kernels for 0%

profile of v1, /device:TPU:0, one launch (start us, length us, event | category | flops | bytes accessed | tf_op | source)
XLA Modules:
  0.0 376.2 jit_solution(11499995704136373403)
XLA Ops:
  10.1 3.0 collective-permute-start.3
  27.9 3.2 collective-permute-done.12
  38.0 10.8 %collective-permute-done = bf16[272,1024]{1,0:T(8,128)(2,1)S(1)} collective-permute-done((bf16[272,1024]{1,0:T(8,128)(2,1)S(1)}, bf16[272,1024]{1,0:T(8,128)(2,1)S(1)}, u32[]{:S(2)}, u32[]{:S(2)}) %collective-permute-start) | collective-permute-done | bytes 557088 | tf_op jit(solution)/shard_map/ppermute | solution.py:24
  50.6 7.9 %collective-permute-done.2 = bf16[272,1024]{1,0:T(8,128)(2,1)S(1)} collective-permute-done((bf16[272,1024]{1,0:T(8,128)(2,1)S(1)}, bf16[272,1024]{1,0:T(8,128)(2,1)S(1)}, u32[]{:S(2)}, u32[]{:S(2)}) %collective-permute-start.2) | collective-permute-done | bytes 557088 | tf_op jit(solution)/shard_map/ppermute | solution.py:24
  66.3 4.4 %fusion.50 = f32[1024,768]{1,0:T(8,128)S(1)} fusion(bf16[1024,768]{1,0:T(8,128)(2,1)S(1)} %bitcast.185, f32[1024,1024]{1,0:T(8,128)} %copy-done, f32[1024]{0:T(1024)S(1)} %bitcast.244, f32[1024]{0:T(1024)S(1)} %add_rsqrt_fusion), kind=kOutput, calls=%fused_computation.184 | convolution fusion | flops 1613758464 | bytes 8921088 | tf_op jit(solution)/shard_map/dot_general | solution.py:146
  81.6 10.5 %collective-permute-done.6 = bf16[256,1024]{1,0:T(8,128)(2,1)S(1)} collective-permute-done((bf16[256,1024]{1,0:T(8,128)(2,1)S(1)}, bf16[256,1024]{1,0:T(8,128)(2,1)S(1)}, u32[]{:S(2)}, u32[]{:S(2)}) %collective-permute-start.6) | collective-permute-done | bytes 524320 | tf_op jit(solution)/shard_map/ppermute | solution.py:24
  94.3 5.8 %collective-permute-done.8 = bf16[256,1024]{1,0:T(8,128)(2,1)S(1)} collective-permute-done((bf16[256,1024]{1,0:T(8,128)(2,1)S(1)}, bf16[256,1024]{1,0:T(8,128)(2,1)S(1)}, u32[]{:S(2)}, u32[]{:S(2)}) %collective-permute-start.8) | collective-permute-done | bytes 524320 | tf_op jit(solution)/shard_map/ppermute | solution.py:24
  112.1 4.8 %collective-permute-done.10 = bf16[256,1024]{1,0:T(8,128)(2,1)} collective-permute-done((bf16[256,1024]{1,0:T(8,128)(2,1)}, bf16[256,1024]{1,0:T(8,128)(2,1)}, u32[]{:S(2)}, u32[]{:S(2)}) %collective-permute-start.10) | collective-permute-done | bytes 524320 | tf_op jit(solution)/shard_map/ppermute | solution.py:24
  118.9 10.9 %collective-permute-done.11 = bf16[256,1024]{1,0:T(8,128)(2,1)} collective-permute-done((bf16[256,1024]{1,0:T(8,128)(2,1)}, bf16[256,1024]{1,0:T(8,128)(2,1)}, u32[]{:S(2)}, u32[]{:S(2)}) %collective-permute-start.11) | collective-permute-done | bytes 524320 | tf_op jit(solution)/shard_map/ppermute | solution.py:24
  131.8 9.3 %fusion.26 = f32[1024,2304]{1,0:T(8,128)} fusion(bf16[1024,2304]{1,0:T(8,128)(2,1)S(1)} %bitcast.188, bf16[256,1024]{1,0:T(8,128)(2,1)} %collective-permute-done.11, bf16[256,1024]{1,0:T(8,128)(2,1)} %collective-permute-done.10, bf16[256,1024]{1,0:T(8,128)(2,1)} %collective-permute-done.9, bf16[256,1024]{1,0:T(8,128)(2,1)} %multiply_convert_fusion.7), kind=kOutput, calls=%fused_computation.89 | convolution fusion | flops 4840226816 | bytes 16252928 | tf_op jit(solution)/shard_map/dot_general | solution.py:163
  141.1 5.4 %collective-permute-done.18 = bf16[256,1024]{1,0:T(8,128)(2,1)} collective-permute-done((bf16[256,1024]{1,0:T(8,128)(2,1)}, bf16[256,1024]{1,0:T(8,128)(2,1)}, u32[]{:S(2)}, u32[]{:S(2)}) %collective-permute-start.18) | collective-permute-done | bytes 524320 | tf_op jit(solution)/shard_map/ppermute | solution.py:24
  146.5 9.0 %multiply_convert_fusion.1 = (bf16[1024,1152]{1,0:T(8,128)(2,1)S(1)}, bf16[1024,1152]{1,0:T(8,128)(2,1)S(1)}, bf16[1024,1152]{1,0:T(8,128)(2,1)S(1)}) fusion(f32[1024,2304]{1,0:T(8,128)} %fusion.26, bf16[1152,1024]{1,0:T(8,128)(2,1)} %all-gather.7.cloned.1.call-done, bf16[256,1024]{1,0:T(8,128)(2,1)} %collective-permute-done.20, ...), kind=kOutput, calls=%fused_computation.3 | convolution fusion | flops 2442002432 | bytes 20971520 | tf_op jit(solution)/shard_map/dot_general | solution.py:20
  155.5 6.6 %fusion.63 = (bf16[1024,1024]{1,0:T(8,128)(2,1)S(1)}, f32[1024,1024]{1,0:T(8,128)}) fusion(bf16[1024,2304]{1,0:T(8,128)(2,1)S(1)} %bitcast.189, bf16[1024,1152]{1,0:T(8,128)(2,1)S(1)} %get-tuple-element.48, bf16[1024,1152]{1,0:T(8,128)(2,1)S(1)} %get-tuple-element.47), kind=kOutput, calls=%fused_computation.195 | convolution fusion | flops 4842323968 | bytes 15728640 | tf_op jit(solution)/shard_map/dot_general | solution.py:20
  166.8 4.4 %fusion.64 = (bf16[1024,1024]{1,0:T(8,128)(2,1)S(1)}, f32[1024,1024]{1,0:T(8,128)}) fusion(bf16[1024,1152]{1,0:T(8,128)(2,1)S(1)} %get-tuple-element.49, bf16[1152,1024]{1,0:T(8,128)(2,1)S(1)} %copy-done.27), kind=kOutput, calls=%fused_computation.196 | convolution fusion | flops 2416967680 | bytes 11010048 | tf_op jit(solution)/shard_map/dot_general | solution.py:179
  174.7 5.6 %convolution_convert_fusion.1 = bf16[1152,1024]{1,0:T(8,128)(2,1)} fusion(bf16[1024,1152]{1,0:T(8,128)(2,1)S(1)} %get-tuple-element.49, bf16[256,1024]{1,0:T(8,128)(2,1)} %collective-permute-done.20, bf16[256,1024]{1,0:T(8,128)(2,1)} %collective-permute-done.19, bf16[256,1024]{1,0:T(8,128)(2,1)} %collective-permute-done.18, bf16[256,1024]{1,0:T(8,128)(2,1)} %fusion.23), kind=kOutput, calls=%fused_computation.10 | convolution fusion | flops 2425487360 | bytes 6815744 | tf_op jit(solution)/shard_map/dot_general | solution.py:16
  180.6 4.9 %collective-permute-done.21 = bf16[256,1024]{1,0:T(8,128)(2,1)} collective-permute-done((bf16[256,1024]{1,0:T(8,128)(2,1)}, bf16[256,1024]{1,0:T(8,128)(2,1)}, u32[]{:S(2)}, u32[]{:S(2)}) %collective-permute-start.21) | collective-permute-done | bytes 524320 | tf_op jit(solution)/shard_map/ppermute | solution.py:24
  186.8 4.6 %collective-permute-done.23 = bf16[256,1024]{1,0:T(8,128)(2,1)} collective-permute-done((bf16[256,1024]{1,0:T(8,128)(2,1)}, bf16[256,1024]{1,0:T(8,128)(2,1)}, u32[]{:S(2)}, u32[]{:S(2)}) %collective-permute-start.23) | collective-permute-done | bytes 524320 | tf_op jit(solution)/shard_map/ppermute | solution.py:24
  193.5 6.1 %collective-permute-done.15 = bf16[256,1024]{1,0:T(8,128)(2,1)} collective-permute-done((bf16[256,1024]{1,0:T(8,128)(2,1)}, bf16[256,1024]{1,0:T(8,128)(2,1)}, u32[]{:S(2)}, u32[]{:S(2)}) %collective-permute-start.15) | collective-permute-done | bytes 524320 | tf_op jit(solution)/shard_map/ppermute | solution.py:24
  200.0 5.3 %collective-permute-done.17 = bf16[256,1024]{1,0:T(8,128)(2,1)S(1)} collective-permute-done((bf16[256,1024]{1,0:T(8,128)(2,1)}, bf16[256,1024]{1,0:T(8,128)(2,1)S(1)}, u32[]{:S(2)}, u32[]{:S(2)}) %collective-permute-start.17) | collective-permute-done | bytes 524320 | tf_op jit(solution)/shard_map/ppermute | solution.py:24
  205.3 3.4 fusion.52
  212.3 9.7 %collective-permute-done.24 = bf16[256,1024]{1,0:T(8,128)(2,1)S(1)} collective-permute-done((bf16[256,1024]{1,0:T(8,128)(2,1)S(1)}, bf16[256,1024]{1,0:T(8,128)(2,1)S(1)}, u32[]{:S(2)}, u32[]{:S(2)}) %collective-permute-start.24) | collective-permute-done | bytes 524320 | tf_op jit(solution)/shard_map/ppermute | solution.py:24
  222.3 5.4 %collective-permute-done.26 = bf16[256,1024]{1,0:T(8,128)(2,1)S(1)} collective-permute-done((bf16[256,1024]{1,0:T(8,128)(2,1)S(1)}, bf16[256,1024]{1,0:T(8,128)(2,1)S(1)}, u32[]{:S(2)}, u32[]{:S(2)}) %collective-permute-start.26) | collective-permute-done | bytes 524320 | tf_op jit(solution)/shard_map/ppermute | solution.py:24
  236.8 3.2 convolution_convert_fusion.2
  240.0 4.2 %reshape.315 = bf16[4,2,2,2,32,3,256]{6,5,4,3,2,1,0:T(4,128)(2,1)S(1)} reshape(bf16[1024,768]{1,0:T(8,128)(2,1)} %convolution_convert_fusion.2) | data formatting | bytes 3145728 | tf_op jit(solution)/shard_map/reshape | solution.py:217
  246.4 5.0 %multiply_reduce_fusion = (bf16[1024]{0:T(1024)(128)(2,1)S(1)}, bf16[1024,1024]{1,0:T(8,128)(2,1)S(1)}, f32[1024,1024]{1,0:T(8,128)}) fusion(f32[1024,1024]{1,0:T(8,128)} %copy-done, f32[1024]{0:T(1024)S(1)} %add_rsqrt_fusion, bf16[1024,768]{1,0:T(8,128)(2,1)S(1)} %bitcast.186, bf16[1024,256]{1,0:T(8,128)(2,1)S(1)} %bitcast.209, ...), kind=kOutput, calls=%fused_computation.7 | convolution fusion | flops 1619524608 | bytes 13637632 | tf_op jit(solution)/shard_map/dot_general | solution.py:20
  255.4 8.2 %convolution_convert_fusion = bf16[1024,2304]{1,0:T(8,128)(2,1)S(1)} fusion(bf16[1024,1152]{1,0:T(8,128)(2,1)} %copy-done.33, bf16[1024,1152]{1,0:T(8,128)(2,1)} %copy-done.32, bf16[256,1024]{1,0:T(8,128)(2,1)} %collective-permute-done.11, bf16[256,1024]{1,0:T(8,128)(2,1)} %collective-permute-done.10, bf16[256,1024]{1,0:T(8,128)(2,1)} %collective-permute-done.9, ...), kind=kOutput, calls=%fused_computation | convolution fusion | flops 4852023296 | bytes 11534336 | tf_op jit(solution)/shard_map/dot_general | solution.py:16
  269.9 8.4 %collective-permute-done.27 = bf16[256,1024]{1,0:T(8,128)(2,1)S(1)} collective-permute-done((bf16[256,1024]{1,0:T(8,128)(2,1)S(1)}, bf16[256,1024]{1,0:T(8,128)(2,1)S(1)}, u32[]{:S(2)}, u32[]{:S(2)}) %collective-permute-start.27) | collective-permute-done | bytes 524320 | tf_op jit(solution)/shard_map/ppermute | solution.py:24
  278.5 5.4 %collective-permute-done.29 = bf16[256,1024]{1,0:T(8,128)(2,1)S(1)} collective-permute-done((bf16[256,1024]{1,0:T(8,128)(2,1)S(1)}, bf16[256,1024]{1,0:T(8,128)(2,1)S(1)}, u32[]{:S(2)}, u32[]{:S(2)}) %collective-permute-start.29) | collective-permute-done | bytes 524320 | tf_op jit(solution)/shard_map/ppermute | solution.py:24
  285.7 2.7 fusion.9
  303.7 2.7 reshape.332
  306.5 41.9 %reduce-scatter.6.cloned.1.call-done = bf16[1,128,2304]{2,1,0:T(8,128)(2,1)} async-done(((bf16[8,128,2304]{2,1,0:T(8,128)(2,1)}), bf16[1,128,2304]{2,1,0:T(8,128)(2,1)}) %reduce-scatter.6.cloned.1.call-update) | async-done | bytes 589840 | tf_op jit(solution)/shard_map/reduce_scatter | solution.py:178
  358.8 3.6 reshape.334
  (290 shorter events, 133.9 us)
Async XLA Ops:
  7.2 54.7 %all-gather.9.cloned.1.call-start = ((), (), s32[]{:S(2)}) async-start(), calls=%async_computation.8 | async-start | bytes 2654208 | tf_op jit(solution)/shard_map/all_gather | solution.py:107
  20.6 88.8 %all-gather.5.cloned.1.call-start = ((), (), s32[]{:S(2)}) async-start(), calls=%async_computation.3 | async-start | bytes 5308416 | tf_op jit(solution)/shard_map/all_gather | solution.py:122
  25.5 7.0 %collective-permute-start.14 = (bf16[32,2304]{1,0:T(8,128)(2,1)S(1)}, bf16[32,2304]{1,0:T(8,128)(2,1)S(1)}, u32[]{:S(2)}, u32[]{:S(2)}) collective-permute-start(bf16[32,2304]{1,0:T(8,128)(2,1)S(1)} %get-tuple-element.83), channel_id=1, source_target_pairs={{0,5},{1,4},{4,1},{5,0},{2,7},{3,6},{6,3},{7,2},{8,13},{9,12},{12,... | collective-permute-start | bytes 442376 | tf_op jit(solution)/shard_map/ppermute | solution.py:24
  33.6 112.8 %all-gather.7.cloned.1.call-start = ((), (), s32[]{:S(2)}) async-start(), calls=%async_computation.4 | async-start | bytes 2654208 | tf_op jit(solution)/shard_map/all_gather | solution.py:125
  34.0 14.7 %collective-permute-start = (bf16[272,1024]{1,0:T(8,128)(2,1)S(1)}, bf16[272,1024]{1,0:T(8,128)(2,1)S(1)}, u32[]{:S(2)}, u32[]{:S(2)}) collective-permute-start(bf16[272,1024]{1,0:T(8,128)(2,1)S(1)} %constant_dynamic-update-slice_fusion), channel_id=1, source_target_pairs={{0,1},{1,0},{4,5},{5,4},{2,3},{3,2},{6,7},{7,6},{8,9},{9,8},{12,13... | collective-permute-start | bytes 1671176 | tf_op jit(solution)/shard_map/ppermute | solution.py:24
  35.0 15.6 %collective-permute-start.1 = (bf16[272,1024]{1,0:T(8,128)(2,1)S(1)}, bf16[272,1024]{1,0:T(8,128)(2,1)S(1)}, u32[]{:S(2)}, u32[]{:S(2)}) collective-permute-start(bf16[272,1024]{1,0:T(8,128)(2,1)S(1)} %constant_dynamic-update-slice_fusion), channel_id=1, source_target_pairs={{0,4},{1,5},{4,0},{5,1},{2,6},{3,7},{6,2},{7,3},{8,12},{9,13},{12,... | collective-permute-start | bytes 1671176 | tf_op jit(solution)/shard_map/ppermute | solution.py:24
  36.0 22.5 %collective-permute-start.2 = (bf16[272,1024]{1,0:T(8,128)(2,1)S(1)}, bf16[272,1024]{1,0:T(8,128)(2,1)S(1)}, u32[]{:S(2)}, u32[]{:S(2)}) collective-permute-start(bf16[272,1024]{1,0:T(8,128)(2,1)S(1)} %constant_dynamic-update-slice_fusion), channel_id=1, source_target_pairs={{0,5},{1,4},{4,1},{5,0},{2,7},{3,6},{6,3},{7,2},{8,13},{9,12},{12,... | collective-permute-start | bytes 1671176 | tf_op jit(solution)/shard_map/ppermute | solution.py:24
  37.6 250.7 %reduce-scatter.8.cloned.1.call-start = ((), (), s32[]{:S(2)}) async-start(), calls=%async_computation.7 | async-start | bytes 2654208 | tf_op jit(solution)/shard_map/reduce_scatter | solution.py:175
  78.0 14.0 %collective-permute-start.6 = (bf16[256,1024]{1,0:T(8,128)(2,1)S(1)}, bf16[256,1024]{1,0:T(8,128)(2,1)S(1)}, u32[]{:S(2)}, u32[]{:S(2)}) collective-permute-start(bf16[256,1024]{1,0:T(8,128)(2,1)S(1)} %get-tuple-element.63), channel_id=1, source_target_pairs={{0,1},{1,0},{4,5},{5,4},{2,3},{3,2},{6,7},{7,6},{8,9},{9,8},{12,13... | collective-permute-start | bytes 1572872 | tf_op jit(solution)/shard_map/ppermute | solution.py:24
  79.4 14.9 %collective-permute-start.7 = (bf16[256,1024]{1,0:T(8,128)(2,1)S(1)}, bf16[256,1024]{1,0:T(8,128)(2,1)S(1)}, u32[]{:S(2)}, u32[]{:S(2)}) collective-permute-start(bf16[256,1024]{1,0:T(8,128)(2,1)S(1)} %get-tuple-element.65), channel_id=1, source_target_pairs={{0,4},{1,5},{4,0},{5,1},{2,6},{3,7},{6,2},{7,3},{8,12},{9,13},{12,... | collective-permute-start | bytes 1572872 | tf_op jit(solution)/shard_map/ppermute | solution.py:24
  80.5 19.5 %collective-permute-start.8 = (bf16[256,1024]{1,0:T(8,128)(2,1)S(1)}, bf16[256,1024]{1,0:T(8,128)(2,1)S(1)}, u32[]{:S(2)}, u32[]{:S(2)}) collective-permute-start(bf16[256,1024]{1,0:T(8,128)(2,1)S(1)} %get-tuple-element.64), channel_id=1, source_target_pairs={{0,5},{1,4},{4,1},{5,0},{2,7},{3,6},{6,3},{7,2},{8,13},{9,12},{12,... | collective-permute-start | bytes 1572872 | tf_op jit(solution)/shard_map/ppermute | solution.py:24
  101.5 15.4 %collective-permute-start.10 = (bf16[256,1024]{1,0:T(8,128)(2,1)}, bf16[256,1024]{1,0:T(8,128)(2,1)}, u32[]{:S(2)}, u32[]{:S(2)}) collective-permute-start(bf16[256,1024]{1,0:T(8,128)(2,1)} %multiply_convert_fusion.7), channel_id=1, source_target_pairs={{0,4},{1,5},{4,0},{5,1},{2,6},{3,7},{6,2},{7,3},{8,12},{9,13},{12,... | collective-permute-start | bytes 1572872 | tf_op jit(solution)/shard_map/ppermute | solution.py:24
  103.8 26.1 %collective-permute-start.11 = (bf16[256,1024]{1,0:T(8,128)(2,1)}, bf16[256,1024]{1,0:T(8,128)(2,1)}, u32[]{:S(2)}, u32[]{:S(2)}) collective-permute-start(bf16[256,1024]{1,0:T(8,128)(2,1)} %multiply_convert_fusion.7), channel_id=1, source_target_pairs={{0,5},{1,4},{4,1},{5,0},{2,7},{3,6},{6,3},{7,2},{8,13},{9,12},{12,... | collective-permute-start | bytes 1572872 | tf_op jit(solution)/shard_map/ppermute | solution.py:24
  105.4 26.4 %collective-permute-start.9 = (bf16[256,1024]{1,0:T(8,128)(2,1)}, bf16[256,1024]{1,0:T(8,128)(2,1)}, u32[]{:S(2)}, u32[]{:S(2)}) collective-permute-start(bf16[256,1024]{1,0:T(8,128)(2,1)} %multiply_convert_fusion.7), channel_id=1, source_target_pairs={{0,1},{1,0},{4,5},{5,4},{2,3},{3,2},{6,7},{7,6},{8,9},{9,8},{12,13... | collective-permute-start | bytes 1572872 | tf_op jit(solution)/shard_map/ppermute | solution.py:24
  107.0 39.4 %collective-permute-start.18 = (bf16[256,1024]{1,0:T(8,128)(2,1)}, bf16[256,1024]{1,0:T(8,128)(2,1)}, u32[]{:S(2)}, u32[]{:S(2)}) collective-permute-start(bf16[256,1024]{1,0:T(8,128)(2,1)} %fusion.23), channel_id=1, source_target_pairs={{0,1},{1,0},{4,5},{5,4},{2,3},{3,2},{6,7},{7,6},{8,9},{9,8},{12,13... | collective-permute-start | bytes 1572872 | tf_op jit(solution)/shard_map/ppermute | solution.py:24
  109.0 37.4 %collective-permute-start.19 = (bf16[256,1024]{1,0:T(8,128)(2,1)}, bf16[256,1024]{1,0:T(8,128)(2,1)}, u32[]{:S(2)}, u32[]{:S(2)}) collective-permute-start(bf16[256,1024]{1,0:T(8,128)(2,1)} %fusion.23), channel_id=1, source_target_pairs={{0,4},{1,5},{4,0},{5,1},{2,6},{3,7},{6,2},{7,3},{8,12},{9,13},{12,... | collective-permute-start | bytes 1572872 | tf_op jit(solution)/shard_map/ppermute | solution.py:24
  116.9 29.5 %collective-permute-start.20 = (bf16[256,1024]{1,0:T(8,128)(2,1)}, bf16[256,1024]{1,0:T(8,128)(2,1)}, u32[]{:S(2)}, u32[]{:S(2)}) collective-permute-start(bf16[256,1024]{1,0:T(8,128)(2,1)} %fusion.23), channel_id=1, source_target_pairs={{0,5},{1,4},{4,1},{5,0},{2,7},{3,6},{6,3},{7,2},{8,13},{9,12},{12,... | collective-permute-start | bytes 1572872 | tf_op jit(solution)/shard_map/ppermute | solution.py:24
  163.3 22.2 %collective-permute-start.21 = (bf16[256,1024]{1,0:T(8,128)(2,1)}, bf16[256,1024]{1,0:T(8,128)(2,1)}, u32[]{:S(2)}, u32[]{:S(2)}) collective-permute-start(bf16[256,1024]{1,0:T(8,128)(2,1)} %get-tuple-element.57), channel_id=1, source_target_pairs={{0,1},{1,0},{4,5},{5,4},{2,3},{3,2},{6,7},{7,6},{8,9},{9,8},{12,13... | collective-permute-start | bytes 1572872 | tf_op jit(solution)/shard_map/ppermute | solution.py:24
  164.1 22.6 %collective-permute-start.22 = (bf16[256,1024]{1,0:T(8,128)(2,1)}, bf16[256,1024]{1,0:T(8,128)(2,1)}, u32[]{:S(2)}, u32[]{:S(2)}) collective-permute-start(bf16[256,1024]{1,0:T(8,128)(2,1)} %get-tuple-element.59), channel_id=1, source_target_pairs={{0,4},{1,5},{4,0},{5,1},{2,6},{3,7},{6,2},{7,3},{8,12},{9,13},{12,... | collective-permute-start | bytes 1572872 | tf_op jit(solution)/shard_map/ppermute | solution.py:24
  165.6 25.7 %collective-permute-start.23 = (bf16[256,1024]{1,0:T(8,128)(2,1)}, bf16[256,1024]{1,0:T(8,128)(2,1)}, u32[]{:S(2)}, u32[]{:S(2)}) collective-permute-start(bf16[256,1024]{1,0:T(8,128)(2,1)} %get-tuple-element.58), channel_id=1, source_target_pairs={{0,5},{1,4},{4,1},{5,0},{2,7},{3,6},{6,3},{7,2},{8,13},{9,12},{12,... | collective-permute-start | bytes 1572872 | tf_op jit(solution)/shard_map/ppermute | solution.py:24
  172.4 27.2 %collective-permute-start.15 = (bf16[256,1024]{1,0:T(8,128)(2,1)}, bf16[256,1024]{1,0:T(8,128)(2,1)}, u32[]{:S(2)}, u32[]{:S(2)}) collective-permute-start(bf16[256,1024]{1,0:T(8,128)(2,1)} %get-tuple-element.60), channel_id=1, source_target_pairs={{0,1},{1,0},{4,5},{5,4},{2,3},{3,2},{6,7},{7,6},{8,9},{9,8},{12,13... | collective-permute-start | bytes 1572872 | tf_op jit(solution)/shard_map/ppermute | solution.py:24
  173.2 26.7 %collective-permute-start.16 = (bf16[256,1024]{1,0:T(8,128)(2,1)}, bf16[256,1024]{1,0:T(8,128)(2,1)}, u32[]{:S(2)}, u32[]{:S(2)}) collective-permute-start(bf16[256,1024]{1,0:T(8,128)(2,1)} %get-tuple-element.62), channel_id=1, source_target_pairs={{0,4},{1,5},{4,0},{5,1},{2,6},{3,7},{6,2},{7,3},{8,12},{9,13},{12,... | collective-permute-start | bytes 1572872 | tf_op jit(solution)/shard_map/ppermute | solution.py:24
  180.4 111.7 %reduce-scatter.4.cloned.1.call-start = ((), (), s32[]{:S(2)}) async-start(), calls=%async_computation.5 | async-start | bytes 2727936 | tf_op jit(solution)/shard_map/reduce_scatter | solution.py:231
  185.5 19.8 %collective-permute-start.17 = (bf16[256,1024]{1,0:T(8,128)(2,1)}, bf16[256,1024]{1,0:T(8,128)(2,1)S(1)}, u32[]{:S(2)}, u32[]{:S(2)}) collective-permute-start(bf16[256,1024]{1,0:T(8,128)(2,1)} %get-tuple-element.61), channel_id=1, source_target_pairs={{0,5},{1,4},{4,1},{5,0},{2,7},{3,6},{6,3},{7,2},{8,13},{9,12},{12,... | collective-permute-start | bytes 1572872 | tf_op jit(solution)/shard_map/ppermute | solution.py:24
  208.7 13.3 %collective-permute-start.24 = (bf16[256,1024]{1,0:T(8,128)(2,1)S(1)}, bf16[256,1024]{1,0:T(8,128)(2,1)S(1)}, u32[]{:S(2)}, u32[]{:S(2)}) collective-permute-start(bf16[256,1024]{1,0:T(8,128)(2,1)S(1)} %get-tuple-element.40), channel_id=1, source_target_pairs={{0,1},{1,0},{4,5},{5,4},{2,3},{3,2},{6,7},{7,6},{8,9},{9,8},{12,13... | collective-permute-start | bytes 1572872 | tf_op jit(solution)/shard_map/ppermute | solution.py:24
  210.4 11.9 %collective-permute-start.25 = (bf16[256,1024]{1,0:T(8,128)(2,1)S(1)}, bf16[256,1024]{1,0:T(8,128)(2,1)S(1)}, u32[]{:S(2)}, u32[]{:S(2)}) collective-permute-start(bf16[256,1024]{1,0:T(8,128)(2,1)S(1)} %get-tuple-element.40), channel_id=1, source_target_pairs={{0,4},{1,5},{4,0},{5,1},{2,6},{3,7},{6,2},{7,3},{8,12},{9,13},{12,... | collective-permute-start | bytes 1572872 | tf_op jit(solution)/shard_map/ppermute | solution.py:24
  210.9 16.8 %collective-permute-start.26 = (bf16[256,1024]{1,0:T(8,128)(2,1)S(1)}, bf16[256,1024]{1,0:T(8,128)(2,1)S(1)}, u32[]{:S(2)}, u32[]{:S(2)}) collective-permute-start(bf16[256,1024]{1,0:T(8,128)(2,1)S(1)} %get-tuple-element.40), channel_id=1, source_target_pairs={{0,5},{1,4},{4,1},{5,0},{2,7},{3,6},{6,3},{7,2},{8,13},{9,12},{12,... | collective-permute-start | bytes 1572872 | tf_op jit(solution)/shard_map/ppermute | solution.py:24
  255.2 93.2 %reduce-scatter.6.cloned.1.call-start = ((), (), s32[]{:S(2)}) async-start(), calls=%async_computation.6 | async-start | bytes 5308416 | tf_op jit(solution)/shard_map/reduce_scatter | solution.py:178
  266.4 12.0 %collective-permute-start.27 = (bf16[256,1024]{1,0:T(8,128)(2,1)S(1)}, bf16[256,1024]{1,0:T(8,128)(2,1)S(1)}, u32[]{:S(2)}, u32[]{:S(2)}) collective-permute-start(bf16[256,1024]{1,0:T(8,128)(2,1)S(1)} %get-tuple-element.54), channel_id=1, source_target_pairs={{0,1},{1,0},{4,5},{5,4},{2,3},{3,2},{6,7},{7,6},{8,9},{9,8},{12,13... | collective-permute-start | bytes 1572872 | tf_op jit(solution)/shard_map/ppermute | solution.py:24
  268.1 10.4 %collective-permute-start.28 = (bf16[256,1024]{1,0:T(8,128)(2,1)S(1)}, bf16[256,1024]{1,0:T(8,128)(2,1)S(1)}, u32[]{:S(2)}, u32[]{:S(2)}) collective-permute-start(bf16[256,1024]{1,0:T(8,128)(2,1)S(1)} %get-tuple-element.56), channel_id=1, source_target_pairs={{0,4},{1,5},{4,0},{5,1},{2,6},{3,7},{6,2},{7,3},{8,12},{9,13},{12,... | collective-permute-start | bytes 1572872 | tf_op jit(solution)/shard_map/ppermute | solution.py:24
  268.5 15.5 %collective-permute-start.29 = (bf16[256,1024]{1,0:T(8,128)(2,1)S(1)}, bf16[256,1024]{1,0:T(8,128)(2,1)S(1)}, u32[]{:S(2)}, u32[]{:S(2)}) collective-permute-start(bf16[256,1024]{1,0:T(8,128)(2,1)S(1)} %get-tuple-element.55), channel_id=1, source_target_pairs={{0,5},{1,4},{4,1},{5,0},{2,7},{3,6},{6,3},{7,2},{8,13},{9,12},{12,... | collective-permute-start | bytes 1572872 | tf_op jit(solution)/shard_map/ppermute | solution.py:24
  349.6 6.8 %collective-permute-start.33 = (bf16[32,2304]{1,0:T(8,128)(2,1)S(1)}, bf16[32,2304]{1,0:T(8,128)(2,1)S(1)}, u32[]{:S(2)}, u32[]{:S(2)}) collective-permute-start(bf16[32,2304]{1,0:T(8,128)(2,1)S(1)} %get-tuple-element.77), channel_id=1, source_target_pairs={{0,1},{1,0},{4,5},{5,4},{2,3},{3,2},{6,7},{7,6},{8,9},{9,8},{12,13... | collective-permute-start | bytes 442376 | tf_op jit(solution)/shard_map/ppermute | solution.py:24
  (44 other events, 325.6 us)
Sparse Core Ops, SparseCore 0:
  20.7 31.0 all-gather.8
  54.0 50.8 all-gather.4
  106.5 30.4 all-gather.6
  180.5 36.5 reduce-scatter.7
  255.3 36.6 reduce-scatter.3
  294.3 54.0 reduce-scatter.5

commit v2 on v1

--- a/solution.py
+++ b/solution.py
@@ -44,6 +44,11 @@
     got = [pick(blocks, member)] + [to_peer(pick(blocks, member ^ k), k) for k in (1, 2, 3)]
     got = jnp.stack(got)
     return jnp.stack([pick(got, member ^ j) for j in range(4)])
+
+
+def after(values, other):
+    one = other[(slice(0, 1),) * other.ndim].reshape(())
+    return values + jnp.minimum(jnp.abs(one), 0).astype(values.dtype)
 
 
 def norm_back(grad_norm, source, scale, gain):
@@ -118,12 +123,11 @@
             return w.reshape(r, t, 2, 2, 2, h).transpose(2, 4, 0, 1, 3, 5).reshape(4, r, nb * h)
 
         pair = jnp.concatenate([ff_blocks(gate_weight), ff_blocks(up_weight)], axis=2)
-        pair_mine = plane_swap(pair, member).reshape(4 * r, 2 * nb * h)
+        pair_mine = plane_swap(after(pair, gathered[3]), member).reshape(4 * r, 2 * nb * h)
         pair_all = lax.all_gather(pair_mine, COLUMN)
         pair_full = pair_all.reshape(t, 2, 2, 2 * r, 2 * nb * h).transpose(0, 2, 1, 3, 4)
         pair_full = lax.optimization_barrier(pair_full.reshape(width, 2 * nb * h))
         down_full = lax.all_gather(down_weight, COLUMN, axis=0, tiled=True)
-        dffn = jnp.concatenate(plane_gather(dffn_own))
 
         split = 4 * (3 * r + 16)
         head = conv_all[:, :split].reshape(t, 2, 2, 2, 3 * r + 16, share)
@@ -159,29 +163,38 @@
 
         scale_two = lax.rsqrt(jnp.mean(hidden * hidden, axis=1, keepdims=True) + EPS)
         normed_two_own = (hidden * scale_two * gain_second).astype(BF)
-        normed_two = jnp.concatenate(plane_gather(normed_two_own))
+        normed_two = plane_gather(normed_two_own)
+        dffn = jnp.concatenate(plane_gather(after(dffn_own, normed_two[3])))
+        normed_two = jnp.concatenate(normed_two)
         both = jnp.dot(normed_two, pair_full, preferred_element_type=F32)
         gate = both[:, : nb * h]
         upper = both[:, nb * h :]
         sigma = jax.nn.sigmoid(gate)
         swish = gate * sigma
         act = (swish * upper).astype(BF)
-        dact = cols_by_cols(dffn, down_full)
+        down_grad = rows_by_rows(act, dffn).astype(BF)
+        down_sum = lax.psum_scatter(down_grad, COLUMN, scatter_dimension=0, tiled=True)
+        down_shard = down_sum.astype(F32)
+        dact = after(cols_by_cols(dffn, down_full), down_grad)
         dgate = (dact * upper * sigma * (1.0 + gate * (1.0 - sigma))).astype(BF)
         dupper = (dact * swish).astype(BF)
         dboth = jnp.concatenate([dgate, dupper], axis=1)
-        dnormed_two = plane_sum(cols_by_cols(dboth, pair_full).reshape(4, slots, width))
-        down_grad = rows_by_rows(act, dffn).astype(BF)
-        down_shard = lax.psum_scatter(down_grad, COLUMN, scatter_dimension=0, tiled=True).astype(F32)
-        pair_grad = lax.optimization_barrier(rows_by_rows(normed_two, dboth).astype(BF))
+        dnormed_part = cols_by_cols(dboth, pair_full).reshape(4, slots, width)
+        pair_grad = after(rows_by_rows(normed_two, dboth), dnormed_part)
+        pair_grad = lax.optimization_barrier(pair_grad.astype(BF))
         pair_grad = pair_grad.reshape(t, 2, 2, 2 * r, 2 * nb * h).transpose(0, 2, 1, 3, 4)
-        pair_grad = lax.psum_scatter(pair_grad.reshape(nb, 4 * r, 2 * nb * h), COLUMN, scatter_dimension=0)
-        ffn = plane_sum(jnp.dot(act, down_full, preferred_element_type=F32).reshape(4, slots, width))
-        mixed = (live * (hidden + ffn)).astype(BF)
+        pair_grad = after(pair_grad.reshape(nb, 4 * r, 2 * nb * h), down_sum)
+        pair_sum = lax.psum_scatter(pair_grad, COLUMN, scatter_dimension=0)
+        dnormed_two = after(plane_sum(dnormed_part), pair_grad)
         hidden_part, gain_two_grad = norm_back(dnormed_two, hidden, scale_two, gain_second)
         dhidden = dout + hidden_part
 
-        dbranch = jnp.concatenate(plane_gather(dhidden.astype(BF)))
+        dbranch = plane_gather(dhidden.astype(BF))
+        dbranch_last = dbranch[3]
+        dbranch = jnp.concatenate(dbranch)
+        ffn = after(jnp.dot(act, down_full, preferred_element_type=F32), dbranch_last)
+        ffn = plane_sum(ffn.reshape(4, slots, width))
+        mixed = (live * (hidden + ffn)).astype(BF)
         dmixer = cols_by_cols(dbranch, out_full).reshape(4, slots, share)
         dsecond = dmixer * convolved
         dconv = dmixer * second
@@ -214,20 +227,28 @@
             (kernel_grad, gain_one_grad, gain_two_grad)
         )
         in_grad = lax.optimization_barrier(rows_by_rows(normed_one, dprojected).astype(BF))
-        in_grad = in_grad.reshape(t, 2, 2, 2, r, 3, share).transpose(0, 2, 1, 3, 5, 4, 6)
+        in_grad = jnp.stack(
+            [
+                in_grad[:, i * share : (i + 1) * share].reshape(t, 2, 2, 2, r, share).transpose(0, 2, 1, 3, 4, 5)
+                for i in range(3)
+            ],
+            axis=4,
+        )
         in_grad = in_grad.reshape(nb, 4, 3 * r, share)
         gain_grads = jnp.stack([gain_one_grad, gain_two_grad]).astype(BF)
         gain_grads = gain_grads.reshape(2, t, 2, 2, 2, r).transpose(1, 3, 2, 4, 0, 5).reshape(nb, 4, 2 * r)
         gain_grads = jnp.pad(gain_grads, ((0, 0), (0, 0), (0, 16 * share - 2 * r)))
         in_grad = jnp.concatenate([in_grad, lax.optimization_barrier(gain_grads.reshape(nb, 4, 16, share))], axis=2)
         out_grad = lax.optimization_barrier(rows_by_rows(mixer, dbranch).astype(BF))
-        out_grad = out_grad.reshape(nb, ch, slabs, LANES).transpose(0, 2, 1, 3).reshape(nb, slabs * ch, LANES)
+        out_grad = jnp.concatenate(
+            [out_grad[:, i * LANES : (i + 1) * LANES].reshape(nb, ch, LANES) for i in range(slabs)], axis=1
+        )
         kernel_grad = kernel_grad.astype(BF).reshape(taps, nb, ch).transpose(1, 0, 2).reshape(nb, taps * ch)
         kernel_grad = jnp.pad(kernel_grad, ((0, 0), (0, 16 * share - taps * ch))).reshape(nb, 16, share)
         in_grad, out_grad, kernel_grad = lax.optimization_barrier(
             (in_grad.reshape(nb, split, share), out_grad, kernel_grad)
         )
-        conv_grad = lax.optimization_barrier(jnp.concatenate([in_grad, out_grad, kernel_grad], axis=1))
+        conv_grad = after(jnp.concatenate([in_grad, out_grad, kernel_grad], axis=1), pair_sum)
         conv_grad = lax.psum_scatter(conv_grad, COLUMN, scatter_dimension=0)
         out_shard = conv_grad[split : split + slabs * ch].reshape(slabs, ch, LANES).transpose(1, 0, 2)
         out_shard = out_shard.reshape(ch, width).astype(F32)
@@ -236,7 +257,7 @@
         gain_shards = swapped[:, 3 * r :].reshape(4, 16 * share)[:, : 2 * r].astype(F32).sum(axis=0)
         in_shard = swapped[:, : 3 * r].reshape(2, 2, 3, r, t, 2, ch).transpose(3, 2, 4, 0, 5, 1, 6)
         in_shard = in_shard.reshape(r, 3 * width).astype(F32)
-        pair_shard = plane_swap(pair_grad.reshape(4, r, 2 * nb * h), member)
+        pair_shard = plane_swap(pair_sum.reshape(4, r, 2 * nb * h), member)
         pair_shard = pair_shard.reshape(2, 2, r, 2, t, 2, h).transpose(3, 2, 4, 0, 5, 1, 6)
         pair_shard = pair_shard.reshape(2, r, 4 * nb * h).astype(F32)
         return (

time: 382 us -> 375 us (0.982)
  the two profiles are of different devices: /device:TPU:0 before, /device:TPU:24 now
where the time goes in v2:
time: 375 us; the launch traced here: 369 us
  waiting for transfers between devices  143 us (38%)
  local copies, waits for them, and re-layouts  70.2 us (19%)
  matrix products  59.6 us (16%)
  starting transfers between devices  44.8 us (12%)
  other arithmetic  30.8 us (8%)
  between operations  21.4 us (6%)
    ppermute x36, waiting for transfers between devices, to_peer(): return lax.ppermute(values, PLANE, [(i, i ^ k) for i in range(4)])  140 us
    ppermute x36, starting transfers between devices, to_peer(): return lax.ppermute(values, PLANE, [(i, i ^ k) for i in range(4)])  43.4 us
    dot_general x4, matrix products, cols_by_cols(): lax.dot_general(left, right, (((1,), (1,)), ((), ())), preferred_element_...  21.5 us
    dot_general x4, matrix products, rows_by_rows(): lax.dot_general(left, right, (((0,), (0,)), ((), ())), preferred_element_...  18.3 us
    unnamed x74, local copies, waits for them, and re-layouts  11.8 us
    convert_element_type x3, local copies, waits for them, and re-layouts, local(): in_shard = in_shard.reshape(r, 3 * width).astype(F32)  7.79 us
    add x4, other arithmetic, after(): return values + jnp.minimum(jnp.abs(one), 0).astype(values.dtype)  7.65 us
    dot_general x1, matrix products, local(): both = jnp.dot(normed_two, pair_full, preferred_element_type=F32)  7.59 us
  transfers between devices with their start and end apart: 42, of which 28 were waited for; matrix products, arithmetic and copies ran while one was open for 34% of the time, Pallas kernels for 0%

profile of v2, /device:TPU:24, one launch (start us, length us, event | category | flops | bytes accessed | tf_op | source)
XLA Modules:
  0.0 369.3 jit_solution(857972076989412581)
XLA Ops:
  24.7 8.5 %collective-permute-done.2 = bf16[272,1024]{1,0:T(8,128)(2,1)S(1)} collective-permute-done((bf16[272,1024]{1,0:T(8,128)(2,1)S(1)}, bf16[272,1024]{1,0:T(8,128)(2,1)S(1)}, u32[]{:S(2)}, u32[]{:S(2)}) %collective-permute-start.2) | collective-permute-done | bytes 557088 | tf_op jit(solution)/shard_map/ppermute | solution.py:24
  46.4 8.9 %collective-permute-done = bf16[272,1024]{1,0:T(8,128)(2,1)S(1)} collective-permute-done((bf16[272,1024]{1,0:T(8,128)(2,1)S(1)}, bf16[272,1024]{1,0:T(8,128)(2,1)S(1)}, u32[]{:S(2)}, u32[]{:S(2)}) %collective-permute-start) | collective-permute-done | bytes 557088 | tf_op jit(solution)/shard_map/ppermute | solution.py:24
  66.3 4.0 %fusion.51 = f32[1024,768]{1,0:T(8,128)S(1)} fusion(bf16[1024,768]{1,0:T(8,128)(2,1)S(1)} %bitcast.217, f32[1024,1024]{1,0:T(8,128)} %copy-done, f32[1024]{0:T(1024)S(1)} %bitcast.284, f32[1024]{0:T(1024)S(1)} %add_rsqrt_fusion), kind=kOutput, calls=%fused_computation.193 | convolution fusion | flops 1613758464 | bytes 8921088 | tf_op jit(solution)/shard_map/dot_general | solution.py:150
  72.3 2.7 fusion.65
  80.0 11.0 %collective-permute-done.6 = bf16[256,1024]{1,0:T(8,128)(2,1)S(1)} collective-permute-done((bf16[256,1024]{1,0:T(8,128)(2,1)}, bf16[256,1024]{1,0:T(8,128)(2,1)S(1)}, u32[]{:S(2)}, u32[]{:S(2)}) %collective-permute-start.6) | collective-permute-done | bytes 524320 | tf_op jit(solution)/shard_map/ppermute | solution.py:24
  91.3 6.5 %collective-permute-done.8 = bf16[256,1024]{1,0:T(8,128)(2,1)} collective-permute-done((bf16[256,1024]{1,0:T(8,128)(2,1)}, bf16[256,1024]{1,0:T(8,128)(2,1)}, u32[]{:S(2)}, u32[]{:S(2)}) %collective-permute-start.8) | collective-permute-done | bytes 524320 | tf_op jit(solution)/shard_map/ppermute | solution.py:24
  105.1 11.8 %collective-permute-done.11 = bf16[256,1024]{1,0:T(8,128)(2,1)S(1)} collective-permute-done((bf16[256,1024]{1,0:T(8,128)(2,1)}, bf16[256,1024]{1,0:T(8,128)(2,1)S(1)}, u32[]{:S(2)}, u32[]{:S(2)}) %collective-permute-start.11) | collective-permute-done | bytes 524320 | tf_op jit(solution)/shard_map/ppermute | solution.py:24
  124.4 2.8 copy.88
  127.5 7.6 %fusion.27 = f32[1024,2304]{1,0:T(8,128)S(1)} fusion(bf16[1024,2304]{1,0:T(8,128)(2,1)S(1)} %bitcast.220, bf16[256,1024]{1,0:T(8,128)(2,1)S(1)} %copy-done.28, bf16[256,1024]{1,0:T(8,128)(2,1)} %collective-permute-done.10, bf16[256,1024]{1,0:T(8,128)(2,1)} %collective-permute-done.9, bf16[256,1024]{1,0:T(8,128)(2,1)} %multiply_convert_fusion.7), kind=kOutput, calls=%fused_computation.100 | convolution fusion | flops 4840226816 | bytes 16252928 | tf_op jit(solution)/shard_map/dot_general | solution.py:169
  138.7 4.9 %collective-permute-done.17 = bf16[256,1024]{1,0:T(8,128)(2,1)} collective-permute-done((bf16[256,1024]{1,0:T(8,128)(2,1)}, bf16[256,1024]{1,0:T(8,128)(2,1)}, u32[]{:S(2)}, u32[]{:S(2)}) %collective-permute-start.17) | collective-permute-done | bytes 524320 | tf_op jit(solution)/shard_map/ppermute | solution.py:24
  143.6 5.6 %convolution_convert_fusion = bf16[1152,1024]{1,0:T(8,128)(2,1)} fusion(bf16[1024,1152]{1,0:T(8,128)(2,1)S(1)} %multiply_convert_fusion.2, bf16[256,1024]{1,0:T(8,128)(2,1)} %collective-permute-done.17, bf16[256,1024]{1,0:T(8,128)(2,1)} %collective-permute-done.16, bf16[256,1024]{1,0:T(8,128)(2,1)} %collective-permute-done.15, bf16[256,1024]{1,0:T(8,128)(2,1)} %fusion.26), kind=kOutput, calls=%fused_computation.11 | convolution fusion | flops 2425487360 | bytes 6815744 | tf_op jit(solution)/shard_map/dot_general | solution.py:16
  151.3 8.5 %multiply_convert_fusion.1 = (bf16[1024,1152]{1,0:T(8,128)(2,1)S(1)}, bf16[1024,1152]{1,0:T(8,128)(2,1)S(1)}) fusion(f32[1024,2304]{1,0:T(8,128)} %copy-done.5, f32[]{:T(128)S(6)} %convert.68, bf16[1152,1024]{1,0:T(8,128)(2,1)} %all-gather.7.cloned.1.call-done, bf16[256,1024]{1,0:T(8,128)(2,1)} %collective-permute-done.17, ...), kind=kOutput, calls=%fused_computation.3 | convolution fusion | flops 2440822784 | bytes 18612228 | tf_op jit(solution)/shard_map/dot_general | solution.py:20
  159.8 8.1 %fusion.66 = (bf16[1024,1024]{1,0:T(8,128)(2,1)}, f32[1024,1024]{1,0:T(8,128)S(1)}) fusion(bf16[1024,2304]{1,0:T(8,128)(2,1)} %bitcast.221, bf16[1024,1152]{1,0:T(8,128)(2,1)S(1)} %get-tuple-element.48, bf16[1024,1152]{1,0:T(8,128)(2,1)S(1)} %get-tuple-element.47), kind=kOutput, calls=%fused_computation.206 | convolution fusion | flops 4842323968 | bytes 15728640 | tf_op jit(solution)/shard_map/dot_general | solution.py:20
  171.0 9.1 %add_convert_fusion = bf16[1024,2304]{1,0:T(8,128)(2,1)} fusion(f32[]{:T(128)} %bitcast.52, bf16[1024,1152]{1,0:T(8,128)(2,1)S(1)} %get-tuple-element.48, bf16[1024,1152]{1,0:T(8,128)(2,1)S(1)} %get-tuple-element.47, bf16[256,1024]{1,0:T(8,128)(2,1)S(1)} %copy-done.29, bf16[256,1024]{1,0:T(8,128)(2,1)} %collective-permute-done.10, ...), kind=kOutput, calls=%fused_computation | convolution fusion | flops 4854382592 | bytes 11534340 | tf_op jit(solution)/shard_map/dot_general | solution.py:16
  184.1 2.6 broadcast_add_fusion
  186.7 2.4 copy.89
  189.5 2.5 fusion.58
  197.3 8.1 %collective-permute-done.18 = bf16[256,1024]{1,0:T(8,128)(2,1)} collective-permute-done((bf16[256,1024]{1,0:T(8,128)(2,1)}, bf16[256,1024]{1,0:T(8,128)(2,1)}, u32[]{:S(2)}, u32[]{:S(2)}) %collective-permute-start.18) | collective-permute-done | bytes 524320 | tf_op jit(solution)/shard_map/ppermute | solution.py:24
  207.3 11.1 %collective-permute-done.20 = bf16[256,1024]{1,0:T(8,128)(2,1)} collective-permute-done((bf16[256,1024]{1,0:T(8,128)(2,1)}, bf16[256,1024]{1,0:T(8,128)(2,1)}, u32[]{:S(2)}, u32[]{:S(2)}) %collective-permute-start.20) | collective-permute-done | bytes 524320 | tf_op jit(solution)/shard_map/ppermute | solution.py:24
  222.0 2.7 collective-permute-start.21
  225.5 12.0 %collective-permute-done.21 = bf16[256,1024]{1,0:T(8,128)(2,1)S(1)} collective-permute-done((bf16[256,1024]{1,0:T(8,128)(2,1)S(1)}, bf16[256,1024]{1,0:T(8,128)(2,1)S(1)}, u32[]{:S(2)}, u32[]{:S(2)}) %collective-permute-start.21) | collective-permute-done | bytes 524320 | tf_op jit(solution)/shard_map/ppermute | solution.py:24
  237.5 11.4 %collective-permute-done.25 = bf16[256,1024]{1,0:T(8,128)(2,1)S(1)} collective-permute-done((bf16[256,1024]{1,0:T(8,128)(2,1)S(1)}, bf16[256,1024]{1,0:T(8,128)(2,1)S(1)}, u32[]{:S(2)}, u32[]{:S(2)}) %collective-permute-start.25) | collective-permute-done | bytes 524320 | tf_op jit(solution)/shard_map/ppermute | solution.py:24
  259.3 4.2 %multiply_reduce_fusion = (bf16[1024]{0:T(1024)(128)(2,1)S(1)}, bf16[1024,1024]{1,0:T(8,128)(2,1)}, f32[1024,1024]{1,0:T(8,128)}) fusion(f32[1024,1024]{1,0:T(8,128)S(1)} %copy-done.1, f32[1024]{0:T(1024)S(1)} %add_rsqrt_fusion, bf16[1024,768]{1,0:T(8,128)(2,1)S(1)} %bitcast.218, bf16[1024,256]{1,0:T(8,128)(2,1)S(1)} %bitcast.243, ...), kind=kOutput, calls=%fused_computation.8 | convolution fusion | flops 1619524608 | bytes 13637632 | tf_op jit(solution)/shard_map/dot_general | solution.py:20
  269.1 2.9 maximum_add_fusion
  273.9 2.5 fusion.56
  281.8 5.4 %fusion.67 = (bf16[1024,1024]{1,0:T(8,128)(2,1)S(1)}, f32[1024,1024]{1,0:T(8,128)S(1)}) fusion(f32[]{:T(128)S(6)} %convert.70, bf16[1024,1152]{1,0:T(8,128)(2,1)} %copy-done.12, bf16[1152,1024]{1,0:T(8,128)(2,1)} %all-gather.7.cloned.1.call-done), kind=kOutput, calls=%fused_computation.207 | convolution fusion | flops 2418016256 | bytes 11010052 | tf_op jit(solution)/shard_map/dot_general | solution.py:195
  294.2 10.0 %collective-permute-done.29 = bf16[256,1024]{1,0:T(8,128)(2,1)S(1)} collective-permute-done((bf16[256,1024]{1,0:T(8,128)(2,1)}, bf16[256,1024]{1,0:T(8,128)(2,1)S(1)}, u32[]{:S(2)}, u32[]{:S(2)}) %collective-permute-start.29) | collective-permute-done | bytes 524320 | tf_op jit(solution)/shard_map/ppermute | solution.py:24
  308.8 5.8 %collective-permute-done.22 = bf16[256,1024]{1,0:T(8,128)(2,1)S(1)} collective-permute-done((bf16[256,1024]{1,0:T(8,128)(2,1)S(1)}, bf16[256,1024]{1,0:T(8,128)(2,1)S(1)}, u32[]{:S(2)}, u32[]{:S(2)}) %collective-permute-start.22) | collective-permute-done | bytes 524320 | tf_op jit(solution)/shard_map/ppermute | solution.py:24
  316.6 10.1 %collective-permute-done.24 = bf16[256,1024]{1,0:T(8,128)(2,1)S(1)} collective-permute-done((bf16[256,1024]{1,0:T(8,128)(2,1)S(1)}, bf16[256,1024]{1,0:T(8,128)(2,1)S(1)}, u32[]{:S(2)}, u32[]{:S(2)}) %collective-permute-start.24) | collective-permute-done | bytes 524320 | tf_op jit(solution)/shard_map/ppermute | solution.py:24
  333.1 4.8 %reshape.392 = f32[2,2,32,2,4,2,144]{6,5,4,3,2,1,0:T(2,128)S(1)} reshape(f32[4,32,2304]{2,1,0:T(8,128)} %maximum_convert_fusion) | data formatting | bytes 2359296 | tf_op jit(solution)/shard_map/convert_element_type | solution.py:262
  355.2 2.4 copy.97
  357.5 4.1 %reshape.390 = f32[32,3072]{1,0:T(8,128)} reshape(f32[32,3,4,2,2,2,32]{6,5,4,3,2,1,0:T(2,128)} %copy.97) | data formatting | bytes 786432 | tf_op jit(solution)/shard_map/convert_element_type | solution.py:259
  (295 shorter events, 143.0 us)
Async XLA Ops:
  7.2 52.4 %all-gather.9.cloned.1.call-start = ((), (), s32[]{:S(2)}) async-start(), calls=%async_computation.8 | async-start | bytes 2654208 | tf_op jit(solution)/shard_map/all_gather | solution.py:112
  19.2 105.2 %all-gather.5.cloned.1.call-start = ((), (), s32[]{:S(2)}) async-start(), calls=%async_computation.3 | async-start | bytes 5308416 | tf_op jit(solution)/shard_map/all_gather | solution.py:127
  19.6 13.6 %collective-permute-start.2 = (bf16[272,1024]{1,0:T(8,128)(2,1)S(1)}, bf16[272,1024]{1,0:T(8,128)(2,1)S(1)}, u32[]{:S(2)}, u32[]{:S(2)}) collective-permute-start(bf16[272,1024]{1,0:T(8,128)(2,1)S(1)} %constant_dynamic-update-slice_fusion), channel_id=1, source_target_pairs={{0,5},{1,4},{4,1},{5,0},{2,7},{3,6},{6,3},{7,2},{8,13},{9,12},{12,... | collective-permute-start | bytes 1671176 | tf_op jit(solution)/shard_map/ppermute | solution.py:24
  43.8 107.5 %all-gather.7.cloned.1.call-start = ((), (), s32[]{:S(2)}) async-start(), calls=%async_computation.4 | async-start | bytes 2654208 | tf_op jit(solution)/shard_map/all_gather | solution.py:130
  45.3 10.9 %collective-permute-start.1 = (bf16[272,1024]{1,0:T(8,128)(2,1)S(1)}, bf16[272,1024]{1,0:T(8,128)(2,1)S(1)}, u32[]{:S(2)}, u32[]{:S(2)}) collective-permute-start(bf16[272,1024]{1,0:T(8,128)(2,1)S(1)} %constant_dynamic-update-slice_fusion), channel_id=1, source_target_pairs={{0,4},{1,5},{4,0},{5,1},{2,6},{3,7},{6,2},{7,3},{8,12},{9,13},{12,... | collective-permute-start | bytes 1671176 | tf_op jit(solution)/shard_map/ppermute | solution.py:24
  76.2 14.8 %collective-permute-start.6 = (bf16[256,1024]{1,0:T(8,128)(2,1)}, bf16[256,1024]{1,0:T(8,128)(2,1)S(1)}, u32[]{:S(2)}, u32[]{:S(2)}) collective-permute-start(bf16[256,1024]{1,0:T(8,128)(2,1)} %get-tuple-element.62), channel_id=1, source_target_pairs={{0,1},{1,0},{4,5},{5,4},{2,3},{3,2},{6,7},{7,6},{8,9},{9,8},{12,13... | collective-permute-start | bytes 1572872 | tf_op jit(solution)/shard_map/ppermute | solution.py:24
  76.8 14.6 %collective-permute-start.7 = (bf16[256,1024]{1,0:T(8,128)(2,1)}, bf16[256,1024]{1,0:T(8,128)(2,1)S(1)}, u32[]{:S(2)}, u32[]{:S(2)}) collective-permute-start(bf16[256,1024]{1,0:T(8,128)(2,1)} %get-tuple-element.64), channel_id=1, source_target_pairs={{0,4},{1,5},{4,0},{5,1},{2,6},{3,7},{6,2},{7,3},{8,12},{9,13},{12,... | collective-permute-start | bytes 1572872 | tf_op jit(solution)/shard_map/ppermute | solution.py:24
  78.2 19.7 %collective-permute-start.8 = (bf16[256,1024]{1,0:T(8,128)(2,1)}, bf16[256,1024]{1,0:T(8,128)(2,1)}, u32[]{:S(2)}, u32[]{:S(2)}) collective-permute-start(bf16[256,1024]{1,0:T(8,128)(2,1)} %get-tuple-element.63), channel_id=1, source_target_pairs={{0,5},{1,4},{4,1},{5,0},{2,7},{3,6},{6,3},{7,2},{8,13},{9,12},{12,... | collective-permute-start | bytes 1572872 | tf_op jit(solution)/shard_map/ppermute | solution.py:24
  79.7 102.5 %reduce-scatter.4.cloned.1.call-start = ((), (), s32[]{:S(2)}) async-start(), calls=%async_computation.5 | async-start | bytes 2654208 | tf_op jit(solution)/shard_map/reduce_scatter | solution.py:176
  100.9 16.0 %collective-permute-start.11 = (bf16[256,1024]{1,0:T(8,128)(2,1)}, bf16[256,1024]{1,0:T(8,128)(2,1)S(1)}, u32[]{:S(2)}, u32[]{:S(2)}) collective-permute-start(bf16[256,1024]{1,0:T(8,128)(2,1)} %multiply_convert_fusion.7), channel_id=1, source_target_pairs={{0,5},{1,4},{4,1},{5,0},{2,7},{3,6},{6,3},{7,2},{8,13},{9,12},{12,... | collective-permute-start | bytes 1572872 | tf_op jit(solution)/shard_map/ppermute | solution.py:24
  102.7 24.8 %collective-permute-start.10 = (bf16[256,1024]{1,0:T(8,128)(2,1)}, bf16[256,1024]{1,0:T(8,128)(2,1)}, u32[]{:S(2)}, u32[]{:S(2)}) collective-permute-start(bf16[256,1024]{1,0:T(8,128)(2,1)} %multiply_convert_fusion.7), channel_id=1, source_target_pairs={{0,4},{1,5},{4,0},{5,1},{2,6},{3,7},{6,2},{7,3},{8,12},{9,13},{12,... | collective-permute-start | bytes 1572872 | tf_op jit(solution)/shard_map/ppermute | solution.py:24
  103.1 24.4 %collective-permute-start.9 = (bf16[256,1024]{1,0:T(8,128)(2,1)}, bf16[256,1024]{1,0:T(8,128)(2,1)}, u32[]{:S(2)}, u32[]{:S(2)}) collective-permute-start(bf16[256,1024]{1,0:T(8,128)(2,1)} %multiply_convert_fusion.7), channel_id=1, source_target_pairs={{0,1},{1,0},{4,5},{5,4},{2,3},{3,2},{6,7},{7,6},{8,9},{9,8},{12,13... | collective-permute-start | bytes 1572872 | tf_op jit(solution)/shard_map/ppermute | solution.py:24
  120.9 17.8 %collective-permute-start.15 = (bf16[256,1024]{1,0:T(8,128)(2,1)}, bf16[256,1024]{1,0:T(8,128)(2,1)}, u32[]{:S(2)}, u32[]{:S(2)}) collective-permute-start(bf16[256,1024]{1,0:T(8,128)(2,1)} %fusion.26), channel_id=1, source_target_pairs={{0,1},{1,0},{4,5},{5,4},{2,3},{3,2},{6,7},{7,6},{8,9},{9,8},{12,13... | collective-permute-start | bytes 1572872 | tf_op jit(solution)/shard_map/ppermute | solution.py:24
  121.6 17.1 %collective-permute-start.16 = (bf16[256,1024]{1,0:T(8,128)(2,1)}, bf16[256,1024]{1,0:T(8,128)(2,1)}, u32[]{:S(2)}, u32[]{:S(2)}) collective-permute-start(bf16[256,1024]{1,0:T(8,128)(2,1)} %fusion.26), channel_id=1, source_target_pairs={{0,4},{1,5},{4,0},{5,1},{2,6},{3,7},{6,2},{7,3},{8,12},{9,13},{12,... | collective-permute-start | bytes 1572872 | tf_op jit(solution)/shard_map/ppermute | solution.py:24
  123.2 20.4 %collective-permute-start.17 = (bf16[256,1024]{1,0:T(8,128)(2,1)}, bf16[256,1024]{1,0:T(8,128)(2,1)}, u32[]{:S(2)}, u32[]{:S(2)}) collective-permute-start(bf16[256,1024]{1,0:T(8,128)(2,1)} %fusion.26), channel_id=1, source_target_pairs={{0,5},{1,4},{4,1},{5,0},{2,7},{3,6},{6,3},{7,2},{8,13},{9,12},{12,... | collective-permute-start | bytes 1572872 | tf_op jit(solution)/shard_map/ppermute | solution.py:24
  149.2 118.1 %reduce-scatter.6.cloned.1.call-start = ((), (), s32[]{:S(2)}) async-start(), calls=%async_computation.6 | async-start | bytes 5308416 | tf_op jit(solution)/shard_map/reduce_scatter | solution.py:187
  189.2 155.8 %reduce-scatter.8.cloned.1.call-start = ((), (), s32[]{:S(2)}) async-start(), calls=%async_computation.7 | async-start | bytes 2727936 | tf_op jit(solution)/shard_map/reduce_scatter | solution.py:252
  192.0 13.4 %collective-permute-start.18 = (bf16[256,1024]{1,0:T(8,128)(2,1)}, bf16[256,1024]{1,0:T(8,128)(2,1)}, u32[]{:S(2)}, u32[]{:S(2)}) collective-permute-start(bf16[256,1024]{1,0:T(8,128)(2,1)} %get-tuple-element.59), channel_id=1, source_target_pairs={{0,1},{1,0},{4,5},{5,4},{2,3},{3,2},{6,7},{7,6},{8,9},{9,8},{12,13... | collective-permute-start | bytes 1572872 | tf_op jit(solution)/shard_map/ppermute | solution.py:24
  193.5 13.7 %collective-permute-start.19 = (bf16[256,1024]{1,0:T(8,128)(2,1)}, bf16[256,1024]{1,0:T(8,128)(2,1)}, u32[]{:S(2)}, u32[]{:S(2)}) collective-permute-start(bf16[256,1024]{1,0:T(8,128)(2,1)} %get-tuple-element.61), channel_id=1, source_target_pairs={{0,4},{1,5},{4,0},{5,1},{2,6},{3,7},{6,2},{7,3},{8,12},{9,13},{12,... | collective-permute-start | bytes 1572872 | tf_op jit(solution)/shard_map/ppermute | solution.py:24
  195.1 23.3 %collective-permute-start.20 = (bf16[256,1024]{1,0:T(8,128)(2,1)}, bf16[256,1024]{1,0:T(8,128)(2,1)}, u32[]{:S(2)}, u32[]{:S(2)}) collective-permute-start(bf16[256,1024]{1,0:T(8,128)(2,1)} %get-tuple-element.60), channel_id=1, source_target_pairs={{0,5},{1,4},{4,1},{5,0},{2,7},{3,6},{6,3},{7,2},{8,13},{9,12},{12,... | collective-permute-start | bytes 1572872 | tf_op jit(solution)/shard_map/ppermute | solution.py:24
  222.0 15.5 %collective-permute-start.21 = (bf16[256,1024]{1,0:T(8,128)(2,1)S(1)}, bf16[256,1024]{1,0:T(8,128)(2,1)S(1)}, u32[]{:S(2)}, u32[]{:S(2)}) collective-permute-start(bf16[256,1024]{1,0:T(8,128)(2,1)S(1)} %get-tuple-element.40), channel_id=1, source_target_pairs={{0,5},{1,4},{4,1},{5,0},{2,7},{3,6},{6,3},{7,2},{8,13},{9,12},{12,... | collective-permute-start | bytes 1572872 | tf_op jit(solution)/shard_map/ppermute | solution.py:24
  224.7 24.3 %collective-permute-start.25 = (bf16[256,1024]{1,0:T(8,128)(2,1)S(1)}, bf16[256,1024]{1,0:T(8,128)(2,1)S(1)}, u32[]{:S(2)}, u32[]{:S(2)}) collective-permute-start(bf16[256,1024]{1,0:T(8,128)(2,1)S(1)} %get-tuple-element.40), channel_id=1, source_target_pairs={{0,1},{1,0},{4,5},{5,4},{2,3},{3,2},{6,7},{7,6},{8,9},{9,8},{12,13... | collective-permute-start | bytes 1572872 | tf_op jit(solution)/shard_map/ppermute | solution.py:24
  225.0 24.0 %collective-permute-start.26 = (bf16[256,1024]{1,0:T(8,128)(2,1)S(1)}, bf16[256,1024]{1,0:T(8,128)(2,1)S(1)}, u32[]{:S(2)}, u32[]{:S(2)}) collective-permute-start(bf16[256,1024]{1,0:T(8,128)(2,1)S(1)} %get-tuple-element.40), channel_id=1, source_target_pairs={{0,4},{1,5},{4,0},{5,1},{2,6},{3,7},{6,2},{7,3},{8,12},{9,13},{12,... | collective-permute-start | bytes 1572872 | tf_op jit(solution)/shard_map/ppermute | solution.py:24
  276.4 15.8 %collective-permute-start.27 = (bf16[256,1024]{1,0:T(8,128)(2,1)}, bf16[256,1024]{1,0:T(8,128)(2,1)S(1)}, u32[]{:S(2)}, u32[]{:S(2)}) collective-permute-start(bf16[256,1024]{1,0:T(8,128)(2,1)} %get-tuple-element.53), channel_id=1, source_target_pairs={{0,1},{1,0},{4,5},{5,4},{2,3},{3,2},{6,7},{7,6},{8,9},{9,8},{12,13... | collective-permute-start | bytes 1572872 | tf_op jit(solution)/shard_map/ppermute | solution.py:24
  278.0 16.2 %collective-permute-start.28 = (bf16[256,1024]{1,0:T(8,128)(2,1)}, bf16[256,1024]{1,0:T(8,128)(2,1)S(1)}, u32[]{:S(2)}, u32[]{:S(2)}) collective-permute-start(bf16[256,1024]{1,0:T(8,128)(2,1)} %get-tuple-element.55), channel_id=1, source_target_pairs={{0,4},{1,5},{4,0},{5,1},{2,6},{3,7},{6,2},{7,3},{8,12},{9,13},{12,... | collective-permute-start | bytes 1572872 | tf_op jit(solution)/shard_map/ppermute | solution.py:24
  279.0 25.2 %collective-permute-start.29 = (bf16[256,1024]{1,0:T(8,128)(2,1)}, bf16[256,1024]{1,0:T(8,128)(2,1)S(1)}, u32[]{:S(2)}, u32[]{:S(2)}) collective-permute-start(bf16[256,1024]{1,0:T(8,128)(2,1)} %get-tuple-element.54), channel_id=1, source_target_pairs={{0,5},{1,4},{4,1},{5,0},{2,7},{3,6},{6,3},{7,2},{8,13},{9,12},{12,... | collective-permute-start | bytes 1572872 | tf_op jit(solution)/shard_map/ppermute | solution.py:24
  287.4 27.3 %collective-permute-start.22 = (bf16[256,1024]{1,0:T(8,128)(2,1)S(1)}, bf16[256,1024]{1,0:T(8,128)(2,1)S(1)}, u32[]{:S(2)}, u32[]{:S(2)}) collective-permute-start(bf16[256,1024]{1,0:T(8,128)(2,1)S(1)} %get-tuple-element.56), channel_id=1, source_target_pairs={{0,1},{1,0},{4,5},{5,4},{2,3},{3,2},{6,7},{7,6},{8,9},{9,8},{12,13... | collective-permute-start | bytes 1572872 | tf_op jit(solution)/shard_map/ppermute | solution.py:24
  289.0 27.6 %collective-permute-start.23 = (bf16[256,1024]{1,0:T(8,128)(2,1)S(1)}, bf16[256,1024]{1,0:T(8,128)(2,1)S(1)}, u32[]{:S(2)}, u32[]{:S(2)}) collective-permute-start(bf16[256,1024]{1,0:T(8,128)(2,1)S(1)} %get-tuple-element.58), channel_id=1, source_target_pairs={{0,4},{1,5},{4,0},{5,1},{2,6},{3,7},{6,2},{7,3},{8,12},{9,13},{12,... | collective-permute-start | bytes 1572872 | tf_op jit(solution)/shard_map/ppermute | solution.py:24
  292.2 34.5 %collective-permute-start.24 = (bf16[256,1024]{1,0:T(8,128)(2,1)S(1)}, bf16[256,1024]{1,0:T(8,128)(2,1)S(1)}, u32[]{:S(2)}, u32[]{:S(2)}) collective-permute-start(bf16[256,1024]{1,0:T(8,128)(2,1)S(1)} %get-tuple-element.57), channel_id=1, source_target_pairs={{0,5},{1,4},{4,1},{5,0},{2,7},{3,6},{6,3},{7,2},{8,13},{9,12},{12,... | collective-permute-start | bytes 1572872 | tf_op jit(solution)/shard_map/ppermute | solution.py:24
  306.2 21.6 %collective-permute-start.33 = (bf16[32,2304]{1,0:T(8,128)(2,1)S(1)}, bf16[32,2304]{1,0:T(8,128)(2,1)S(1)}, u32[]{:S(2)}, u32[]{:S(2)}) collective-permute-start(bf16[32,2304]{1,0:T(8,128)(2,1)S(1)} %get-tuple-element.78), channel_id=1, source_target_pairs={{0,1},{1,0},{4,5},{5,4},{2,3},{3,2},{6,7},{7,6},{8,9},{9,8},{12,13... | collective-permute-start | bytes 442376 | tf_op jit(solution)/shard_map/ppermute | solution.py:24
  307.8 22.1 %collective-permute-start.34 = (bf16[32,2304]{1,0:T(8,128)(2,1)S(1)}, bf16[32,2304]{1,0:T(8,128)(2,1)S(1)}, u32[]{:S(2)}, u32[]{:S(2)}) collective-permute-start(bf16[32,2304]{1,0:T(8,128)(2,1)S(1)} %get-tuple-element.77), channel_id=1, source_target_pairs={{0,4},{1,5},{4,0},{5,1},{2,6},{3,7},{6,2},{7,3},{8,12},{9,13},{12,... | collective-permute-start | bytes 442376 | tf_op jit(solution)/shard_map/ppermute | solution.py:24
  314.6 17.2 %collective-permute-start.35 = (bf16[32,2304]{1,0:T(8,128)(2,1)S(1)}, bf16[32,2304]{1,0:T(8,128)(2,1)S(1)}, u32[]{:S(2)}, u32[]{:S(2)}) collective-permute-start(bf16[32,2304]{1,0:T(8,128)(2,1)S(1)} %get-tuple-element.76), channel_id=1, source_target_pairs={{0,5},{1,4},{4,1},{5,0},{2,7},{3,6},{6,3},{7,2},{8,13},{9,12},{12,... | collective-permute-start | bytes 442376 | tf_op jit(solution)/shard_map/ppermute | solution.py:24
  (41 other events, 282.9 us)
Sparse Core Ops, SparseCore 0:
  19.3 28.9 all-gather.8
  50.5 50.1 all-gather.4
  102.3 31.1 all-gather.6
  149.3 32.8 reduce-scatter.3
  189.3 55.5 reduce-scatter.5
  272.1 33.4 reduce-scatter.7

commit v3 on v2

--- a/solution.py
+++ b/solution.py
@@ -28,8 +28,8 @@
     return [values] + [to_peer(values, k) for k in (1, 2, 3)]
 
 
-def plane_sum(blocks):
-    sent = [blocks[k].astype(BF) for k in (1, 2, 3)]
+def plane_sum(blocks, *others):
+    sent = [after(blocks[k].astype(BF), *others) for k in (1, 2, 3)]
     total = blocks[0].astype(F32)
     for k in (1, 2, 3):
         total = total + to_peer(sent[k - 1], k).astype(F32)
@@ -46,9 +46,11 @@
     return jnp.stack([pick(got, member ^ j) for j in range(4)])
 
 
-def after(values, other):
-    one = other[(slice(0, 1),) * other.ndim].reshape(())
-    return values + jnp.minimum(jnp.abs(one), 0).astype(values.dtype)
+def after(values, *others):
+    for other in others:
+        one = other[(slice(0, 1),) * other.ndim].reshape(())
+        values = values + jnp.minimum(jnp.abs(one), 0).astype(values.dtype)
+    return values
 
 
 def norm_back(grad_norm, source, scale, gain):
@@ -123,7 +125,7 @@
             return w.reshape(r, t, 2, 2, 2, h).transpose(2, 4, 0, 1, 3, 5).reshape(4, r, nb * h)
 
         pair = jnp.concatenate([ff_blocks(gate_weight), ff_blocks(up_weight)], axis=2)
-        pair_mine = plane_swap(after(pair, gathered[3]), member).reshape(4 * r, 2 * nb * h)
+        pair_mine = plane_swap(after(pair, *gathered[1:]), member).reshape(4 * r, 2 * nb * h)
         pair_all = lax.all_gather(pair_mine, COLUMN)
         pair_full = pair_all.reshape(t, 2, 2, 2 * r, 2 * nb * h).transpose(0, 2, 1, 3, 4)
         pair_full = lax.optimization_barrier(pair_full.reshape(width, 2 * nb * h))
@@ -158,13 +160,14 @@
         convolved = kernel_vals[0] * product + kernel_vals[1] * back_one + kernel_vals[2] * back_two
         mixer = (second * convolved).astype(BF).reshape(4 * slots, share)
         branch = jnp.dot(mixer, out_full, preferred_element_type=F32).reshape(4, slots, width)
+        dffn = plane_gather(after(dffn_own, conv_all))
         own = tokens.astype(F32)
-        hidden = own + plane_sum(branch)
+        hidden = own + plane_sum(branch, *dffn[1:])
+        dffn = jnp.concatenate(dffn)
 
         scale_two = lax.rsqrt(jnp.mean(hidden * hidden, axis=1, keepdims=True) + EPS)
         normed_two_own = (hidden * scale_two * gain_second).astype(BF)
         normed_two = plane_gather(normed_two_own)
-        dffn = jnp.concatenate(plane_gather(after(dffn_own, normed_two[3])))
         normed_two = jnp.concatenate(normed_two)
         both = jnp.dot(normed_two, pair_full, preferred_element_type=F32)
         gate = both[:, : nb * h]
@@ -185,15 +188,15 @@
         pair_grad = pair_grad.reshape(t, 2, 2, 2 * r, 2 * nb * h).transpose(0, 2, 1, 3, 4)
         pair_grad = after(pair_grad.reshape(nb, 4 * r, 2 * nb * h), down_sum)
         pair_sum = lax.psum_scatter(pair_grad, COLUMN, scatter_dimension=0)
-        dnormed_two = after(plane_sum(dnormed_part), pair_grad)
+        dnormed_two = plane_sum(dnormed_part)
         hidden_part, gain_two_grad = norm_back(dnormed_two, hidden, scale_two, gain_second)
         dhidden = dout + hidden_part
 
-        dbranch = plane_gather(dhidden.astype(BF))
-        dbranch_last = dbranch[3]
+        dbranch = plane_gather(after(dhidden.astype(BF), pair_grad))
+        dbranch_parts = dbranch[1:]
         dbranch = jnp.concatenate(dbranch)
-        ffn = after(jnp.dot(act, down_full, preferred_element_type=F32), dbranch_last)
-        ffn = plane_sum(ffn.reshape(4, slots, width))
+        ffn = jnp.dot(act, down_full, preferred_element_type=F32).reshape(4, slots, width)
+        ffn = plane_sum(lax.optimization_barrier(ffn), *dbranch_parts)
         mixed = (live * (hidden + ffn)).astype(BF)
         dmixer = cols_by_cols(dbranch, out_full).reshape(4, slots, share)
         dsecond = dmixer * convolved

time: 375 us -> 380 us (1.013)
  local copies, waits for them, and re-layouts: 70.2 us -> 77.3 us
  waiting for transfers between devices: 143 us -> 137 us
  between operations: 21.4 us -> 26.1 us
    slice x8 -> x15, local copies, waits for them, and re-layouts: 7.37 us -> 15.1 us  [after(): one = other[(slice(0, 1),) * other.ndim].reshape(())]
    ppermute x36, waiting for transfers between devices: 140 us -> 135 us  [to_peer(): return lax.ppermute(values, PLANE, [(i, i ^ k) for i in range(4)])]
    unnamed x74 -> x76, local copies, waits for them, and re-layouts: 11.8 us -> 13.9 us
    add x4 -> x7, other arithmetic: 7.65 us -> 9.42 us  [after(): values = values + jnp.minimum(jnp.abs(one), 0).astype(values.dtype)]
  transfers between devices with their start and end apart: 42 -> 42, of which waited for: 28 -> 28; matrix products, arithmetic and copies ran while one was open for 34% -> 35% of each run, Pallas kernels for 0% -> 0%
where the time goes in v3:
time: 380 us; the launch traced here: 374 us
  waiting for transfers between devices  137 us (36%)
  local copies, waits for them, and re-layouts  77.3 us (20%)
  matrix products  58.5 us (15%)
  starting transfers between devices  45.7 us (12%)
  other arithmetic  30 us (8%)
  between operations  26.1 us (7%)
    ppermute x36, waiting for transfers between devices, to_peer(): return lax.ppermute(values, PLANE, [(i, i ^ k) for i in range(4)])  135 us
    ppermute x36, starting transfers between devices, to_peer(): return lax.ppermute(values, PLANE, [(i, i ^ k) for i in range(4)])  44.3 us
    dot_general x4, matrix products, cols_by_cols(): lax.dot_general(left, right, (((1,), (1,)), ((), ())), preferred_element_...  21.4 us
    dot_general x4, matrix products, rows_by_rows(): lax.dot_general(left, right, (((0,), (0,)), ((), ())), preferred_element_...  18.5 us
    slice x15, local copies, waits for them, and re-layouts, after(): one = other[(slice(0, 1),) * other.ndim].reshape(())  15.1 us
    unnamed x76, local copies, waits for them, and re-layouts  13.9 us
    add x7, other arithmetic, after(): values = values + jnp.minimum(jnp.abs(one), 0).astype(values.dtype)  9.42 us
    convert_element_type x3, local copies, waits for them, and re-layouts, local(): in_shard = in_shard.reshape(r, 3 * width).astype(F32)  7.79 us
  transfers between devices with their start and end apart: 42, of which 28 were waited for; matrix products, arithmetic and copies ran while one was open for 35% of the time, Pallas kernels for 0%

profile of v3, /device:TPU:24, one launch (start us, length us, event | category | flops | bytes accessed | tf_op | source)
XLA Modules:
  0.0 374.2 jit_solution(9138240693820349318)
XLA Ops:
  22.1 2.3 collective-permute-start.2
  28.9 6.9 %collective-permute-done = bf16[272,1024]{1,0:T(8,128)(2,1)S(1)} collective-permute-done((bf16[272,1024]{1,0:T(8,128)(2,1)}, bf16[272,1024]{1,0:T(8,128)(2,1)S(1)}, u32[]{:S(2)}, u32[]{:S(2)}) %collective-permute-start) | collective-permute-done | bytes 557088 | tf_op jit(solution)/shard_map/ppermute | solution.py:24
  38.4 8.5 %collective-permute-done.2 = bf16[272,1024]{1,0:T(8,128)(2,1)S(1)} collective-permute-done((bf16[272,1024]{1,0:T(8,128)(2,1)}, bf16[272,1024]{1,0:T(8,128)(2,1)S(1)}, u32[]{:S(2)}, u32[]{:S(2)}) %collective-permute-start.2) | collective-permute-done | bytes 557088 | tf_op jit(solution)/shard_map/ppermute | solution.py:24
  75.1 4.0 %fusion.68 = f32[1024,768]{1,0:T(8,128)S(1)} fusion(bf16[1024,768]{1,0:T(8,128)(2,1)S(1)} %bitcast.244, f32[1024,1024]{1,0:T(8,128)} %copy-done, f32[1024]{0:T(1024)S(1)} %bitcast.312, f32[1024]{0:T(1024)S(1)} %add_rsqrt_fusion), kind=kOutput, calls=%fused_computation.216 | convolution fusion | flops 1613758464 | bytes 8921088 | tf_op jit(solution)/shard_map/dot_general | solution.py:152
  81.1 2.7 fusion.79
  87.5 2.9 collective-permute-done.8
  97.1 10.4 %collective-permute-done.10 = bf16[256,1024]{1,0:T(8,128)(2,1)S(1)} collective-permute-done((bf16[256,1024]{1,0:T(8,128)(2,1)}, bf16[256,1024]{1,0:T(8,128)(2,1)S(1)}, u32[]{:S(2)}, u32[]{:S(2)}) %collective-permute-start.10) | collective-permute-done | bytes 524320 | tf_op jit(solution)/shard_map/ppermute | solution.py:24
  107.6 6.8 %collective-permute-done.11 = bf16[256,1024]{1,0:T(8,128)(2,1)} collective-permute-done((bf16[256,1024]{1,0:T(8,128)(2,1)}, bf16[256,1024]{1,0:T(8,128)(2,1)}, u32[]{:S(2)}, u32[]{:S(2)}) %collective-permute-start.11) | collective-permute-done | bytes 524320 | tf_op jit(solution)/shard_map/ppermute | solution.py:24
  114.4 2.2 collective-permute-done.9
  123.3 2.7 copy.92
  126.0 12.0 %collective-permute-done.12 = bf16[256,1024]{1,0:T(8,128)(2,1)} collective-permute-done((bf16[256,1024]{1,0:T(8,128)(2,1)}, bf16[256,1024]{1,0:T(8,128)(2,1)}, u32[]{:S(2)}, u32[]{:S(2)}) %collective-permute-start.12) | collective-permute-done | bytes 524320 | tf_op jit(solution)/shard_map/ppermute | solution.py:24
  138.0 7.4 %fusion.44 = f32[1024,2304]{1,0:T(8,128)S(1)} fusion(bf16[1024,2304]{1,0:T(8,128)(2,1)S(1)} %bitcast.247, bf16[256,1024]{1,0:T(8,128)(2,1)} %collective-permute-done.14, bf16[256,1024]{1,0:T(8,128)(2,1)} %collective-permute-done.13, bf16[256,1024]{1,0:T(8,128)(2,1)} %collective-permute-done.12, bf16[256,1024]{1,0:T(8,128)(2,1)} %multiply_convert_fusion.7), kind=kOutput, calls=%fused_computation.123 | convolution fusion | flops 4840226816 | bytes 16252928 | tf_op jit(solution)/shard_map/dot_general | solution.py:172
  150.5 5.6 %convolution_convert_fusion = bf16[1152,1024]{1,0:T(8,128)(2,1)} fusion(bf16[1024,1152]{1,0:T(8,128)(2,1)S(1)} %multiply_convert_fusion.2, bf16[256,1024]{1,0:T(8,128)(2,1)} %collective-permute-done.8, bf16[256,1024]{1,0:T(8,128)(2,1)} %collective-permute-done.7, bf16[256,1024]{1,0:T(8,128)(2,1)} %collective-permute-done.6, bf16[256,1024]{1,0:T(8,128)(2,1)} %fusion.28), kind=kOutput, calls=%fused_computation.11 | convolution fusion | flops 2425487360 | bytes 6815744 | tf_op jit(solution)/shard_map/dot_general | solution.py:16
  158.3 8.5 %multiply_convert_fusion.1 = (bf16[1024,1152]{1,0:T(8,128)(2,1)S(1)}, bf16[1024,1152]{1,0:T(8,128)(2,1)S(1)}) fusion(f32[1024,2304]{1,0:T(8,128)} %copy-done.5, f32[]{:T(128)S(6)} %convert.66, bf16[1152,1024]{1,0:T(8,128)(2,1)} %all-gather.7.cloned.1.call-done, bf16[256,1024]{1,0:T(8,128)(2,1)} %collective-permute-done.8, ...), kind=kOutput, calls=%fused_computation.3 | convolution fusion | flops 2440822784 | bytes 18612228 | tf_op jit(solution)/shard_map/dot_general | solution.py:20
  166.8 8.0 %fusion.80 = (bf16[1024,1024]{1,0:T(8,128)(2,1)}, f32[1024,1024]{1,0:T(8,128)S(1)}) fusion(bf16[1024,2304]{1,0:T(8,128)(2,1)} %bitcast.248, bf16[1024,1152]{1,0:T(8,128)(2,1)S(1)} %get-tuple-element.48, bf16[1024,1152]{1,0:T(8,128)(2,1)S(1)} %get-tuple-element.47), kind=kOutput, calls=%fused_computation.226 | convolution fusion | flops 4842323968 | bytes 15728640 | tf_op jit(solution)/shard_map/dot_general | solution.py:20
  178.0 9.2 %add_convert_fusion = bf16[1024,2304]{1,0:T(8,128)(2,1)} fusion(f32[]{:T(128)} %bitcast.59, bf16[1024,1152]{1,0:T(8,128)(2,1)S(1)} %get-tuple-element.48, bf16[1024,1152]{1,0:T(8,128)(2,1)S(1)} %get-tuple-element.47, bf16[256,1024]{1,0:T(8,128)(2,1)} %collective-permute-done.14, bf16[256,1024]{1,0:T(8,128)(2,1)} %collective-permute-done.13, ...), kind=kOutput, calls=%fused_computation | convolution fusion | flops 4854382592 | bytes 11534340 | tf_op jit(solution)/shard_map/dot_general | solution.py:16
  190.6 2.6 broadcast_add_fusion
  193.3 2.5 copy.93
  201.2 9.6 %collective-permute-done.18 = bf16[256,1024]{1,0:T(8,128)(2,1)S(1)} collective-permute-done((bf16[256,1024]{1,0:T(8,128)(2,1)S(1)}, bf16[256,1024]{1,0:T(8,128)(2,1)S(1)}, u32[]{:S(2)}, u32[]{:S(2)}) %collective-permute-start.18) | collective-permute-done | bytes 524320 | tf_op jit(solution)/shard_map/ppermute | solution.py:24
  212.8 11.0 %collective-permute-done.20 = bf16[256,1024]{1,0:T(8,128)(2,1)S(1)} collective-permute-done((bf16[256,1024]{1,0:T(8,128)(2,1)S(1)}, bf16[256,1024]{1,0:T(8,128)(2,1)S(1)}, u32[]{:S(2)}, u32[]{:S(2)}) %collective-permute-start.20) | collective-permute-done | bytes 524320 | tf_op jit(solution)/shard_map/ppermute | solution.py:24
  232.5 11.1 %collective-permute-done.21 = bf16[256,1024]{1,0:T(8,128)(2,1)S(1)} collective-permute-done((bf16[256,1024]{1,0:T(8,128)(2,1)S(1)}, bf16[256,1024]{1,0:T(8,128)(2,1)S(1)}, u32[]{:S(2)}, u32[]{:S(2)}) %collective-permute-start.21) | collective-permute-done | bytes 524320 | tf_op jit(solution)/shard_map/ppermute | solution.py:24
  245.4 11.0 %collective-permute-done.23 = bf16[256,1024]{1,0:T(8,128)(2,1)S(1)} collective-permute-done((bf16[256,1024]{1,0:T(8,128)(2,1)S(1)}, bf16[256,1024]{1,0:T(8,128)(2,1)S(1)}, u32[]{:S(2)}, u32[]{:S(2)}) %collective-permute-start.23) | collective-permute-done | bytes 524320 | tf_op jit(solution)/shard_map/ppermute | solution.py:24
  266.8 4.2 %multiply_reduce_fusion = (bf16[1024]{0:T(1024)(128)(2,1)S(1)}, bf16[1024,1024]{1,0:T(8,128)(2,1)}, f32[1024,1024]{1,0:T(8,128)}) fusion(f32[1024,1024]{1,0:T(8,128)S(1)} %copy-done.1, f32[1024]{0:T(1024)S(1)} %add_rsqrt_fusion, bf16[1024,768]{1,0:T(8,128)(2,1)S(1)} %bitcast.245, bf16[1024,256]{1,0:T(8,128)(2,1)S(1)} %bitcast.271, ...), kind=kOutput, calls=%fused_computation.8 | convolution fusion | flops 1619524608 | bytes 13637632 | tf_op jit(solution)/shard_map/dot_general | solution.py:20
  276.6 2.9 maximum_add_fusion
  284.7 4.5 %fusion.81 = f32[1024,1024]{1,0:T(8,128)S(1)} fusion(bf16[1024,1152]{1,0:T(8,128)(2,1)S(1)} %copy-done.13, bf16[1152,1024]{1,0:T(8,128)(2,1)} %all-gather.7.cloned.1.call-done), kind=kOutput, calls=%fused_computation.227 | convolution fusion | flops 2415919104 | bytes 8912896 | tf_op jit(solution)/shard_map/dot_general | solution.py:198
  300.4 8.3 %collective-permute-done.29 = bf16[256,1024]{1,0:T(8,128)(2,1)S(1)} collective-permute-done((bf16[256,1024]{1,0:T(8,128)(2,1)S(1)}, bf16[256,1024]{1,0:T(8,128)(2,1)S(1)}, u32[]{:S(2)}, u32[]{:S(2)}) %collective-permute-start.29) | collective-permute-done | bytes 524320 | tf_op jit(solution)/shard_map/ppermute | solution.py:24
  313.8 6.2 %collective-permute-done.24 = bf16[256,1024]{1,0:T(8,128)(2,1)S(1)} collective-permute-done((bf16[256,1024]{1,0:T(8,128)(2,1)S(1)}, bf16[256,1024]{1,0:T(8,128)(2,1)S(1)}, u32[]{:S(2)}, u32[]{:S(2)}) %collective-permute-start.24) | collective-permute-done | bytes 524320 | tf_op jit(solution)/shard_map/ppermute | solution.py:24
  320.0 2.5 collective-permute-start.35
  322.5 8.7 %collective-permute-done.26 = bf16[256,1024]{1,0:T(8,128)(2,1)S(1)} collective-permute-done((bf16[256,1024]{1,0:T(8,128)(2,1)S(1)}, bf16[256,1024]{1,0:T(8,128)(2,1)S(1)}, u32[]{:S(2)}, u32[]{:S(2)}) %collective-permute-start.26) | collective-permute-done | bytes 524320 | tf_op jit(solution)/shard_map/ppermute | solution.py:24
  337.6 4.8 %reshape.442 = f32[2,2,32,2,4,2,144]{6,5,4,3,2,1,0:T(2,128)S(1)} reshape(f32[4,32,2304]{2,1,0:T(8,128)} %maximum_convert_fusion) | data formatting | bytes 2359296 | tf_op jit(solution)/shard_map/convert_element_type | solution.py:265
  360.0 2.4 copy.101
  362.4 4.1 %reshape.440 = f32[32,3072]{1,0:T(8,128)} reshape(f32[32,3,4,2,2,2,32]{6,5,4,3,2,1,0:T(2,128)} %copy.101) | data formatting | bytes 786432 | tf_op jit(solution)/shard_map/convert_element_type | solution.py:262
  (305 shorter events, 151.3 us)
Async XLA Ops:
  7.2 55.2 %all-gather.9.cloned.1.call-start = ((), (), s32[]{:S(2)}) async-start(), calls=%async_computation.8 | async-start | bytes 2654208 | tf_op jit(solution)/shard_map/all_gather | solution.py:114
  19.2 104.1 %all-gather.5.cloned.1.call-start = ((), (), s32[]{:S(2)}) async-start(), calls=%async_computation.3 | async-start | bytes 5308416 | tf_op jit(solution)/shard_map/all_gather | solution.py:129
  20.9 14.9 %collective-permute-start = (bf16[272,1024]{1,0:T(8,128)(2,1)}, bf16[272,1024]{1,0:T(8,128)(2,1)S(1)}, u32[]{:S(2)}, u32[]{:S(2)}) collective-permute-start(bf16[272,1024]{1,0:T(8,128)(2,1)} %constant_dynamic-update-slice_fusion), channel_id=1, source_target_pairs={{0,1},{1,0},{4,5},{5,4},{2,3},{3,2},{6,7},{7,6},{8,9},{9,8},{12,13... | collective-permute-start | bytes 1671176 | tf_op jit(solution)/shard_map/ppermute | solution.py:24
  21.4 15.8 %collective-permute-start.1 = (bf16[272,1024]{1,0:T(8,128)(2,1)}, bf16[272,1024]{1,0:T(8,128)(2,1)S(1)}, u32[]{:S(2)}, u32[]{:S(2)}) collective-permute-start(bf16[272,1024]{1,0:T(8,128)(2,1)} %constant_dynamic-update-slice_fusion), channel_id=1, source_target_pairs={{0,4},{1,5},{4,0},{5,1},{2,6},{3,7},{6,2},{7,3},{8,12},{9,13},{12,... | collective-permute-start | bytes 1671176 | tf_op jit(solution)/shard_map/ppermute | solution.py:24
  22.1 24.8 %collective-permute-start.2 = (bf16[272,1024]{1,0:T(8,128)(2,1)}, bf16[272,1024]{1,0:T(8,128)(2,1)S(1)}, u32[]{:S(2)}, u32[]{:S(2)}) collective-permute-start(bf16[272,1024]{1,0:T(8,128)(2,1)} %constant_dynamic-update-slice_fusion), channel_id=1, source_target_pairs={{0,5},{1,4},{4,1},{5,0},{2,7},{3,6},{6,3},{7,2},{8,13},{9,12},{12,... | collective-permute-start | bytes 1671176 | tf_op jit(solution)/shard_map/ppermute | solution.py:24
  57.7 100.6 %all-gather.7.cloned.1.call-start = ((), (), s32[]{:S(2)}) async-start(), calls=%async_computation.4 | async-start | bytes 2654208 | tf_op jit(solution)/shard_map/all_gather | solution.py:132
  68.2 15.6 %collective-permute-start.6 = (bf16[256,1024]{1,0:T(8,128)(2,1)}, bf16[256,1024]{1,0:T(8,128)(2,1)}, u32[]{:S(2)}, u32[]{:S(2)}) collective-permute-start(bf16[256,1024]{1,0:T(8,128)(2,1)} %fusion.28), channel_id=1, source_target_pairs={{0,1},{1,0},{4,5},{5,4},{2,3},{3,2},{6,7},{7,6},{8,9},{9,8},{12,13... | collective-permute-start | bytes 1572872 | tf_op jit(solution)/shard_map/ppermute | solution.py:24
  69.1 16.6 %collective-permute-start.7 = (bf16[256,1024]{1,0:T(8,128)(2,1)}, bf16[256,1024]{1,0:T(8,128)(2,1)}, u32[]{:S(2)}, u32[]{:S(2)}) collective-permute-start(bf16[256,1024]{1,0:T(8,128)(2,1)} %fusion.28), channel_id=1, source_target_pairs={{0,4},{1,5},{4,0},{5,1},{2,6},{3,7},{6,2},{7,3},{8,12},{9,13},{12,... | collective-permute-start | bytes 1572872 | tf_op jit(solution)/shard_map/ppermute | solution.py:24
  70.1 20.3 %collective-permute-start.8 = (bf16[256,1024]{1,0:T(8,128)(2,1)}, bf16[256,1024]{1,0:T(8,128)(2,1)}, u32[]{:S(2)}, u32[]{:S(2)}) collective-permute-start(bf16[256,1024]{1,0:T(8,128)(2,1)} %fusion.28), channel_id=1, source_target_pairs={{0,5},{1,4},{4,1},{5,0},{2,7},{3,6},{6,3},{7,2},{8,13},{9,12},{12,... | collective-permute-start | bytes 1572872 | tf_op jit(solution)/shard_map/ppermute | solution.py:24
  93.4 14.1 %collective-permute-start.10 = (bf16[256,1024]{1,0:T(8,128)(2,1)}, bf16[256,1024]{1,0:T(8,128)(2,1)S(1)}, u32[]{:S(2)}, u32[]{:S(2)}) collective-permute-start(bf16[256,1024]{1,0:T(8,128)(2,1)} %get-tuple-element.64), channel_id=1, source_target_pairs={{0,4},{1,5},{4,0},{5,1},{2,6},{3,7},{6,2},{7,3},{8,12},{9,13},{12,... | collective-permute-start | bytes 1572872 | tf_op jit(solution)/shard_map/ppermute | solution.py:24
  94.8 19.6 %collective-permute-start.11 = (bf16[256,1024]{1,0:T(8,128)(2,1)}, bf16[256,1024]{1,0:T(8,128)(2,1)}, u32[]{:S(2)}, u32[]{:S(2)}) collective-permute-start(bf16[256,1024]{1,0:T(8,128)(2,1)} %get-tuple-element.63), channel_id=1, source_target_pairs={{0,5},{1,4},{4,1},{5,0},{2,7},{3,6},{6,3},{7,2},{8,13},{9,12},{12,... | collective-permute-start | bytes 1572872 | tf_op jit(solution)/shard_map/ppermute | solution.py:24
  96.1 20.5 %collective-permute-start.9 = (bf16[256,1024]{1,0:T(8,128)(2,1)S(1)}, bf16[256,1024]{1,0:T(8,128)(2,1)}, u32[]{:S(2)}, u32[]{:S(2)}) collective-permute-start(bf16[256,1024]{1,0:T(8,128)(2,1)S(1)} %get-tuple-element.62), channel_id=1, source_target_pairs={{0,1},{1,0},{4,5},{5,4},{2,3},{3,2},{6,7},{7,6},{8,9},{9,8},{12,13... | collective-permute-start | bytes 1572872 | tf_op jit(solution)/shard_map/ppermute | solution.py:24
  96.9 91.9 %reduce-scatter.4.cloned.1.call-start = ((), (), s32[]{:S(2)}) async-start(), calls=%async_computation.5 | async-start | bytes 2654208 | tf_op jit(solution)/shard_map/reduce_scatter | solution.py:179
  119.8 18.2 %collective-permute-start.12 = (bf16[256,1024]{1,0:T(8,128)(2,1)}, bf16[256,1024]{1,0:T(8,128)(2,1)}, u32[]{:S(2)}, u32[]{:S(2)}) collective-permute-start(bf16[256,1024]{1,0:T(8,128)(2,1)} %multiply_convert_fusion.7), channel_id=1, source_target_pairs={{0,1},{1,0},{4,5},{5,4},{2,3},{3,2},{6,7},{7,6},{8,9},{9,8},{12,13... | collective-permute-start | bytes 1572872 | tf_op jit(solution)/shard_map/ppermute | solution.py:24
  120.3 17.7 %collective-permute-start.13 = (bf16[256,1024]{1,0:T(8,128)(2,1)}, bf16[256,1024]{1,0:T(8,128)(2,1)}, u32[]{:S(2)}, u32[]{:S(2)}) collective-permute-start(bf16[256,1024]{1,0:T(8,128)(2,1)} %multiply_convert_fusion.7), channel_id=1, source_target_pairs={{0,4},{1,5},{4,0},{5,1},{2,6},{3,7},{6,2},{7,3},{8,12},{9,13},{12,... | collective-permute-start | bytes 1572872 | tf_op jit(solution)/shard_map/ppermute | solution.py:24
  122.0 16.0 %collective-permute-start.14 = (bf16[256,1024]{1,0:T(8,128)(2,1)}, bf16[256,1024]{1,0:T(8,128)(2,1)}, u32[]{:S(2)}, u32[]{:S(2)}) collective-permute-start(bf16[256,1024]{1,0:T(8,128)(2,1)} %multiply_convert_fusion.7), channel_id=1, source_target_pairs={{0,5},{1,4},{4,1},{5,0},{2,7},{3,6},{6,3},{7,2},{8,13},{9,12},{12,... | collective-permute-start | bytes 1572872 | tf_op jit(solution)/shard_map/ppermute | solution.py:24
  156.2 118.5 %reduce-scatter.6.cloned.1.call-start = ((), (), s32[]{:S(2)}) async-start(), calls=%async_computation.6 | async-start | bytes 5308416 | tf_op jit(solution)/shard_map/reduce_scatter | solution.py:190
  195.9 153.7 %reduce-scatter.8.cloned.1.call-start = ((), (), s32[]{:S(2)}) async-start(), calls=%async_computation.7 | async-start | bytes 2727936 | tf_op jit(solution)/shard_map/reduce_scatter | solution.py:255
  199.3 13.5 %collective-permute-start.19 = (bf16[256,1024]{1,0:T(8,128)(2,1)S(1)}, bf16[256,1024]{1,0:T(8,128)(2,1)S(1)}, u32[]{:S(2)}, u32[]{:S(2)}) collective-permute-start(bf16[256,1024]{1,0:T(8,128)(2,1)S(1)} %get-tuple-element.61), channel_id=1, source_target_pairs={{0,4},{1,5},{4,0},{5,1},{2,6},{3,7},{6,2},{7,3},{8,12},{9,13},{12,... | collective-permute-start | bytes 1572872 | tf_op jit(solution)/shard_map/ppermute | solution.py:24
  200.7 23.1 %collective-permute-start.20 = (bf16[256,1024]{1,0:T(8,128)(2,1)S(1)}, bf16[256,1024]{1,0:T(8,128)(2,1)S(1)}, u32[]{:S(2)}, u32[]{:S(2)}) collective-permute-start(bf16[256,1024]{1,0:T(8,128)(2,1)S(1)} %get-tuple-element.60), channel_id=1, source_target_pairs={{0,5},{1,4},{4,1},{5,0},{2,7},{3,6},{6,3},{7,2},{8,13},{9,12},{12,... | collective-permute-start | bytes 1572872 | tf_op jit(solution)/shard_map/ppermute | solution.py:24
  229.0 14.6 %collective-permute-start.21 = (bf16[256,1024]{1,0:T(8,128)(2,1)S(1)}, bf16[256,1024]{1,0:T(8,128)(2,1)S(1)}, u32[]{:S(2)}, u32[]{:S(2)}) collective-permute-start(bf16[256,1024]{1,0:T(8,128)(2,1)S(1)} %get-tuple-element.40), channel_id=1, source_target_pairs={{0,1},{1,0},{4,5},{5,4},{2,3},{3,2},{6,7},{7,6},{8,9},{9,8},{12,13... | collective-permute-start | bytes 1572872 | tf_op jit(solution)/shard_map/ppermute | solution.py:24
  230.6 14.8 %collective-permute-start.22 = (bf16[256,1024]{1,0:T(8,128)(2,1)S(1)}, bf16[256,1024]{1,0:T(8,128)(2,1)S(1)}, u32[]{:S(2)}, u32[]{:S(2)}) collective-permute-start(bf16[256,1024]{1,0:T(8,128)(2,1)S(1)} %get-tuple-element.40), channel_id=1, source_target_pairs={{0,4},{1,5},{4,0},{5,1},{2,6},{3,7},{6,2},{7,3},{8,12},{9,13},{12,... | collective-permute-start | bytes 1572872 | tf_op jit(solution)/shard_map/ppermute | solution.py:24
  232.1 24.3 %collective-permute-start.23 = (bf16[256,1024]{1,0:T(8,128)(2,1)S(1)}, bf16[256,1024]{1,0:T(8,128)(2,1)S(1)}, u32[]{:S(2)}, u32[]{:S(2)}) collective-permute-start(bf16[256,1024]{1,0:T(8,128)(2,1)S(1)} %get-tuple-element.40), channel_id=1, source_target_pairs={{0,5},{1,4},{4,1},{5,0},{2,7},{3,6},{6,3},{7,2},{8,13},{9,12},{12,... | collective-permute-start | bytes 1572872 | tf_op jit(solution)/shard_map/ppermute | solution.py:24
  281.1 18.8 %collective-permute-start.27 = (bf16[256,1024]{1,0:T(8,128)(2,1)S(1)}, bf16[256,1024]{1,0:T(8,128)(2,1)S(1)}, u32[]{:S(2)}, u32[]{:S(2)}) collective-permute-start(bf16[256,1024]{1,0:T(8,128)(2,1)S(1)} %get-tuple-element.53), channel_id=1, source_target_pairs={{0,1},{1,0},{4,5},{5,4},{2,3},{3,2},{6,7},{7,6},{8,9},{9,8},{12,13... | collective-permute-start | bytes 1572872 | tf_op jit(solution)/shard_map/ppermute | solution.py:24
  282.8 17.6 %collective-permute-start.28 = (bf16[256,1024]{1,0:T(8,128)(2,1)S(1)}, bf16[256,1024]{1,0:T(8,128)(2,1)S(1)}, u32[]{:S(2)}, u32[]{:S(2)}) collective-permute-start(bf16[256,1024]{1,0:T(8,128)(2,1)S(1)} %get-tuple-element.55), channel_id=1, source_target_pairs={{0,4},{1,5},{4,0},{5,1},{2,6},{3,7},{6,2},{7,3},{8,12},{9,13},{12,... | collective-permute-start | bytes 1572872 | tf_op jit(solution)/shard_map/ppermute | solution.py:24
  284.2 24.5 %collective-permute-start.29 = (bf16[256,1024]{1,0:T(8,128)(2,1)S(1)}, bf16[256,1024]{1,0:T(8,128)(2,1)S(1)}, u32[]{:S(2)}, u32[]{:S(2)}) collective-permute-start(bf16[256,1024]{1,0:T(8,128)(2,1)S(1)} %get-tuple-element.54), channel_id=1, source_target_pairs={{0,5},{1,4},{4,1},{5,0},{2,7},{3,6},{6,3},{7,2},{8,13},{9,12},{12,... | collective-permute-start | bytes 1572872 | tf_op jit(solution)/shard_map/ppermute | solution.py:24
  296.8 23.2 %collective-permute-start.24 = (bf16[256,1024]{1,0:T(8,128)(2,1)S(1)}, bf16[256,1024]{1,0:T(8,128)(2,1)S(1)}, u32[]{:S(2)}, u32[]{:S(2)}) collective-permute-start(bf16[256,1024]{1,0:T(8,128)(2,1)S(1)} %get-tuple-element.56), channel_id=1, source_target_pairs={{0,1},{1,0},{4,5},{5,4},{2,3},{3,2},{6,7},{7,6},{8,9},{9,8},{12,13... | collective-permute-start | bytes 1572872 | tf_op jit(solution)/shard_map/ppermute | solution.py:24
  298.5 24.0 %collective-permute-start.25 = (bf16[256,1024]{1,0:T(8,128)(2,1)S(1)}, bf16[256,1024]{1,0:T(8,128)(2,1)S(1)}, u32[]{:S(2)}, u32[]{:S(2)}) collective-permute-start(bf16[256,1024]{1,0:T(8,128)(2,1)S(1)} %get-tuple-element.58), channel_id=1, source_target_pairs={{0,4},{1,5},{4,0},{5,1},{2,6},{3,7},{6,2},{7,3},{8,12},{9,13},{12,... | collective-permute-start | bytes 1572872 | tf_op jit(solution)/shard_map/ppermute | solution.py:24
  299.9 31.3 %collective-permute-start.26 = (bf16[256,1024]{1,0:T(8,128)(2,1)S(1)}, bf16[256,1024]{1,0:T(8,128)(2,1)S(1)}, u32[]{:S(2)}, u32[]{:S(2)}) collective-permute-start(bf16[256,1024]{1,0:T(8,128)(2,1)S(1)} %get-tuple-element.57), channel_id=1, source_target_pairs={{0,5},{1,4},{4,1},{5,0},{2,7},{3,6},{6,3},{7,2},{8,13},{9,12},{12,... | collective-permute-start | bytes 1572872 | tf_op jit(solution)/shard_map/ppermute | solution.py:24
  310.7 23.6 %collective-permute-start.33 = (bf16[32,2304]{1,0:T(8,128)(2,1)S(1)}, bf16[32,2304]{1,0:T(8,128)(2,1)S(1)}, u32[]{:S(2)}, u32[]{:S(2)}) collective-permute-start(bf16[32,2304]{1,0:T(8,128)(2,1)S(1)} %get-tuple-element.78), channel_id=1, source_target_pairs={{0,1},{1,0},{4,5},{5,4},{2,3},{3,2},{6,7},{7,6},{8,9},{9,8},{12,13... | collective-permute-start | bytes 442376 | tf_op jit(solution)/shard_map/ppermute | solution.py:24
  312.3 22.2 %collective-permute-start.34 = (bf16[32,2304]{1,0:T(8,128)(2,1)S(1)}, bf16[32,2304]{1,0:T(8,128)(2,1)S(1)}, u32[]{:S(2)}, u32[]{:S(2)}) collective-permute-start(bf16[32,2304]{1,0:T(8,128)(2,1)S(1)} %get-tuple-element.77), channel_id=1, source_target_pairs={{0,4},{1,5},{4,0},{5,1},{2,6},{3,7},{6,2},{7,3},{8,12},{9,13},{12,... | collective-permute-start | bytes 442376 | tf_op jit(solution)/shard_map/ppermute | solution.py:24
  320.0 16.3 %collective-permute-start.35 = (bf16[32,2304]{1,0:T(8,128)(2,1)S(1)}, bf16[32,2304]{1,0:T(8,128)(2,1)S(1)}, u32[]{:S(2)}, u32[]{:S(2)}) collective-permute-start(bf16[32,2304]{1,0:T(8,128)(2,1)S(1)} %get-tuple-element.76), channel_id=1, source_target_pairs={{0,5},{1,4},{4,1},{5,0},{2,7},{3,6},{6,3},{7,2},{8,13},{9,12},{12,... | collective-permute-start | bytes 442376 | tf_op jit(solution)/shard_map/ppermute | solution.py:24
  (42 other events, 303.5 us)
Sparse Core Ops, SparseCore 0:
  19.3 28.9 all-gather.8
  57.8 49.1 all-gather.4
  108.6 31.0 all-gather.6
  156.3 32.4 reduce-scatter.3
  196.0 55.4 reduce-scatter.5
  279.6 33.6 reduce-scatter.7

commit v4 on v3

--- a/solution.py
+++ b/solution.py
@@ -48,18 +48,18 @@
 
 def after(values, *others):
     for other in others:
-        one = other[(slice(0, 1),) * other.ndim].reshape(())
-        values = values + jnp.minimum(jnp.abs(one), 0).astype(values.dtype)
+        if other.shape != values.shape:
+            other = other[(slice(0, 1),) * other.ndim].reshape(())
+        values = values + jnp.minimum(jnp.abs(other), 0).astype(values.dtype)
     return values
 
 
 def norm_back(grad_norm, source, scale, gain):
     weighted = grad_norm * gain
     gain_grad = jnp.sum(grad_norm * source * scale, axis=0)
-    source_grad = scale * weighted - source * scale**3 * jnp.mean(
-        weighted * source, axis=1, keepdims=True
-    )
-    return (source_grad, gain_grad)
+    row_mean = jnp.mean(weighted * source, axis=1, keepdims=True)
+    source_grad = scale * weighted - source * scale**3 * row_mean
+    return (source_grad, gain_grad, row_mean)
 
 
 def shifted(values, steps):
@@ -124,8 +124,10 @@
         def ff_blocks(w):
             return w.reshape(r, t, 2, 2, 2, h).transpose(2, 4, 0, 1, 3, 5).reshape(4, r, nb * h)
 
-        pair = jnp.concatenate([ff_blocks(gate_weight), ff_blocks(up_weight)], axis=2)
-        pair_mine = plane_swap(after(pair, *gathered[1:]), member).reshape(4 * r, 2 * nb * h)
+        tile = sum(g[:16, :128] for g in gathered[1:])
+        pair = after(jnp.concatenate([ff_blocks(gate_weight), ff_blocks(up_weight)], axis=2), tile)
+        pair_mine = plane_swap(pair, member).reshape(4 * r, 2 * nb * h)
+        dffn = plane_gather(after(dffn_own, *[g[:slots] for g in gathered[1:]]))
         pair_all = lax.all_gather(pair_mine, COLUMN)
         pair_full = pair_all.reshape(t, 2, 2, 2 * r, 2 * nb * h).transpose(0, 2, 1, 3, 4)
         pair_full = lax.optimization_barrier(pair_full.reshape(width, 2 * nb * h))
@@ -160,7 +162,6 @@
         convolved = kernel_vals[0] * product + kernel_vals[1] * back_one + kernel_vals[2] * back_two
         mixer = (second * convolved).astype(BF).reshape(4 * slots, share)
         branch = jnp.dot(mixer, out_full, preferred_element_type=F32).reshape(4, slots, width)
-        dffn = plane_gather(after(dffn_own, conv_all))
         own = tokens.astype(F32)
         hidden = own + plane_sum(branch, *dffn[1:])
         dffn = jnp.concatenate(dffn)
@@ -183,16 +184,15 @@
         dupper = (dact * swish).astype(BF)
         dboth = jnp.concatenate([dgate, dupper], axis=1)
         dnormed_part = cols_by_cols(dboth, pair_full).reshape(4, slots, width)
-        pair_grad = after(rows_by_rows(normed_two, dboth), dnormed_part)
-        pair_grad = lax.optimization_barrier(pair_grad.astype(BF))
+        pair_grad = lax.optimization_barrier(rows_by_rows(normed_two, dboth).astype(BF))
+        dnormed_two = plane_sum(dnormed_part)
+        hidden_part, gain_two_grad, row_mean = norm_back(dnormed_two, hidden, scale_two, gain_second)
         pair_grad = pair_grad.reshape(t, 2, 2, 2 * r, 2 * nb * h).transpose(0, 2, 1, 3, 4)
-        pair_grad = after(pair_grad.reshape(nb, 4 * r, 2 * nb * h), down_sum)
+        pair_grad = after(pair_grad.reshape(nb, 4 * r, 2 * nb * h), down_sum, row_mean)
         pair_sum = lax.psum_scatter(pair_grad, COLUMN, scatter_dimension=0)
-        dnormed_two = plane_sum(dnormed_part)
-        hidden_part, gain_two_grad = norm_back(dnormed_two, hidden, scale_two, gain_second)
         dhidden = dout + hidden_part
 
-        dbranch = plane_gather(after(dhidden.astype(BF), pair_grad))
+        dbranch = plane_gather(dhidden.astype(BF))
         dbranch_parts = dbranch[1:]
         dbranch = jnp.concatenate(dbranch)
         ffn = jnp.dot(act, down_full, preferred_element_type=F32).reshape(4, slots, width)
@@ -215,9 +215,10 @@
         )
         dprojected = jnp.concatenate([dproduct * stream, dsecond, dproduct * first], axis=2)
         dprojected = dprojected.astype(BF).reshape(4 * slots, 3 * share)
-        dnormed_part = cols_by_cols(dprojected, in_full)
+        dnormed_part = after(cols_by_cols(dprojected, in_full), mixed[:16, :128])
         gain_one_grad = jnp.sum(dnormed_part * source * scale_one, axis=0)
-        dnormed_one = plane_sum(dnormed_part.reshape(4, slots, width))
+        pair_shard = plane_swap(pair_sum.reshape(4, r, 2 * nb * h), member)
+        dnormed_one = plane_sum(dnormed_part.reshape(4, slots, width), pair_shard[3])
         own_scale = scale_one[:slots]
         weighted = dnormed_one * gain_first
         token_grad = (
@@ -258,9 +259,11 @@
         kernel_shard = conv_grad[split + slabs * ch :].reshape(-1)[: taps * ch].reshape(taps, ch).astype(F32)
         swapped = plane_swap(conv_grad[:split].reshape(4, 3 * r + 16, share), member)
         gain_shards = swapped[:, 3 * r :].reshape(4, 16 * share)[:, : 2 * r].astype(F32).sum(axis=0)
-        in_shard = swapped[:, : 3 * r].reshape(2, 2, 3, r, t, 2, ch).transpose(3, 2, 4, 0, 5, 1, 6)
-        in_shard = in_shard.reshape(r, 3 * width).astype(F32)
-        pair_shard = plane_swap(pair_sum.reshape(4, r, 2 * nb * h), member)
+        place = jnp.arange(width).reshape(t, 2, 2, 2, ch).transpose(1, 3, 0, 2, 4).reshape(-1)
+        order = (place[:, None] == jnp.arange(width)[None, :]).astype(BF)
+        in_shard = swapped[:, : 3 * r].transpose(1, 0, 2).reshape(3 * r, width)
+        in_shard = jnp.dot(in_shard, order, preferred_element_type=F32)
+        in_shard = jnp.concatenate([in_shard[i * r : (i + 1) * r] for i in range(3)], axis=1)
         pair_shard = pair_shard.reshape(2, 2, r, 2, t, 2, h).transpose(3, 2, 4, 0, 5, 1, 6)
         pair_shard = pair_shard.reshape(2, r, 4 * nb * h).astype(F32)
         return (

time: 380 us -> 332 us (0.87)
  the two profiles are of different devices: /device:TPU:24 before, /device:TPU:0 now
where the time goes in v4:
time: 332 us; the launch traced here: 326 us
  waiting for transfers between devices  105 us (32%)
  matrix products  61.5 us (19%)
  local copies, waits for them, and re-layouts  53.8 us (16%)
  starting transfers between devices  44.7 us (13%)
  other arithmetic  39.4 us (12%)
  between operations  22.3 us (7%)
    ppermute x36, waiting for transfers between devices, to_peer(): return lax.ppermute(values, PLANE, [(i, i ^ k) for i in range(4)])  102 us
    ppermute x36, starting transfers between devices, to_peer(): return lax.ppermute(values, PLANE, [(i, i ^ k) for i in range(4)])  43.3 us
    dot_general x4, matrix products, cols_by_cols(): lax.dot_general(left, right, (((1,), (1,)), ((), ())), preferred_element_...  23.8 us
    dot_general x4, matrix products, rows_by_rows(): lax.dot_general(left, right, (((0,), (0,)), ((), ())), preferred_element_...  17.5 us
    unnamed x66, local copies, waits for them, and re-layouts  11.6 us
    add x7, other arithmetic, after(): values = values + jnp.minimum(jnp.abs(other), 0).astype(values.dtype)  10.1 us
    dot_general x1, matrix products, local(): both = jnp.dot(normed_two, pair_full, preferred_element_type=F32)  7.39 us
  transfers between devices with their start and end apart: 42, of which 26 were waited for; matrix products, arithmetic and copies ran while one was open for 40% of the time, Pallas kernels for 0%

profile of v4, /device:TPU:0, one launch (start us, length us, event | category | flops | bytes accessed | tf_op | source)
XLA Modules:
  0.0 326.5 jit_solution(12453884959051679884)
XLA Ops:
  10.1 3.0 collective-permute-start.3
  15.3 2.4 collective-permute-done.4
  30.4 6.9 %collective-permute-done = bf16[272,1024]{1,0:T(8,128)(2,1)S(1)} collective-permute-done((bf16[272,1024]{1,0:T(8,128)(2,1)}, bf16[272,1024]{1,0:T(8,128)(2,1)S(1)}, u32[]{:S(2)}, u32[]{:S(2)}) %collective-permute-start) | collective-permute-done | bytes 557088 | tf_op jit(solution)/shard_map/ppermute | solution.py:24
  40.5 7.9 %collective-permute-done.2 = bf16[272,1024]{1,0:T(8,128)(2,1)S(1)} collective-permute-done((bf16[272,1024]{1,0:T(8,128)(2,1)}, bf16[272,1024]{1,0:T(8,128)(2,1)S(1)}, u32[]{:S(2)}, u32[]{:S(2)}) %collective-permute-start.2) | collective-permute-done | bytes 557088 | tf_op jit(solution)/shard_map/ppermute | solution.py:24
  75.5 4.6 %fusion.69 = f32[1024,768]{1,0:T(8,128)S(1)} fusion(bf16[1024,768]{1,0:T(8,128)(2,1)} %bitcast.277, f32[1024,1024]{1,0:T(8,128)} %copy-done, f32[1024]{0:T(1024)S(1)} %bitcast.326, f32[1024]{0:T(1024)S(1)} %add_rsqrt_fusion), kind=kOutput, calls=%fused_computation.229 | convolution fusion | flops 1613758464 | bytes 8921088 | tf_op jit(solution)/shard_map/dot_general | solution.py:154
  82.1 2.7 fusion.81
  84.8 2.9 fusion.44
  91.7 10.3 %collective-permute-done.10 = bf16[256,1024]{1,0:T(8,128)(2,1)S(1)} collective-permute-done((bf16[256,1024]{1,0:T(8,128)(2,1)}, bf16[256,1024]{1,0:T(8,128)(2,1)S(1)}, u32[]{:S(2)}, u32[]{:S(2)}) %collective-permute-start.10) | collective-permute-done | bytes 524320 | tf_op jit(solution)/shard_map/ppermute | solution.py:24
  102.1 6.4 %collective-permute-done.11 = bf16[256,1024]{1,0:T(8,128)(2,1)S(1)} collective-permute-done((bf16[256,1024]{1,0:T(8,128)(2,1)}, bf16[256,1024]{1,0:T(8,128)(2,1)S(1)}, u32[]{:S(2)}, u32[]{:S(2)}) %collective-permute-start.11) | collective-permute-done | bytes 524320 | tf_op jit(solution)/shard_map/ppermute | solution.py:24
  117.2 2.8 copy.89
  120.1 7.1 %collective-permute-done.12 = bf16[256,1024]{1,0:T(8,128)(2,1)} collective-permute-done((bf16[256,1024]{1,0:T(8,128)(2,1)}, bf16[256,1024]{1,0:T(8,128)(2,1)}, u32[]{:S(2)}, u32[]{:S(2)}) %collective-permute-start.12) | collective-permute-done | bytes 524320 | tf_op jit(solution)/shard_map/ppermute | solution.py:24
  127.2 5.6 %collective-permute-done.14 = bf16[256,1024]{1,0:T(8,128)(2,1)} collective-permute-done((bf16[256,1024]{1,0:T(8,128)(2,1)}, bf16[256,1024]{1,0:T(8,128)(2,1)}, u32[]{:S(2)}, u32[]{:S(2)}) %collective-permute-start.14) | collective-permute-done | bytes 524320 | tf_op jit(solution)/shard_map/ppermute | solution.py:24
  132.8 7.4 %fusion.45 = f32[1024,2304]{1,0:T(8,128)S(1)} fusion(bf16[1024,2304]{1,0:T(8,128)(2,1)S(1)} %bitcast.259, bf16[256,1024]{1,0:T(8,128)(2,1)} %collective-permute-done.14, bf16[256,1024]{1,0:T(8,128)(2,1)} %collective-permute-done.13, bf16[256,1024]{1,0:T(8,128)(2,1)} %collective-permute-done.12, bf16[256,1024]{1,0:T(8,128)(2,1)} %multiply_convert_fusion.7), kind=kOutput, calls=%fused_computation.135 | convolution fusion | flops 4840226816 | bytes 16252928 | tf_op jit(solution)/shard_map/dot_general | solution.py:173
  145.4 5.6 %convolution_convert_fusion.1 = bf16[1152,1024]{1,0:T(8,128)(2,1)} fusion(bf16[1024,1152]{1,0:T(8,128)(2,1)S(1)} %multiply_convert_fusion.2, bf16[256,1024]{1,0:T(8,128)(2,1)} %collective-permute-done.8, bf16[256,1024]{1,0:T(8,128)(2,1)} %collective-permute-done.7, bf16[256,1024]{1,0:T(8,128)(2,1)} %collective-permute-done.6, ...), kind=kOutput, calls=%fused_computation.14 | convolution fusion | flops 2425487360 | bytes 6815744 | tf_op jit(solution)/shard_map/dot_general | solution.py:16
  153.0 8.5 %multiply_convert_fusion.1 = (bf16[1024,1152]{1,0:T(8,128)(2,1)S(1)}, bf16[1024,1152]{1,0:T(8,128)(2,1)S(1)}) fusion(f32[1024,2304]{1,0:T(8,128)} %copy-done.5, f32[]{:T(128)S(6)} %convert.64, bf16[1152,1024]{1,0:T(8,128)(2,1)} %all-gather.7.cloned.1.call-done, bf16[256,1024]{1,0:T(8,128)(2,1)} %collective-permute-done.8, ...), kind=kOutput, calls=%fused_computation.4 | convolution fusion | flops 2440822784 | bytes 18612228 | tf_op jit(solution)/shard_map/dot_general | solution.py:20
  161.5 7.0 %fusion.82 = (bf16[1024,1024]{1,0:T(8,128)(2,1)S(1)}, f32[1024,1024]{1,0:T(8,128)S(1)}) fusion(bf16[1024,2304]{1,0:T(8,128)(2,1)} %bitcast.260, bf16[1024,1152]{1,0:T(8,128)(2,1)S(1)} %get-tuple-element.48, bf16[1024,1152]{1,0:T(8,128)(2,1)S(1)} %get-tuple-element.47), kind=kOutput, calls=%fused_computation.240 | convolution fusion | flops 4842323968 | bytes 15728640 | tf_op jit(solution)/shard_map/dot_general | solution.py:20
  172.1 9.2 %convolution_convert_fusion = bf16[1024,2304]{1,0:T(8,128)(2,1)} fusion(bf16[1024,1152]{1,0:T(8,128)(2,1)S(1)} %get-tuple-element.48, bf16[1024,1152]{1,0:T(8,128)(2,1)S(1)} %get-tuple-element.47, bf16[256,1024]{1,0:T(8,128)(2,1)} %collective-permute-done.14, bf16[256,1024]{1,0:T(8,128)(2,1)} %collective-permute-done.13, ...), kind=kOutput, calls=%fused_computation | convolution fusion | flops 4852023296 | bytes 11534336 | tf_op jit(solution)/shard_map/dot_general | solution.py:16
  181.3 4.9 %collective-permute-done.20 = bf16[256,1024]{1,0:T(8,128)(2,1)S(1)} collective-permute-done((bf16[256,1024]{1,0:T(8,128)(2,1)S(1)}, bf16[256,1024]{1,0:T(8,128)(2,1)S(1)}, u32[]{:S(2)}, u32[]{:S(2)}) %collective-permute-start.20) | collective-permute-done | bytes 524320 | tf_op jit(solution)/shard_map/ppermute | solution.py:24
  190.7 2.7 add_add_fusion
  193.4 2.5 copy.90
  196.2 2.9 fusion.71
  202.6 4.7 %fusion.83 = f32[1024,1024]{1,0:T(8,128)S(1)} fusion(bf16[1024,1152]{1,0:T(8,128)(2,1)S(1)} %copy-done.10, bf16[1152,1024]{1,0:T(8,128)(2,1)} %all-gather.7.cloned.1.call-done), kind=kOutput, calls=%fused_computation.241 | convolution fusion | flops 2415919104 | bytes 8912896 | tf_op jit(solution)/shard_map/dot_general | solution.py:198
  207.6 5.5 %collective-permute-done.21 = bf16[256,1024]{1,0:T(8,128)(2,1)S(1)} collective-permute-done((bf16[256,1024]{1,0:T(8,128)(2,1)S(1)}, bf16[256,1024]{1,0:T(8,128)(2,1)S(1)}, u32[]{:S(2)}, u32[]{:S(2)}) %collective-permute-start.21) | collective-permute-done | bytes 524320 | tf_op jit(solution)/shard_map/ppermute | solution.py:24
  214.6 7.5 %collective-permute-done.23 = bf16[256,1024]{1,0:T(8,128)(2,1)S(1)} collective-permute-done((bf16[256,1024]{1,0:T(8,128)(2,1)S(1)}, bf16[256,1024]{1,0:T(8,128)(2,1)S(1)}, u32[]{:S(2)}, u32[]{:S(2)}) %collective-permute-start.23) | collective-permute-done | bytes 524320 | tf_op jit(solution)/shard_map/ppermute | solution.py:24
  236.2 8.7 %collective-permute-done.24 = bf16[256,1024]{1,0:T(8,128)(2,1)S(1)} collective-permute-done((bf16[256,1024]{1,0:T(8,128)(2,1)S(1)}, bf16[256,1024]{1,0:T(8,128)(2,1)S(1)}, u32[]{:S(2)}, u32[]{:S(2)}) %collective-permute-start.24) | collective-permute-done | bytes 524320 | tf_op jit(solution)/shard_map/ppermute | solution.py:24
  244.9 2.5 collective-permute-done.25
  247.3 6.1 %collective-permute-done.26 = bf16[256,1024]{1,0:T(8,128)(2,1)S(1)} collective-permute-done((bf16[256,1024]{1,0:T(8,128)(2,1)S(1)}, bf16[256,1024]{1,0:T(8,128)(2,1)S(1)}, u32[]{:S(2)}, u32[]{:S(2)}) %collective-permute-start.26) | collective-permute-done | bytes 524320 | tf_op jit(solution)/shard_map/ppermute | solution.py:24
  255.1 7.6 %multiply_reduce_fusion = (bf16[1024]{0:T(1024)(128)(2,1)S(1)}, bf16[1024,1024]{1,0:T(8,128)(2,1)}, f32[1024,1024]{1,0:T(8,128)}) fusion(f32[1024,1024]{1,0:T(8,128)} %copy-done, f32[1024]{0:T(1024)S(1)} %add_rsqrt_fusion, f32[]{:T(128)S(6)} %convert.65, bf16[1024,768]{1,0:T(8,128)(2,1)} %bitcast.278, bf16[1024,256]{1,0:T(8,128)(2,1)} %bitcast.291, ...), kind=kOutput, calls=%fused_computation.10 | convolution fusion | flops 1620573184 | bytes 13637636 | tf_op jit(solution)/shard_map/dot_general | solution.py:20
  275.5 2.4 collective-permute-done.29
  285.3 4.6 %reshape.490 = f32[2,2,32,2,4,2,144]{6,5,4,3,2,1,0:T(2,128)S(1)} reshape(f32[4,32,2304]{2,1,0:T(8,128)} %maximum_convert_fusion) | data formatting | bytes 2359296 | tf_op jit(solution)/shard_map/convert_element_type | solution.py:268
  297.1 3.4 %collective-permute-done.32 = bf16[256,1024]{1,0:T(8,128)(2,1)} collective-permute-done((bf16[256,1024]{1,0:T(8,128)(2,1)}, bf16[256,1024]{1,0:T(8,128)(2,1)}, u32[]{:S(2)}, u32[]{:S(2)}) %collective-permute-start.32) | collective-permute-done | bytes 524320 | tf_op jit(solution)/shard_map/ppermute | solution.py:24
  302.5 3.0 fusion.11
  (289 shorter events, 135.2 us)
Async XLA Ops:
  7.2 60.8 %all-gather.9.cloned.1.call-start = ((), (), s32[]{:S(2)}) async-start(), calls=%async_computation.8 | async-start | bytes 2654208 | tf_op jit(solution)/shard_map/all_gather | solution.py:114
  20.6 96.6 %all-gather.5.cloned.1.call-start = ((), (), s32[]{:S(2)}) async-start(), calls=%async_computation.3 | async-start | bytes 5308416 | tf_op jit(solution)/shard_map/all_gather | solution.py:131
  22.4 14.9 %collective-permute-start = (bf16[272,1024]{1,0:T(8,128)(2,1)}, bf16[272,1024]{1,0:T(8,128)(2,1)S(1)}, u32[]{:S(2)}, u32[]{:S(2)}) collective-permute-start(bf16[272,1024]{1,0:T(8,128)(2,1)} %constant_dynamic-update-slice_fusion), channel_id=1, source_target_pairs={{0,1},{1,0},{4,5},{5,4},{2,3},{3,2},{6,7},{7,6},{8,9},{9,8},{12,13... | collective-permute-start | bytes 1671176 | tf_op jit(solution)/shard_map/ppermute | solution.py:24
  22.9 15.8 %collective-permute-start.1 = (bf16[272,1024]{1,0:T(8,128)(2,1)}, bf16[272,1024]{1,0:T(8,128)(2,1)S(1)}, u32[]{:S(2)}, u32[]{:S(2)}) collective-permute-start(bf16[272,1024]{1,0:T(8,128)(2,1)} %constant_dynamic-update-slice_fusion), channel_id=1, source_target_pairs={{0,4},{1,5},{4,0},{5,1},{2,6},{3,7},{6,2},{7,3},{8,12},{9,13},{12,... | collective-permute-start | bytes 1671176 | tf_op jit(solution)/shard_map/ppermute | solution.py:24
  23.6 24.8 %collective-permute-start.2 = (bf16[272,1024]{1,0:T(8,128)(2,1)}, bf16[272,1024]{1,0:T(8,128)(2,1)S(1)}, u32[]{:S(2)}, u32[]{:S(2)}) collective-permute-start(bf16[272,1024]{1,0:T(8,128)(2,1)} %constant_dynamic-update-slice_fusion), channel_id=1, source_target_pairs={{0,5},{1,4},{4,1},{5,0},{2,7},{3,6},{6,3},{7,2},{8,13},{9,12},{12,... | collective-permute-start | bytes 1671176 | tf_op jit(solution)/shard_map/ppermute | solution.py:24
  51.3 6.7 %collective-permute-start.17 = (bf16[32,2304]{1,0:T(8,128)(2,1)S(1)}, bf16[32,2304]{1,0:T(8,128)(2,1)S(1)}, u32[]{:S(2)}, u32[]{:S(2)}) collective-permute-start(bf16[32,2304]{1,0:T(8,128)(2,1)S(1)} %get-tuple-element.84), channel_id=1, source_target_pairs={{0,5},{1,4},{4,1},{5,0},{2,7},{3,6},{6,3},{7,2},{8,13},{9,12},{12,... | collective-permute-start | bytes 442376 | tf_op jit(solution)/shard_map/ppermute | solution.py:24
  59.0 94.0 %all-gather.7.cloned.1.call-start = ((), (), s32[]{:S(2)}) async-start(), calls=%async_computation.4 | async-start | bytes 2654208 | tf_op jit(solution)/shard_map/all_gather | solution.py:134
  61.2 23.6 %collective-permute-start.6 = (bf16[256,1024]{1,0:T(8,128)(2,1)}, bf16[256,1024]{1,0:T(8,128)(2,1)}, u32[]{:S(2)}, u32[]{:S(2)}) collective-permute-start(bf16[256,1024]{1,0:T(8,128)(2,1)} %get-tuple-element.87), channel_id=1, source_target_pairs={{0,1},{1,0},{4,5},{5,4},{2,3},{3,2},{6,7},{7,6},{8,9},{9,8},{12,13... | collective-permute-start | bytes 1572872 | tf_op jit(solution)/shard_map/ppermute | solution.py:24
  62.0 22.8 %collective-permute-start.7 = (bf16[256,1024]{1,0:T(8,128)(2,1)}, bf16[256,1024]{1,0:T(8,128)(2,1)}, u32[]{:S(2)}, u32[]{:S(2)}) collective-permute-start(bf16[256,1024]{1,0:T(8,128)(2,1)} %get-tuple-element.87), channel_id=1, source_target_pairs={{0,4},{1,5},{4,0},{5,1},{2,6},{3,7},{6,2},{7,3},{8,12},{9,13},{12,... | collective-permute-start | bytes 1572872 | tf_op jit(solution)/shard_map/ppermute | solution.py:24
  63.1 21.7 %collective-permute-start.8 = (bf16[256,1024]{1,0:T(8,128)(2,1)}, bf16[256,1024]{1,0:T(8,128)(2,1)}, u32[]{:S(2)}, u32[]{:S(2)}) collective-permute-start(bf16[256,1024]{1,0:T(8,128)(2,1)} %get-tuple-element.87), channel_id=1, source_target_pairs={{0,5},{1,4},{4,1},{5,0},{2,7},{3,6},{6,3},{7,2},{8,13},{9,12},{12,... | collective-permute-start | bytes 1572872 | tf_op jit(solution)/shard_map/ppermute | solution.py:24
  87.7 14.4 %collective-permute-start.10 = (bf16[256,1024]{1,0:T(8,128)(2,1)}, bf16[256,1024]{1,0:T(8,128)(2,1)S(1)}, u32[]{:S(2)}, u32[]{:S(2)}) collective-permute-start(bf16[256,1024]{1,0:T(8,128)(2,1)} %get-tuple-element.56), channel_id=1, source_target_pairs={{0,4},{1,5},{4,0},{5,1},{2,6},{3,7},{6,2},{7,3},{8,12},{9,13},{12,... | collective-permute-start | bytes 1572872 | tf_op jit(solution)/shard_map/ppermute | solution.py:24
  89.0 19.5 %collective-permute-start.11 = (bf16[256,1024]{1,0:T(8,128)(2,1)}, bf16[256,1024]{1,0:T(8,128)(2,1)S(1)}, u32[]{:S(2)}, u32[]{:S(2)}) collective-permute-start(bf16[256,1024]{1,0:T(8,128)(2,1)} %get-tuple-element.55), channel_id=1, source_target_pairs={{0,5},{1,4},{4,1},{5,0},{2,7},{3,6},{6,3},{7,2},{8,13},{9,12},{12,... | collective-permute-start | bytes 1572872 | tf_op jit(solution)/shard_map/ppermute | solution.py:24
  90.3 20.3 %collective-permute-start.9 = (bf16[256,1024]{1,0:T(8,128)(2,1)}, bf16[256,1024]{1,0:T(8,128)(2,1)}, u32[]{:S(2)}, u32[]{:S(2)}) collective-permute-start(bf16[256,1024]{1,0:T(8,128)(2,1)} %get-tuple-element.54), channel_id=1, source_target_pairs={{0,1},{1,0},{4,5},{5,4},{2,3},{3,2},{6,7},{7,6},{8,9},{9,8},{12,13... | collective-permute-start | bytes 1572872 | tf_op jit(solution)/shard_map/ppermute | solution.py:24
  91.2 97.7 %reduce-scatter.4.cloned.1.call-start = ((), (), s32[]{:S(2)}) async-start(), calls=%async_computation.5 | async-start | bytes 2654208 | tf_op jit(solution)/shard_map/reduce_scatter | solution.py:180
  113.7 13.5 %collective-permute-start.12 = (bf16[256,1024]{1,0:T(8,128)(2,1)}, bf16[256,1024]{1,0:T(8,128)(2,1)}, u32[]{:S(2)}, u32[]{:S(2)}) collective-permute-start(bf16[256,1024]{1,0:T(8,128)(2,1)} %multiply_convert_fusion.7), channel_id=1, source_target_pairs={{0,1},{1,0},{4,5},{5,4},{2,3},{3,2},{6,7},{7,6},{8,9},{9,8},{12,13... | collective-permute-start | bytes 1572872 | tf_op jit(solution)/shard_map/ppermute | solution.py:24
  114.6 12.6 %collective-permute-start.13 = (bf16[256,1024]{1,0:T(8,128)(2,1)}, bf16[256,1024]{1,0:T(8,128)(2,1)}, u32[]{:S(2)}, u32[]{:S(2)}) collective-permute-start(bf16[256,1024]{1,0:T(8,128)(2,1)} %multiply_convert_fusion.7), channel_id=1, source_target_pairs={{0,4},{1,5},{4,0},{5,1},{2,6},{3,7},{6,2},{7,3},{8,12},{9,13},{12,... | collective-permute-start | bytes 1572872 | tf_op jit(solution)/shard_map/ppermute | solution.py:24
  115.9 16.9 %collective-permute-start.14 = (bf16[256,1024]{1,0:T(8,128)(2,1)}, bf16[256,1024]{1,0:T(8,128)(2,1)}, u32[]{:S(2)}, u32[]{:S(2)}) collective-permute-start(bf16[256,1024]{1,0:T(8,128)(2,1)} %multiply_convert_fusion.7), channel_id=1, source_target_pairs={{0,5},{1,4},{4,1},{5,0},{2,7},{3,6},{6,3},{7,2},{8,13},{9,12},{12,... | collective-permute-start | bytes 1572872 | tf_op jit(solution)/shard_map/ppermute | solution.py:24
  151.0 113.9 %reduce-scatter.6.cloned.1.call-start = ((), (), s32[]{:S(2)}) async-start(), calls=%async_computation.6 | async-start | bytes 5308416 | tf_op jit(solution)/shard_map/reduce_scatter | solution.py:192
  168.6 12.7 %collective-permute-start.18 = (bf16[256,1024]{1,0:T(8,128)(2,1)S(1)}, bf16[256,1024]{1,0:T(8,128)(2,1)S(1)}, u32[]{:S(2)}, u32[]{:S(2)}) collective-permute-start(bf16[256,1024]{1,0:T(8,128)(2,1)S(1)} %get-tuple-element.62), channel_id=1, source_target_pairs={{0,1},{1,0},{4,5},{5,4},{2,3},{3,2},{6,7},{7,6},{8,9},{9,8},{12,13... | collective-permute-start | bytes 1572872 | tf_op jit(solution)/shard_map/ppermute | solution.py:24
  169.3 12.0 %collective-permute-start.19 = (bf16[256,1024]{1,0:T(8,128)(2,1)S(1)}, bf16[256,1024]{1,0:T(8,128)(2,1)S(1)}, u32[]{:S(2)}, u32[]{:S(2)}) collective-permute-start(bf16[256,1024]{1,0:T(8,128)(2,1)S(1)} %get-tuple-element.64), channel_id=1, source_target_pairs={{0,4},{1,5},{4,0},{5,1},{2,6},{3,7},{6,2},{7,3},{8,12},{9,13},{12,... | collective-permute-start | bytes 1572872 | tf_op jit(solution)/shard_map/ppermute | solution.py:24
  170.8 15.4 %collective-permute-start.20 = (bf16[256,1024]{1,0:T(8,128)(2,1)S(1)}, bf16[256,1024]{1,0:T(8,128)(2,1)S(1)}, u32[]{:S(2)}, u32[]{:S(2)}) collective-permute-start(bf16[256,1024]{1,0:T(8,128)(2,1)S(1)} %get-tuple-element.63), channel_id=1, source_target_pairs={{0,5},{1,4},{4,1},{5,0},{2,7},{3,6},{6,3},{7,2},{8,13},{9,12},{12,... | collective-permute-start | bytes 1572872 | tf_op jit(solution)/shard_map/ppermute | solution.py:24
  196.0 111.6 %reduce-scatter.8.cloned.1.call-start = ((), (), s32[]{:S(2)}) async-start(), calls=%async_computation.7 | async-start | bytes 2727936 | tf_op jit(solution)/shard_map/reduce_scatter | solution.py:256
  199.1 14.0 %collective-permute-start.21 = (bf16[256,1024]{1,0:T(8,128)(2,1)S(1)}, bf16[256,1024]{1,0:T(8,128)(2,1)S(1)}, u32[]{:S(2)}, u32[]{:S(2)}) collective-permute-start(bf16[256,1024]{1,0:T(8,128)(2,1)S(1)} %get-tuple-element.40), channel_id=1, source_target_pairs={{0,1},{1,0},{4,5},{5,4},{2,3},{3,2},{6,7},{7,6},{8,9},{9,8},{12,13... | collective-permute-start | bytes 1572872 | tf_op jit(solution)/shard_map/ppermute | solution.py:24
  199.7 14.9 %collective-permute-start.22 = (bf16[256,1024]{1,0:T(8,128)(2,1)S(1)}, bf16[256,1024]{1,0:T(8,128)(2,1)S(1)}, u32[]{:S(2)}, u32[]{:S(2)}) collective-permute-start(bf16[256,1024]{1,0:T(8,128)(2,1)S(1)} %get-tuple-element.40), channel_id=1, source_target_pairs={{0,4},{1,5},{4,0},{5,1},{2,6},{3,7},{6,2},{7,3},{8,12},{9,13},{12,... | collective-permute-start | bytes 1572872 | tf_op jit(solution)/shard_map/ppermute | solution.py:24
  201.1 20.9 %collective-permute-start.23 = (bf16[256,1024]{1,0:T(8,128)(2,1)S(1)}, bf16[256,1024]{1,0:T(8,128)(2,1)S(1)}, u32[]{:S(2)}, u32[]{:S(2)}) collective-permute-start(bf16[256,1024]{1,0:T(8,128)(2,1)S(1)} %get-tuple-element.40), channel_id=1, source_target_pairs={{0,5},{1,4},{4,1},{5,0},{2,7},{3,6},{6,3},{7,2},{8,13},{9,12},{12,... | collective-permute-start | bytes 1572872 | tf_op jit(solution)/shard_map/ppermute | solution.py:24
  231.0 13.9 %collective-permute-start.24 = (bf16[256,1024]{1,0:T(8,128)(2,1)S(1)}, bf16[256,1024]{1,0:T(8,128)(2,1)S(1)}, u32[]{:S(2)}, u32[]{:S(2)}) collective-permute-start(bf16[256,1024]{1,0:T(8,128)(2,1)S(1)} %get-tuple-element.51), channel_id=1, source_target_pairs={{0,1},{1,0},{4,5},{5,4},{2,3},{3,2},{6,7},{7,6},{8,9},{9,8},{12,13... | collective-permute-start | bytes 1572872 | tf_op jit(solution)/shard_map/ppermute | solution.py:24
  232.5 14.9 %collective-permute-start.25 = (bf16[256,1024]{1,0:T(8,128)(2,1)S(1)}, bf16[256,1024]{1,0:T(8,128)(2,1)S(1)}, u32[]{:S(2)}, u32[]{:S(2)}) collective-permute-start(bf16[256,1024]{1,0:T(8,128)(2,1)S(1)} %get-tuple-element.53), channel_id=1, source_target_pairs={{0,4},{1,5},{4,0},{5,1},{2,6},{3,7},{6,2},{7,3},{8,12},{9,13},{12,... | collective-permute-start | bytes 1572872 | tf_op jit(solution)/shard_map/ppermute | solution.py:24
  233.9 19.6 %collective-permute-start.26 = (bf16[256,1024]{1,0:T(8,128)(2,1)S(1)}, bf16[256,1024]{1,0:T(8,128)(2,1)S(1)}, u32[]{:S(2)}, u32[]{:S(2)}) collective-permute-start(bf16[256,1024]{1,0:T(8,128)(2,1)S(1)} %get-tuple-element.52), channel_id=1, source_target_pairs={{0,5},{1,4},{4,1},{5,0},{2,7},{3,6},{6,3},{7,2},{8,13},{9,12},{12,... | collective-permute-start | bytes 1572872 | tf_op jit(solution)/shard_map/ppermute | solution.py:24
  280.4 16.6 %collective-permute-start.30 = (bf16[256,1024]{1,0:T(8,128)(2,1)}, bf16[256,1024]{1,0:T(8,128)(2,1)S(1)}, u32[]{:S(2)}, u32[]{:S(2)}) collective-permute-start(bf16[256,1024]{1,0:T(8,128)(2,1)} %get-tuple-element.59), channel_id=1, source_target_pairs={{0,1},{1,0},{4,5},{5,4},{2,3},{3,2},{6,7},{7,6},{8,9},{9,8},{12,13... | collective-permute-start | bytes 1572872 | tf_op jit(solution)/shard_map/ppermute | solution.py:24
  281.2 15.9 %collective-permute-start.31 = (bf16[256,1024]{1,0:T(8,128)(2,1)}, bf16[256,1024]{1,0:T(8,128)(2,1)}, u32[]{:S(2)}, u32[]{:S(2)}) collective-permute-start(bf16[256,1024]{1,0:T(8,128)(2,1)} %get-tuple-element.61), channel_id=1, source_target_pairs={{0,4},{1,5},{4,0},{5,1},{2,6},{3,7},{6,2},{7,3},{8,12},{9,13},{12,... | collective-permute-start | bytes 1572872 | tf_op jit(solution)/shard_map/ppermute | solution.py:24
  282.6 17.9 %collective-permute-start.32 = (bf16[256,1024]{1,0:T(8,128)(2,1)}, bf16[256,1024]{1,0:T(8,128)(2,1)}, u32[]{:S(2)}, u32[]{:S(2)}) collective-permute-start(bf16[256,1024]{1,0:T(8,128)(2,1)} %get-tuple-element.60), channel_id=1, source_target_pairs={{0,5},{1,4},{4,1},{5,0},{2,7},{3,6},{6,3},{7,2},{8,13},{9,12},{12,... | collective-permute-start | bytes 1572872 | tf_op jit(solution)/shard_map/ppermute | solution.py:24
  308.6 6.5 %collective-permute-start.33 = (bf16[112,256]{1,0:T(8,128)(2,1)S(1)}, bf16[112,256]{1,0:T(8,128)(2,1)S(1)}, u32[]{:S(2)}, u32[]{:S(2)}) collective-permute-start(bf16[112,256]{1,0:T(8,128)(2,1)S(1)} %get-tuple-element.105), channel_id=1, source_target_pairs={{0,1},{1,0},{4,5},{5,4},{2,3},{3,2},{6,7},{7,6},{8,9},{9,8},{12,13... | collective-permute-start | bytes 172040 | tf_op jit(solution)/shard_map/ppermute | solution.py:24
  (37 other events, 229.8 us)
Sparse Core Ops, SparseCore 0:
  20.7 31.0 all-gather.8
  59.2 51.8 all-gather.4
  112.7 30.4 all-gather.6
  151.1 36.7 reduce-scatter.3
  196.1 55.7 reduce-scatter.5
  268.6 38.9 reduce-scatter.7

commit v5 on v4

--- a/solution.py
+++ b/solution.py
@@ -52,6 +52,12 @@
             other = other[(slice(0, 1),) * other.ndim].reshape(())
         values = values + jnp.minimum(jnp.abs(other), 0).astype(values.dtype)
     return values
+
+
+def tile_after(values, *others):
+    corner = (0,) * values.ndim
+    tile = lax.slice(values, corner, (1,) * (values.ndim - 2) + (16, 128))
+    return lax.dynamic_update_slice(values, after(tile, *others), corner)
 
 
 def norm_back(grad_norm, source, scale, gain):
@@ -188,7 +194,8 @@
         dnormed_two = plane_sum(dnormed_part)
         hidden_part, gain_two_grad, row_mean = norm_back(dnormed_two, hidden, scale_two, gain_second)
         pair_grad = pair_grad.reshape(t, 2, 2, 2 * r, 2 * nb * h).transpose(0, 2, 1, 3, 4)
-        pair_grad = after(pair_grad.reshape(nb, 4 * r, 2 * nb * h), down_sum, row_mean)
+        pair_grad = lax.optimization_barrier(pair_grad.reshape(nb, 4 * r, 2 * nb * h))
+        pair_grad = tile_after(pair_grad, down_sum, row_mean)
         pair_sum = lax.psum_scatter(pair_grad, COLUMN, scatter_dimension=0)
         dhidden = dout + hidden_part
 
@@ -214,8 +221,8 @@
             + kernel_vals[2] * lifted(dconv * same_two, 2)
         )
         dprojected = jnp.concatenate([dproduct * stream, dsecond, dproduct * first], axis=2)
-        dprojected = dprojected.astype(BF).reshape(4 * slots, 3 * share)
-        dnormed_part = after(cols_by_cols(dprojected, in_full), mixed[:16, :128])
+        dprojected = after(dprojected.astype(BF).reshape(4 * slots, 3 * share), mixed[:16, :128])
+        dnormed_part = cols_by_cols(dprojected, in_full)
         gain_one_grad = jnp.sum(dnormed_part * source * scale_one, axis=0)
         pair_shard = plane_swap(pair_sum.reshape(4, r, 2 * nb * h), member)
         dnormed_one = plane_sum(dnormed_part.reshape(4, slots, width), pair_shard[3])

time: 332 us -> 320 us (0.964)
  other arithmetic: 39.4 us -> 34 us
  matrix products: 61.5 us -> 56.6 us
    dot_general x4, matrix products: 23.8 us -> 20.2 us  [cols_by_cols(): lax.dot_general(left, right, (((1,), (1,)), ((), ())), preferred_element_...]
    add x7 -> x6, other arithmetic: 10.1 us -> 7.35 us  [after(): values = values + jnp.minimum(jnp.abs(other), 0).astype(values.dtype)]
    unnamed x66 -> x64, local copies, waits for them, and re-layouts: 11.6 us -> 10.6 us
  transfers between devices with their start and end apart: 42 -> 42, of which waited for: 26 -> 27; matrix products, arithmetic and copies ran while one was open for 40% -> 40% of each run, Pallas kernels for 0% -> 0%
where the time goes in v5:
time: 320 us; the launch traced here: 314 us
  waiting for transfers between devices  102 us (32%)
  matrix products  56.6 us (18%)
  local copies, waits for them, and re-layouts  54.5 us (17%)
  starting transfers between devices  44.8 us (14%)
  other arithmetic  34 us (11%)
  between operations  22.3 us (7%)
    ppermute x36, waiting for transfers between devices, to_peer(): return lax.ppermute(values, PLANE, [(i, i ^ k) for i in range(4)])  100 us
    ppermute x36, starting transfers between devices, to_peer(): return lax.ppermute(values, PLANE, [(i, i ^ k) for i in range(4)])  43.3 us
    dot_general x4, matrix products, cols_by_cols(): lax.dot_general(left, right, (((1,), (1,)), ((), ())), preferred_element_...  20.2 us
    dot_general x4, matrix products, rows_by_rows(): lax.dot_general(left, right, (((0,), (0,)), ((), ())), preferred_element_...  16.1 us
    unnamed x64, local copies, waits for them, and re-layouts  10.6 us
    dot_general x1, matrix products, local(): both = jnp.dot(normed_two, pair_full, preferred_element_type=F32)  7.39 us
    add x6, other arithmetic, after(): values = values + jnp.minimum(jnp.abs(other), 0).astype(values.dtype)  7.35 us
    slice x9, local copies, waits for them, and re-layouts, after(): other = other[(slice(0, 1),) * other.ndim].reshape(())  6.67 us
  transfers between devices with their start and end apart: 42, of which 27 were waited for; matrix products, arithmetic and copies ran while one was open for 40% of the time, Pallas kernels for 0%

profile of v5, /device:TPU:0, one launch (start us, length us, event | category | flops | bytes accessed | tf_op | source)
XLA Modules:
  0.0 313.8 jit_solution(15980161035699784108)
XLA Ops:
  10.1 3.0 collective-permute-start.3
  15.3 2.4 collective-permute-done.4
  23.6 2.3 collective-permute-start.2
  30.4 6.9 %collective-permute-done = bf16[272,1024]{1,0:T(8,128)(2,1)S(1)} collective-permute-done((bf16[272,1024]{1,0:T(8,128)(2,1)}, bf16[272,1024]{1,0:T(8,128)(2,1)S(1)}, u32[]{:S(2)}, u32[]{:S(2)}) %collective-permute-start) | collective-permute-done | bytes 557088 | tf_op jit(solution)/shard_map/ppermute | solution.py:24
  40.5 7.9 %collective-permute-done.2 = bf16[272,1024]{1,0:T(8,128)(2,1)S(1)} collective-permute-done((bf16[272,1024]{1,0:T(8,128)(2,1)}, bf16[272,1024]{1,0:T(8,128)(2,1)S(1)}, u32[]{:S(2)}, u32[]{:S(2)}) %collective-permute-start.2) | collective-permute-done | bytes 557088 | tf_op jit(solution)/shard_map/ppermute | solution.py:24
  75.5 4.6 %fusion.71 = f32[1024,768]{1,0:T(8,128)S(1)} fusion(bf16[1024,768]{1,0:T(8,128)(2,1)} %bitcast.276, f32[1024,1024]{1,0:T(8,128)} %copy-done, f32[1024]{0:T(1024)S(1)} %bitcast.325, f32[1024]{0:T(1024)S(1)} %add_rsqrt_fusion), kind=kOutput, calls=%fused_computation.231 | convolution fusion | flops 1613758464 | bytes 8921088 | tf_op jit(solution)/shard_map/dot_general | solution.py:160
  82.1 2.7 fusion.83
  84.8 2.9 fusion.44
  91.9 10.3 %collective-permute-done.10 = bf16[256,1024]{1,0:T(8,128)(2,1)S(1)} collective-permute-done((bf16[256,1024]{1,0:T(8,128)(2,1)}, bf16[256,1024]{1,0:T(8,128)(2,1)S(1)}, u32[]{:S(2)}, u32[]{:S(2)}) %collective-permute-start.10) | collective-permute-done | bytes 524320 | tf_op jit(solution)/shard_map/ppermute | solution.py:24
  102.1 6.4 %collective-permute-done.11 = bf16[256,1024]{1,0:T(8,128)(2,1)S(1)} collective-permute-done((bf16[256,1024]{1,0:T(8,128)(2,1)}, bf16[256,1024]{1,0:T(8,128)(2,1)S(1)}, u32[]{:S(2)}, u32[]{:S(2)}) %collective-permute-start.11) | collective-permute-done | bytes 524320 | tf_op jit(solution)/shard_map/ppermute | solution.py:24
  117.3 2.8 copy.89
  120.1 7.1 %collective-permute-done.12 = bf16[256,1024]{1,0:T(8,128)(2,1)} collective-permute-done((bf16[256,1024]{1,0:T(8,128)(2,1)}, bf16[256,1024]{1,0:T(8,128)(2,1)}, u32[]{:S(2)}, u32[]{:S(2)}) %collective-permute-start.12) | collective-permute-done | bytes 524320 | tf_op jit(solution)/shard_map/ppermute | solution.py:24
  127.2 5.6 %collective-permute-done.14 = bf16[256,1024]{1,0:T(8,128)(2,1)} collective-permute-done((bf16[256,1024]{1,0:T(8,128)(2,1)}, bf16[256,1024]{1,0:T(8,128)(2,1)}, u32[]{:S(2)}, u32[]{:S(2)}) %collective-permute-start.14) | collective-permute-done | bytes 524320 | tf_op jit(solution)/shard_map/ppermute | solution.py:24
  132.9 7.4 %fusion.46 = f32[1024,2304]{1,0:T(8,128)S(1)} fusion(bf16[1024,2304]{1,0:T(8,128)(2,1)S(1)} %bitcast.257, bf16[256,1024]{1,0:T(8,128)(2,1)} %collective-permute-done.14, bf16[256,1024]{1,0:T(8,128)(2,1)} %collective-permute-done.13, bf16[256,1024]{1,0:T(8,128)(2,1)} %collective-permute-done.12, bf16[256,1024]{1,0:T(8,128)(2,1)} %multiply_convert_fusion.7), kind=kOutput, calls=%fused_computation.134 | convolution fusion | flops 4840226816 | bytes 16252928 | tf_op jit(solution)/shard_map/dot_general | solution.py:179
  145.4 5.6 %convolution_convert_fusion.1 = bf16[1152,1024]{1,0:T(8,128)(2,1)} fusion(bf16[1024,1152]{1,0:T(8,128)(2,1)S(1)} %multiply_convert_fusion.2, bf16[256,1024]{1,0:T(8,128)(2,1)} %collective-permute-done.8, bf16[256,1024]{1,0:T(8,128)(2,1)} %collective-permute-done.7, bf16[256,1024]{1,0:T(8,128)(2,1)} %collective-permute-done.6, ...), kind=kOutput, calls=%fused_computation.13 | convolution fusion | flops 2425487360 | bytes 6815744 | tf_op jit(solution)/shard_map/dot_general | solution.py:16
  153.1 8.5 %multiply_convert_fusion.1 = (bf16[1024,1152]{1,0:T(8,128)(2,1)S(1)}, bf16[1024,1152]{1,0:T(8,128)(2,1)S(1)}) fusion(f32[1024,2304]{1,0:T(8,128)} %copy-done.5, f32[]{:T(128)S(6)} %convert.63, bf16[1152,1024]{1,0:T(8,128)(2,1)} %all-gather.7.cloned.1.call-done, bf16[256,1024]{1,0:T(8,128)(2,1)} %collective-permute-done.8, ...), kind=kOutput, calls=%fused_computation.3 | convolution fusion | flops 2440822784 | bytes 18612228 | tf_op jit(solution)/shard_map/dot_general | solution.py:20
  161.6 7.0 %fusion.84 = (bf16[1024,1024]{1,0:T(8,128)(2,1)S(1)}, f32[1024,1024]{1,0:T(8,128)S(1)}) fusion(bf16[1024,2304]{1,0:T(8,128)(2,1)} %bitcast.258, bf16[1024,1152]{1,0:T(8,128)(2,1)S(1)} %get-tuple-element.48, bf16[1024,1152]{1,0:T(8,128)(2,1)S(1)} %get-tuple-element.47), kind=kOutput, calls=%fused_computation.242 | convolution fusion | flops 4842323968 | bytes 15728640 | tf_op jit(solution)/shard_map/dot_general | solution.py:20
  172.2 7.7 %convolution_convert_fusion = bf16[1024,2304]{1,0:T(8,128)(2,1)S(1)} fusion(bf16[1024,1152]{1,0:T(8,128)(2,1)S(1)} %get-tuple-element.48, bf16[1024,1152]{1,0:T(8,128)(2,1)S(1)} %get-tuple-element.47, bf16[256,1024]{1,0:T(8,128)(2,1)} %collective-permute-done.14, bf16[256,1024]{1,0:T(8,128)(2,1)} %collective-permute-done.13, ...), kind=kOutput, calls=%fused_computation | convolution fusion | flops 4852023296 | bytes 11534336 | tf_op jit(solution)/shard_map/dot_general | solution.py:16
  179.9 2.6 copy.90
  182.5 3.8 %collective-permute-done.20 = bf16[256,1024]{1,0:T(8,128)(2,1)S(1)} collective-permute-done((bf16[256,1024]{1,0:T(8,128)(2,1)S(1)}, bf16[256,1024]{1,0:T(8,128)(2,1)S(1)}, u32[]{:S(2)}, u32[]{:S(2)}) %collective-permute-start.20) | collective-permute-done | bytes 524320 | tf_op jit(solution)/shard_map/ppermute | solution.py:24
  192.4 2.9 fusion.73
  198.7 4.7 %fusion.85 = f32[1024,1024]{1,0:T(8,128)S(1)} fusion(bf16[1024,1152]{1,0:T(8,128)(2,1)S(1)} %copy-done.10, bf16[1152,1024]{1,0:T(8,128)(2,1)} %all-gather.7.cloned.1.call-done), kind=kOutput, calls=%fused_computation.243 | convolution fusion | flops 2415919104 | bytes 8912896 | tf_op jit(solution)/shard_map/dot_general | solution.py:205
  203.8 5.4 %collective-permute-done.21 = bf16[256,1024]{1,0:T(8,128)(2,1)S(1)} collective-permute-done((bf16[256,1024]{1,0:T(8,128)(2,1)S(1)}, bf16[256,1024]{1,0:T(8,128)(2,1)S(1)}, u32[]{:S(2)}, u32[]{:S(2)}) %collective-permute-start.21) | collective-permute-done | bytes 524320 | tf_op jit(solution)/shard_map/ppermute | solution.py:24
  210.6 7.5 %collective-permute-done.23 = bf16[256,1024]{1,0:T(8,128)(2,1)S(1)} collective-permute-done((bf16[256,1024]{1,0:T(8,128)(2,1)S(1)}, bf16[256,1024]{1,0:T(8,128)(2,1)S(1)}, u32[]{:S(2)}, u32[]{:S(2)}) %collective-permute-start.23) | collective-permute-done | bytes 524320 | tf_op jit(solution)/shard_map/ppermute | solution.py:24
  226.1 6.9 %collective-permute-done.24 = bf16[256,1024]{1,0:T(8,128)(2,1)S(1)} collective-permute-done((bf16[256,1024]{1,0:T(8,128)(2,1)S(1)}, bf16[256,1024]{1,0:T(8,128)(2,1)S(1)}, u32[]{:S(2)}, u32[]{:S(2)}) %collective-permute-start.24) | collective-permute-done | bytes 524320 | tf_op jit(solution)/shard_map/ppermute | solution.py:24
  233.0 2.6 collective-permute-done.25
  235.6 6.3 %collective-permute-done.26 = bf16[256,1024]{1,0:T(8,128)(2,1)S(1)} collective-permute-done((bf16[256,1024]{1,0:T(8,128)(2,1)S(1)}, bf16[256,1024]{1,0:T(8,128)(2,1)S(1)}, u32[]{:S(2)}, u32[]{:S(2)}) %collective-permute-start.26) | collective-permute-done | bytes 524320 | tf_op jit(solution)/shard_map/ppermute | solution.py:24
  247.1 4.0 %multiply_reduce_fusion = (bf16[1024]{0:T(1024)(128)(2,1)S(1)}, bf16[1024,1024]{1,0:T(8,128)(2,1)}, f32[1024,1024]{1,0:T(8,128)}) fusion(f32[1024,1024]{1,0:T(8,128)S(1)} %copy-done.1, f32[1024]{0:T(1024)S(1)} %add_rsqrt_fusion, bf16[1024,768]{1,0:T(8,128)(2,1)S(1)} %bitcast.277, bf16[1024,256]{1,0:T(8,128)(2,1)S(1)} %bitcast.290, ...), kind=kOutput, calls=%fused_computation.9 | convolution fusion | flops 1621097472 | bytes 13637634 | tf_op jit(solution)/shard_map/dot_general | solution.py:20
  264.2 2.3 collective-permute-done.29
  273.6 4.9 %reshape.485 = f32[2,2,32,2,4,2,144]{6,5,4,3,2,1,0:T(2,128)S(1)} reshape(f32[4,32,2304]{2,1,0:T(8,128)} %maximum_convert_fusion) | data formatting | bytes 2359296 | tf_op jit(solution)/shard_map/convert_element_type | solution.py:275
  285.7 3.3 %collective-permute-done.32 = bf16[256,1024]{1,0:T(8,128)(2,1)} collective-permute-done((bf16[256,1024]{1,0:T(8,128)(2,1)}, bf16[256,1024]{1,0:T(8,128)(2,1)}, u32[]{:S(2)}, u32[]{:S(2)}) %collective-permute-start.32) | collective-permute-done | bytes 524320 | tf_op jit(solution)/shard_map/ppermute | solution.py:24
  291.0 3.0 fusion.11
  (287 shorter events, 130.5 us)
Async XLA Ops:
  7.2 60.9 %all-gather.9.cloned.1.call-start = ((), (), s32[]{:S(2)}) async-start(), calls=%async_computation.8 | async-start | bytes 2654208 | tf_op jit(solution)/shard_map/all_gather | solution.py:120
  20.6 96.7 %all-gather.5.cloned.1.call-start = ((), (), s32[]{:S(2)}) async-start(), calls=%async_computation.3 | async-start | bytes 5308416 | tf_op jit(solution)/shard_map/all_gather | solution.py:137
  22.4 14.9 %collective-permute-start = (bf16[272,1024]{1,0:T(8,128)(2,1)}, bf16[272,1024]{1,0:T(8,128)(2,1)S(1)}, u32[]{:S(2)}, u32[]{:S(2)}) collective-permute-start(bf16[272,1024]{1,0:T(8,128)(2,1)} %constant_dynamic-update-slice_fusion.1), channel_id=1, source_target_pairs={{0,1},{1,0},{4,5},{5,4},{2,3},{3,2},{6,7},{7,6},{8,9},{9,8},{12,13... | collective-permute-start | bytes 1671176 | tf_op jit(solution)/shard_map/ppermute | solution.py:24
  22.9 15.8 %collective-permute-start.1 = (bf16[272,1024]{1,0:T(8,128)(2,1)}, bf16[272,1024]{1,0:T(8,128)(2,1)S(1)}, u32[]{:S(2)}, u32[]{:S(2)}) collective-permute-start(bf16[272,1024]{1,0:T(8,128)(2,1)} %constant_dynamic-update-slice_fusion.1), channel_id=1, source_target_pairs={{0,4},{1,5},{4,0},{5,1},{2,6},{3,7},{6,2},{7,3},{8,12},{9,13},{12,... | collective-permute-start | bytes 1671176 | tf_op jit(solution)/shard_map/ppermute | solution.py:24
  23.6 24.8 %collective-permute-start.2 = (bf16[272,1024]{1,0:T(8,128)(2,1)}, bf16[272,1024]{1,0:T(8,128)(2,1)S(1)}, u32[]{:S(2)}, u32[]{:S(2)}) collective-permute-start(bf16[272,1024]{1,0:T(8,128)(2,1)} %constant_dynamic-update-slice_fusion.1), channel_id=1, source_target_pairs={{0,5},{1,4},{4,1},{5,0},{2,7},{3,6},{6,3},{7,2},{8,13},{9,12},{12,... | collective-permute-start | bytes 1671176 | tf_op jit(solution)/shard_map/ppermute | solution.py:24
  51.3 6.7 %collective-permute-start.17 = (bf16[32,2304]{1,0:T(8,128)(2,1)S(1)}, bf16[32,2304]{1,0:T(8,128)(2,1)S(1)}, u32[]{:S(2)}, u32[]{:S(2)}) collective-permute-start(bf16[32,2304]{1,0:T(8,128)(2,1)S(1)} %get-tuple-element.84), channel_id=1, source_target_pairs={{0,5},{1,4},{4,1},{5,0},{2,7},{3,6},{6,3},{7,2},{8,13},{9,12},{12,... | collective-permute-start | bytes 442376 | tf_op jit(solution)/shard_map/ppermute | solution.py:24
  59.0 94.1 %all-gather.7.cloned.1.call-start = ((), (), s32[]{:S(2)}) async-start(), calls=%async_computation.4 | async-start | bytes 2654208 | tf_op jit(solution)/shard_map/all_gather | solution.py:140
  61.2 23.6 %collective-permute-start.6 = (bf16[256,1024]{1,0:T(8,128)(2,1)}, bf16[256,1024]{1,0:T(8,128)(2,1)}, u32[]{:S(2)}, u32[]{:S(2)}) collective-permute-start(bf16[256,1024]{1,0:T(8,128)(2,1)} %get-tuple-element.87), channel_id=1, source_target_pairs={{0,1},{1,0},{4,5},{5,4},{2,3},{3,2},{6,7},{7,6},{8,9},{9,8},{12,13... | collective-permute-start | bytes 1572872 | tf_op jit(solution)/shard_map/ppermute | solution.py:24
  62.1 22.8 %collective-permute-start.7 = (bf16[256,1024]{1,0:T(8,128)(2,1)}, bf16[256,1024]{1,0:T(8,128)(2,1)}, u32[]{:S(2)}, u32[]{:S(2)}) collective-permute-start(bf16[256,1024]{1,0:T(8,128)(2,1)} %get-tuple-element.87), channel_id=1, source_target_pairs={{0,4},{1,5},{4,0},{5,1},{2,6},{3,7},{6,2},{7,3},{8,12},{9,13},{12,... | collective-permute-start | bytes 1572872 | tf_op jit(solution)/shard_map/ppermute | solution.py:24
  63.1 21.7 %collective-permute-start.8 = (bf16[256,1024]{1,0:T(8,128)(2,1)}, bf16[256,1024]{1,0:T(8,128)(2,1)}, u32[]{:S(2)}, u32[]{:S(2)}) collective-permute-start(bf16[256,1024]{1,0:T(8,128)(2,1)} %get-tuple-element.87), channel_id=1, source_target_pairs={{0,5},{1,4},{4,1},{5,0},{2,7},{3,6},{6,3},{7,2},{8,13},{9,12},{12,... | collective-permute-start | bytes 1572872 | tf_op jit(solution)/shard_map/ppermute | solution.py:24
  87.7 14.4 %collective-permute-start.10 = (bf16[256,1024]{1,0:T(8,128)(2,1)}, bf16[256,1024]{1,0:T(8,128)(2,1)S(1)}, u32[]{:S(2)}, u32[]{:S(2)}) collective-permute-start(bf16[256,1024]{1,0:T(8,128)(2,1)} %get-tuple-element.56), channel_id=1, source_target_pairs={{0,4},{1,5},{4,0},{5,1},{2,6},{3,7},{6,2},{7,3},{8,12},{9,13},{12,... | collective-permute-start | bytes 1572872 | tf_op jit(solution)/shard_map/ppermute | solution.py:24
  89.0 19.5 %collective-permute-start.11 = (bf16[256,1024]{1,0:T(8,128)(2,1)}, bf16[256,1024]{1,0:T(8,128)(2,1)S(1)}, u32[]{:S(2)}, u32[]{:S(2)}) collective-permute-start(bf16[256,1024]{1,0:T(8,128)(2,1)} %get-tuple-element.55), channel_id=1, source_target_pairs={{0,5},{1,4},{4,1},{5,0},{2,7},{3,6},{6,3},{7,2},{8,13},{9,12},{12,... | collective-permute-start | bytes 1572872 | tf_op jit(solution)/shard_map/ppermute | solution.py:24
  90.4 20.3 %collective-permute-start.9 = (bf16[256,1024]{1,0:T(8,128)(2,1)}, bf16[256,1024]{1,0:T(8,128)(2,1)}, u32[]{:S(2)}, u32[]{:S(2)}) collective-permute-start(bf16[256,1024]{1,0:T(8,128)(2,1)} %get-tuple-element.54), channel_id=1, source_target_pairs={{0,1},{1,0},{4,5},{5,4},{2,3},{3,2},{6,7},{7,6},{8,9},{9,8},{12,13... | collective-permute-start | bytes 1572872 | tf_op jit(solution)/shard_map/ppermute | solution.py:24
  91.2 97.7 %reduce-scatter.4.cloned.1.call-start = ((), (), s32[]{:S(2)}) async-start(), calls=%async_computation.5 | async-start | bytes 2654208 | tf_op jit(solution)/shard_map/reduce_scatter | solution.py:186
  113.8 13.4 %collective-permute-start.12 = (bf16[256,1024]{1,0:T(8,128)(2,1)}, bf16[256,1024]{1,0:T(8,128)(2,1)}, u32[]{:S(2)}, u32[]{:S(2)}) collective-permute-start(bf16[256,1024]{1,0:T(8,128)(2,1)} %multiply_convert_fusion.7), channel_id=1, source_target_pairs={{0,1},{1,0},{4,5},{5,4},{2,3},{3,2},{6,7},{7,6},{8,9},{9,8},{12,13... | collective-permute-start | bytes 1572872 | tf_op jit(solution)/shard_map/ppermute | solution.py:24
  114.7 12.6 %collective-permute-start.13 = (bf16[256,1024]{1,0:T(8,128)(2,1)}, bf16[256,1024]{1,0:T(8,128)(2,1)}, u32[]{:S(2)}, u32[]{:S(2)}) collective-permute-start(bf16[256,1024]{1,0:T(8,128)(2,1)} %multiply_convert_fusion.7), channel_id=1, source_target_pairs={{0,4},{1,5},{4,0},{5,1},{2,6},{3,7},{6,2},{7,3},{8,12},{9,13},{12,... | collective-permute-start | bytes 1572872 | tf_op jit(solution)/shard_map/ppermute | solution.py:24
  116.0 16.9 %collective-permute-start.14 = (bf16[256,1024]{1,0:T(8,128)(2,1)}, bf16[256,1024]{1,0:T(8,128)(2,1)}, u32[]{:S(2)}, u32[]{:S(2)}) collective-permute-start(bf16[256,1024]{1,0:T(8,128)(2,1)} %multiply_convert_fusion.7), channel_id=1, source_target_pairs={{0,5},{1,4},{4,1},{5,0},{2,7},{3,6},{6,3},{7,2},{8,13},{9,12},{12,... | collective-permute-start | bytes 1572872 | tf_op jit(solution)/shard_map/ppermute | solution.py:24
  151.0 101.2 %reduce-scatter.6.cloned.1.call-start = ((), (), s32[]{:S(2)}) async-start(), calls=%async_computation.6 | async-start | bytes 5308416 | tf_op jit(solution)/shard_map/reduce_scatter | solution.py:199
  168.7 13.8 %collective-permute-start.18 = (bf16[256,1024]{1,0:T(8,128)(2,1)S(1)}, bf16[256,1024]{1,0:T(8,128)(2,1)S(1)}, u32[]{:S(2)}, u32[]{:S(2)}) collective-permute-start(bf16[256,1024]{1,0:T(8,128)(2,1)S(1)} %get-tuple-element.62), channel_id=1, source_target_pairs={{0,1},{1,0},{4,5},{5,4},{2,3},{3,2},{6,7},{7,6},{8,9},{9,8},{12,13... | collective-permute-start | bytes 1572872 | tf_op jit(solution)/shard_map/ppermute | solution.py:24
  169.4 13.1 %collective-permute-start.19 = (bf16[256,1024]{1,0:T(8,128)(2,1)S(1)}, bf16[256,1024]{1,0:T(8,128)(2,1)S(1)}, u32[]{:S(2)}, u32[]{:S(2)}) collective-permute-start(bf16[256,1024]{1,0:T(8,128)(2,1)S(1)} %get-tuple-element.64), channel_id=1, source_target_pairs={{0,4},{1,5},{4,0},{5,1},{2,6},{3,7},{6,2},{7,3},{8,12},{9,13},{12,... | collective-permute-start | bytes 1572872 | tf_op jit(solution)/shard_map/ppermute | solution.py:24
  170.9 15.4 %collective-permute-start.20 = (bf16[256,1024]{1,0:T(8,128)(2,1)S(1)}, bf16[256,1024]{1,0:T(8,128)(2,1)S(1)}, u32[]{:S(2)}, u32[]{:S(2)}) collective-permute-start(bf16[256,1024]{1,0:T(8,128)(2,1)S(1)} %get-tuple-element.63), channel_id=1, source_target_pairs={{0,5},{1,4},{4,1},{5,0},{2,7},{3,6},{6,3},{7,2},{8,13},{9,12},{12,... | collective-permute-start | bytes 1572872 | tf_op jit(solution)/shard_map/ppermute | solution.py:24
  192.1 102.9 %reduce-scatter.8.cloned.1.call-start = ((), (), s32[]{:S(2)}) async-start(), calls=%async_computation.7 | async-start | bytes 2727936 | tf_op jit(solution)/shard_map/reduce_scatter | solution.py:263
  195.2 14.0 %collective-permute-start.21 = (bf16[256,1024]{1,0:T(8,128)(2,1)S(1)}, bf16[256,1024]{1,0:T(8,128)(2,1)S(1)}, u32[]{:S(2)}, u32[]{:S(2)}) collective-permute-start(bf16[256,1024]{1,0:T(8,128)(2,1)S(1)} %get-tuple-element.40), channel_id=1, source_target_pairs={{0,1},{1,0},{4,5},{5,4},{2,3},{3,2},{6,7},{7,6},{8,9},{9,8},{12,13... | collective-permute-start | bytes 1572872 | tf_op jit(solution)/shard_map/ppermute | solution.py:24
  195.8 14.9 %collective-permute-start.22 = (bf16[256,1024]{1,0:T(8,128)(2,1)S(1)}, bf16[256,1024]{1,0:T(8,128)(2,1)S(1)}, u32[]{:S(2)}, u32[]{:S(2)}) collective-permute-start(bf16[256,1024]{1,0:T(8,128)(2,1)S(1)} %get-tuple-element.40), channel_id=1, source_target_pairs={{0,4},{1,5},{4,0},{5,1},{2,6},{3,7},{6,2},{7,3},{8,12},{9,13},{12,... | collective-permute-start | bytes 1572872 | tf_op jit(solution)/shard_map/ppermute | solution.py:24
  197.4 20.7 %collective-permute-start.23 = (bf16[256,1024]{1,0:T(8,128)(2,1)S(1)}, bf16[256,1024]{1,0:T(8,128)(2,1)S(1)}, u32[]{:S(2)}, u32[]{:S(2)}) collective-permute-start(bf16[256,1024]{1,0:T(8,128)(2,1)S(1)} %get-tuple-element.40), channel_id=1, source_target_pairs={{0,5},{1,4},{4,1},{5,0},{2,7},{3,6},{6,3},{7,2},{8,13},{9,12},{12,... | collective-permute-start | bytes 1572872 | tf_op jit(solution)/shard_map/ppermute | solution.py:24
  219.1 13.9 %collective-permute-start.24 = (bf16[256,1024]{1,0:T(8,128)(2,1)S(1)}, bf16[256,1024]{1,0:T(8,128)(2,1)S(1)}, u32[]{:S(2)}, u32[]{:S(2)}) collective-permute-start(bf16[256,1024]{1,0:T(8,128)(2,1)S(1)} %get-tuple-element.51), channel_id=1, source_target_pairs={{0,1},{1,0},{4,5},{5,4},{2,3},{3,2},{6,7},{7,6},{8,9},{9,8},{12,13... | collective-permute-start | bytes 1572872 | tf_op jit(solution)/shard_map/ppermute | solution.py:24
  220.8 14.9 %collective-permute-start.25 = (bf16[256,1024]{1,0:T(8,128)(2,1)S(1)}, bf16[256,1024]{1,0:T(8,128)(2,1)S(1)}, u32[]{:S(2)}, u32[]{:S(2)}) collective-permute-start(bf16[256,1024]{1,0:T(8,128)(2,1)S(1)} %get-tuple-element.53), channel_id=1, source_target_pairs={{0,4},{1,5},{4,0},{5,1},{2,6},{3,7},{6,2},{7,3},{8,12},{9,13},{12,... | collective-permute-start | bytes 1572872 | tf_op jit(solution)/shard_map/ppermute | solution.py:24
  222.2 19.7 %collective-permute-start.26 = (bf16[256,1024]{1,0:T(8,128)(2,1)S(1)}, bf16[256,1024]{1,0:T(8,128)(2,1)S(1)}, u32[]{:S(2)}, u32[]{:S(2)}) collective-permute-start(bf16[256,1024]{1,0:T(8,128)(2,1)S(1)} %get-tuple-element.52), channel_id=1, source_target_pairs={{0,5},{1,4},{4,1},{5,0},{2,7},{3,6},{6,3},{7,2},{8,13},{9,12},{12,... | collective-permute-start | bytes 1572872 | tf_op jit(solution)/shard_map/ppermute | solution.py:24
  269.0 16.7 %collective-permute-start.30 = (bf16[256,1024]{1,0:T(8,128)(2,1)}, bf16[256,1024]{1,0:T(8,128)(2,1)S(1)}, u32[]{:S(2)}, u32[]{:S(2)}) collective-permute-start(bf16[256,1024]{1,0:T(8,128)(2,1)} %get-tuple-element.59), channel_id=1, source_target_pairs={{0,1},{1,0},{4,5},{5,4},{2,3},{3,2},{6,7},{7,6},{8,9},{9,8},{12,13... | collective-permute-start | bytes 1572872 | tf_op jit(solution)/shard_map/ppermute | solution.py:24
  269.9 15.8 %collective-permute-start.31 = (bf16[256,1024]{1,0:T(8,128)(2,1)}, bf16[256,1024]{1,0:T(8,128)(2,1)}, u32[]{:S(2)}, u32[]{:S(2)}) collective-permute-start(bf16[256,1024]{1,0:T(8,128)(2,1)} %get-tuple-element.61), channel_id=1, source_target_pairs={{0,4},{1,5},{4,0},{5,1},{2,6},{3,7},{6,2},{7,3},{8,12},{9,13},{12,... | collective-permute-start | bytes 1572872 | tf_op jit(solution)/shard_map/ppermute | solution.py:24
  271.1 17.9 %collective-permute-start.32 = (bf16[256,1024]{1,0:T(8,128)(2,1)}, bf16[256,1024]{1,0:T(8,128)(2,1)}, u32[]{:S(2)}, u32[]{:S(2)}) collective-permute-start(bf16[256,1024]{1,0:T(8,128)(2,1)} %get-tuple-element.60), channel_id=1, source_target_pairs={{0,5},{1,4},{4,1},{5,0},{2,7},{3,6},{6,3},{7,2},{8,13},{9,12},{12,... | collective-permute-start | bytes 1572872 | tf_op jit(solution)/shard_map/ppermute | solution.py:24
  296.0 6.5 %collective-permute-start.33 = (bf16[112,256]{1,0:T(8,128)(2,1)S(1)}, bf16[112,256]{1,0:T(8,128)(2,1)S(1)}, u32[]{:S(2)}, u32[]{:S(2)}) collective-permute-start(bf16[112,256]{1,0:T(8,128)(2,1)S(1)} %get-tuple-element.105), channel_id=1, source_target_pairs={{0,1},{1,0},{4,5},{5,4},{2,3},{3,2},{6,7},{7,6},{8,9},{9,8},{12,13... | collective-permute-start | bytes 172040 | tf_op jit(solution)/shard_map/ppermute | solution.py:24
  (36 other events, 236.4 us)
Sparse Core Ops, SparseCore 0:
  20.7 31.0 all-gather.8
  59.2 51.8 all-gather.4
  112.7 30.4 all-gather.6
  151.1 36.8 reduce-scatter.3
  192.2 55.9 reduce-scatter.5
  256.1 38.8 reduce-scatter.7
